TPU v7x, 32 devices: a whole 2x2x4 slice. The times are simulated.
32 devices in a mesh: chan: 8 (over z, y), blk: 4 (over x, core).
Axes of the slice: x: 2, y: 2, z: 4, core: 2. Of those that a mesh axis runs over, the one named last changes fastest.
Arguments:
- voltages: int32 [1024, 262144], P('chan', 'blk'), may hold values from -127 to 127, as said below
Outputs:
- vis_real: float32 [256, 1024, 1024], P(('chan', 'blk'))
- vis_imag: float32 [256, 1024, 1024], P(('chan', 'blk'))
Inputs may be any that keep to these rules, and one draw needn't show every extreme that they name: `voltages`: integer voltage samples.
All inputs are finite; a program needn't handle non-finite values.
Results may differ from a plain program's by a relative error of at most 0.004.
Values may be sent and summed in bfloat16 or wider, within the bound.
No kernel may reach another device: no remote copies, remote signals or barrier semaphores. Data moves between devices by JAX's collectives and lax.ppermute only.
A program may use at most 256 MiB of HBM per device.

v0:
```python
import jax
import jax.numpy as jnp
from jax import lax
from jax.sharding import PartitionSpec as P

NI = 1024
NC = 256
TAPS = 4
FFT = 512


def shifted(value, axis, steps):
    count = lax.axis_size(axis)
    leading, last = (max(0, -steps), min(count, count - steps))
    return lax.ppermute(value, axis, [(source, source + steps) for source in range(leading, last)])


def build_taps():
    length = TAPS * FFT
    points = jnp.arange(length, dtype=jnp.float32)
    centre = (length - 1) / 2.0
    window = 0.54 - 0.46 * jnp.cos(2.0 * jnp.pi * points / (length - 1))
    return (jnp.sinc((points - centre) / FFT) * window).reshape(TAPS, FFT)


def spectrum_scale(filter_taps):
    energy = jnp.mean(jnp.sum(filter_taps * filter_taps, axis=0))
    return 1.0 / (56.0 * jnp.sqrt(FFT * energy))


def build_transform(blk_count, chan_local):
    points = jnp.arange(FFT, dtype=jnp.int32)[:, None]
    column = jnp.arange(NC, dtype=jnp.int32)
    per_block = NC // blk_count
    block_index = column // per_block
    within = column % per_block
    column = (within // chan_local * blk_count + block_index) * chan_local + within % chan_local
    angle = (points * column[None, :] % FFT).astype(jnp.float32) * (2.0 * jnp.pi / FFT)
    return jnp.concatenate([jnp.cos(angle), -jnp.sin(angle)], axis=1)


def apply_taps(padded, filter_taps, frames_dev):
    filtered = filter_taps[0] * padded[:, 0:frames_dev, :]
    for offset in range(1, TAPS):
        filtered = filtered + filter_taps[offset] * padded[:, offset : offset + frames_dev, :]
    return filtered


def to_spectra(filtered, transform, scale_factor):
    inputs_here = filtered.shape[0]
    frames_dev = filtered.shape[1]
    spectra = (
        jnp.einsum("ifn,nk->kif", filtered, transform, precision=lax.Precision.HIGHEST)
        * scale_factor
    )
    spectra = spectra.reshape(2, NC, inputs_here, frames_dev).transpose(1, 2, 0, 3)
    return spectra.reshape(NC, inputs_here, 2 * frames_dev).astype(jnp.bfloat16)


def local(voltages):
    inputs_here = voltages.shape[0]
    frames_dev = voltages.shape[1] // FFT
    chan_count = lax.axis_size("chan")
    blk_count = lax.axis_size("blk")
    chan_local = NC // (chan_count * blk_count)
    filter_taps = build_taps()
    scale_factor = spectrum_scale(filter_taps)
    history_len = TAPS - 1
    samples = voltages.astype(jnp.float32).reshape(inputs_here, frames_dev, FFT)
    tail = voltages[:, (frames_dev - history_len) * FFT :].astype(jnp.bfloat16)
    earlier = shifted(tail, "blk", 1)
    earlier = earlier.astype(jnp.float32).reshape(inputs_here, history_len, FFT)
    padded = jnp.concatenate([earlier, samples], axis=1)
    filtered = apply_taps(padded, filter_taps, frames_dev)
    spectra = to_spectra(filtered, build_transform(blk_count, chan_local), scale_factor)
    across = lax.all_to_all(spectra, "blk", split_axis=0, concat_axis=2, tiled=True)
    turned = lax.all_to_all(across, "chan", split_axis=0, concat_axis=1, tiled=True)
    stacked = turned.reshape(chan_local, NI, blk_count, 2, frames_dev)
    swapped = jnp.concatenate([stacked[:, :, :, 1:2], -stacked[:, :, :, 0:1]], axis=3)
    swapped = swapped.reshape(chan_local, NI, 2 * blk_count * frames_dev)
    total_frames = blk_count * frames_dev
    vis_real = (
        jnp.einsum("cim,cjm->cij", turned, turned, preferred_element_type=jnp.float32)
        / total_frames
    )
    vis_imag = (
        jnp.einsum("cim,cjm->cij", swapped, turned, preferred_element_type=jnp.float32)
        / total_frames
    )
    return (vis_real, vis_imag)


def solution(mesh):
    return jax.shard_map(
        local,
        mesh=mesh,
        in_specs=(P("chan", "blk"),),
        out_specs=(P(("chan", "blk"), None, None), P(("chan", "blk"), None, None)),
        check_vma=False,
    )
```

profile of v0, /device:TPU:0, one launch (start us, length us, event | category | flops | bytes accessed | tf_op | source)
XLA Modules:
  0.0 876.9 jit_solution(1280378107350742417)
XLA Ops:
  0.6 1.2 slice.46
  1.8 0.3 copy.20
  2.1 2.4 collective-permute-start
  4.5 0.1 fusion.33
  4.6 22.5 %convert_element_type.28 = f32[128,65536]{1,0:T(8,128)} convert(s32[128,65536]{1,0:T(8,128)} %param.1) | non-fusion elementwise | flops 8388608 | bytes 67108864 | tf_op jit(solution)/shard_map/convert_element_type | solution.py:69
  27.1 0.7 multiply_reduce_fusion
  28.4 31.8 %copy.21 = f32[16,8,128,512]{3,2,1,0:T(8,128)} copy(f32[16,8,128,512]{3,1,2,0:T(8,128)} %bitcast.35) | data formatting | bytes 67108864
  60.3 2.1 fusion.28
  62.4 0.0 collective-permute-done
  62.5 0.4 copy.10
  62.9 79.3 %multiply_convert_fusion = bf16[512,128,128]{2,0,1:T(8,128)(2,1)} fusion(f32[]{:T(128)S(6)} %div.89, f32[128,128,512]{2,1,0:T(8,128)} %bitcast.39, f32[128,3,512]{2,1,0:T(4,128)S(1)} %copy.10, f32[512]{0:T(512)S(1)} %get-tuple-element.5, f32[512]{0:T(512)S(1)} %get-tuple-element.6, f32[512]{0:T(512)S(1)} %get-tuple-element.7, f32[512]{0:T(512)S(1)} %get-tuple-element.4, ...), kind=kOutput, calls=%fused_computation.15 | convolution fusion | flops 51640532992 | bytes 52174852 | tf_op jit(solution)/shard_map/ifn,nk->kif/dot_general | solution.py:53
  142.2 23.8 %copy.11 = bf16[2,256,128,128]{2,3,0,1:T(8,128)(2,1)} copy(bf16[2,256,128,128]{3,1,0,2:T(8,128)(2,1)} %bitcast.42) | data formatting | bytes 33554432 | tf_op jit(solution)/shard_map/convert_element_type | solution.py:57
  166.0 187.7 %all_to_all.36 = bf16[256,128,256]{1,2,0:T(8,128)(2,1)S(1)} all-to-all(bf16[256,128,256]{1,2,0:T(8,128)(2,1)} %bitcast.36), channel_id=1, replica_groups=mesh['chan'=8,'blk'=4] {'blk'}, dimensions={0} | all-to-all | bytes 33554432 | tf_op jit(solution)/shard_map/all_to_all | solution.py:76
  353.7 1.9 copy.12
  355.6 369.6 %all_to_all.37 = bf16[64,128,1024]{1,2,0:T(8,128)(2,1)S(1)} all-to-all(bf16[64,128,1024]{1,2,0:T(8,128)(2,1)S(1)} %bitcast.38), channel_id=1, replica_groups=mesh['chan'=8,'blk'=4] {'chan'}, dimensions={0} | all-to-all | bytes 33554432 | tf_op jit(solution)/shard_map/all_to_all | solution.py:77
  725.2 0.0 copy-start
  725.2 6.2 copy-done
  731.4 11.7 %copy.15 = bf16[8,8,128,1024]{2,1,3,0:T(8,128)(2,1)} copy(bf16[8,8,128,1024]{2,3,0,1:T(8,128)(2,1)S(1)} %bitcast.33) | data formatting | bytes 33554432 | tf_op jit(solution)/shard_map/all_to_all | solution.py:77
  743.1 21.6 %copy.14 = bf16[8,8,128,1024]{3,2,1,0:T(8,128)(2,1)} copy(bf16[8,8,128,1024]{2,3,0,1:T(8,128)(2,1)} %bitcast.34) | data formatting | bytes 33554432 | tf_op jit(solution)/shard_map/all_to_all | solution.py:77
  764.7 25.2 %reshape.92 = bf16[8,1024,4,2,128]{1,4,3,2,0:T(8,128)(2,1)} reshape(bf16[8,8,128,1024]{2,1,3,0:T(8,128)(2,1)} %copy.15) | data formatting | bytes 33554432 | tf_op jit(solution)/shard_map/reshape | solution.py:78
  790.0 11.3 %fusion.63 = (bf16[8,1024,4,1,128]{1,4,3,2,0:T(8,128)(2,1)}, bf16[8,1024,4,1,128]{1,4,3,2,0:T(8,128)(2,1)}) fusion(bf16[8,1024,4,2,128]{1,4,3,2,0:T(8,128)(2,1)} %reshape.92), kind=kLoop, calls=%fused_computation.92 | loop fusion | flops 4194304 | bytes 33554432 | tf_op jit(solution)/shard_map/slice | solution.py:79
  801.3 32.2 %broadcast_multiply_fusion.1 = f32[8,1024,1024]{2,1,0:T(8,128)} fusion(bf16[8,1024,1024]{2,1,0:T(8,128)(2,1)} %bitcast.40), kind=kOutput, calls=%fused_computation.19 | convolution fusion | flops 17188257792 | bytes 50331648 | tf_op jit(solution)/shard_map/cim,cjm->cij/dot_general | solution.py:83
  833.5 13.8 %pad_maximum_fusion.1 = bf16[8,1024,4,2,128]{1,4,3,2,0:T(8,128)(2,1)} fusion(bf16[8,1024,4,1,128]{1,4,3,2,0:T(8,128)(2,1)} %get-tuple-element.3, bf16[8,1024,4,1,128]{1,4,3,2,0:T(8,128)(2,1)} %get-tuple-element.2), kind=kLoop, calls=%fused_computation.17 | loop fusion | flops 8388608 | bytes 33554432 | tf_op jit(solution)/shard_map/concatenate | solution.py:79
  847.3 29.6 %broadcast_multiply_fusion = f32[8,1024,1024]{2,1,0:T(8,128)} fusion(bf16[8,1024,1024]{1,2,0:T(8,128)(2,1)} %bitcast.43, bf16[8,1024,1024]{2,1,0:T(8,128)(2,1)} %bitcast.41), kind=kOutput, calls=%fused_computation.18 | convolution fusion | flops 17188257792 | bytes 67108864 | tf_op jit(solution)/shard_map/cim,cjm->cij/dot_general | solution.py:87
  (3 shorter events, 0.1 us)
Async XLA Ops:
  2.1 60.3 %collective-permute-start = (bf16[128,1536]{0,1:T(8,128)(2,1)S(1)}, bf16[128,1536]{0,1:T(8,128)(2,1)S(1)}, u32[]{:S(2)}, u32[]{:S(2)}) collective-permute-start(bf16[128,1536]{0,1:T(8,128)(2,1)S(1)} %convert.4), channel_id=1, source_target_pairs={{0,1},{1,2},{2,3},{4,5},{5,6},{6,7},{8,9},{9,10},{10,11},{12,13},{... | collective-permute-start | bytes 1179656 | tf_op jit(solution)/shard_map/ppermute | solution.py:15
  725.2 6.2 copy-start
where the time goes:
time: 879 us; the launch traced here: 877 us
  blocking collectives  557 us (63%)
  matrix products  141 us (16%)
  local copies, waits for them, and re-layouts  124 us (14%)
  other arithmetic  50.5 us (6%)
    all_to_all x1, blocking collectives, local(): lax.all_to_all(across, 'chan', split_axis=0, concat_axis=1, tiled=True)  370 us
    all_to_all x1, blocking collectives, local(): lax.all_to_all(spectra, 'blk', split_axis=0, concat_axis=2, tiled=True)  188 us
    dot_general x1, matrix products, to_spectra(): jnp.einsum('ifn,nk->kif', filtered, transform, precision=lax.Precision.HI...  79.3 us
    unnamed x4, local copies, waits for them, and re-layouts  38.2 us
    all_to_all x2, local copies, waits for them, and re-layouts, local(): lax.all_to_all(across, 'chan', split_axis=0, concat_axis=1, tiled=True)  33.4 us
    dot_general x1, matrix products, local(): jnp.einsum('cim,cjm->cij', turned, turned, preferred_element_type=jnp.flo...  32.2 us
    dot_general x1, matrix products, local(): jnp.einsum('cim,cjm->cij', swapped, turned, preferred_element_type=jnp.fl...  29.6 us
    reshape x1, local copies, waits for them, and re-layouts, local(): stacked = turned.reshape(chan_local, NI, blk_count, 2, frames_dev)  25.2 us
  transfers between devices with their start and end apart: 1, of which 0 were waited for; matrix products, arithmetic and copies ran while one was open for 7% of the time, Pallas kernels for 0%

commit v1 on v0

v1 whole, which is shorter than its diff:
```python
import functools

import jax
import jax.numpy as jnp
import numpy as np
from jax import lax
from jax.experimental import pallas as pl
from jax.experimental.pallas import tpu as pltpu
from jax.sharding import PartitionSpec as P

NC = 256
TAPS = 4
FFT = 512
HISTORY = TAPS - 1
FRAME_BLOCK = 16
ROWS = 16
VMEM_LIMIT = 56 * 1024 * 1024


def shifted(value, axis, steps):
    count = lax.axis_size(axis)
    leading, last = (max(0, -steps), min(count, count - steps))
    return lax.ppermute(value, axis, [(source, source + steps) for source in range(leading, last)])


def build_taps():
    length = TAPS * FFT
    points = np.arange(length, dtype=np.float64)
    window = 0.54 - 0.46 * np.cos(2.0 * np.pi * points / (length - 1))
    return (np.sinc((points - (length - 1) / 2.0) / FFT) * window).reshape(TAPS, FFT)


def spectrum_scale(filter_taps):
    energy = np.mean(np.sum(filter_taps * filter_taps, axis=0))
    return 1.0 / (56.0 * np.sqrt(FFT * energy))


def build_transform(chunks, devices, chan_local, folds):
    scale = spectrum_scale(build_taps())
    points = np.arange(FFT // folds)
    rows = []
    for chunk in chunks:
        channel = np.arange(devices) * chan_local + chunk
        angle = (channel[:, None] * points[None, :] % FFT) * (2.0 * np.pi / FFT)
        rows.append(np.stack([np.cos(angle), -np.sin(angle)], axis=1))
    matrix = (np.concatenate(rows) * scale).reshape(-1, FFT // folds).astype(np.float32)
    high = matrix.astype(jnp.bfloat16)
    low = (matrix - high.astype(np.float32)).astype(jnp.bfloat16)
    return np.concatenate([high, high, low], axis=1)


def spectra_kernel(groups, folds, *refs):
    chunk_count = sum(len(chunks) for _, chunks in groups)
    voltages, halo, taps = refs[:3]
    transforms = refs[3 : 3 + len(groups)]
    outputs = refs[3 + len(groups) : 3 + len(groups) + chunk_count]
    history, turned = refs[3 + len(groups) + chunk_count :][:2]
    folded = refs[3 + len(groups) + chunk_count + 2 :]
    inputs_here = voltages.shape[0]
    part = FFT // folds
    lanes = 128

    @pl.when(pl.program_id(0) == 0)
    def _():
        history[...] = halo[...].astype(jnp.float32)

    def filter_rows(step, carry):
        rows = pl.ds(pl.multiple_of(step * ROWS, ROWS), ROWS)
        for start in range(0, part, lanes):
            pieces = []
            for fold in range(folds):
                column = fold * part + start
                weights = [taps[offset : offset + 1, column : column + lanes] for offset in range(TAPS)]
                past = [history[rows, frame * FFT + column : frame * FFT + column + lanes] for frame in range(HISTORY)]
                filtered = []
                for frame in range(FRAME_BLOCK):
                    at = frame * FFT + column
                    past.append(voltages[rows, at : at + lanes].astype(jnp.float32))
                    value = weights[0] * past[0]
                    for offset in range(1, TAPS):
                        value = value + weights[offset] * past[offset]
                    filtered.append(value)
                    past = past[1:]
                for frame in range(HISTORY):
                    history[rows, frame * FFT + column : frame * FFT + column + lanes] = past[frame]
                pieces.append(filtered)
            for frame in range(FRAME_BLOCK):
                for (residue, _), target in zip(groups, folded):
                    value = pieces[0][frame]
                    if folds == 2:
                        value = value + pieces[1][frame] if residue == 0 else value - pieces[1][frame]
                    high = value.astype(jnp.bfloat16)
                    low = (value - high.astype(jnp.float32)).astype(jnp.bfloat16)
                    at = pl.ds(pl.multiple_of(frame * inputs_here + step * ROWS, ROWS), ROWS)
                    target[at, start : start + lanes] = high
                    target[at, part + start : part + start + lanes] = low
                    target[at, 2 * part + start : 2 * part + start + lanes] = high
        return carry

    lax.fori_loop(0, inputs_here // ROWS, filter_rows, 0)

    position = 0
    for (_, chunks), transform, source in zip(groups, transforms, folded):
        per_chunk = transform.shape[0] // len(chunks)
        batch = max(1, min(FRAME_BLOCK, 256 // inputs_here)) if inputs_here >= lanes else 1
        for first in range(0, FRAME_BLOCK, batch):
            result = lax.dot_general(
                transform[...],
                source[first * inputs_here : (first + batch) * inputs_here, :],
                (((1,), (1,)), ((), ())),
                preferred_element_type=jnp.float32,
            )
            for frame in range(batch):
                turned[pl.ds(first + frame, transform.shape[0], stride=FRAME_BLOCK), :] = result[
                    :, frame * inputs_here : (frame + 1) * inputs_here
                ]
        for index in range(len(chunks)):
            start = index * per_chunk * FRAME_BLOCK
            block = turned[start : start + per_chunk * FRAME_BLOCK, :]
            outputs[position][...] = block.reshape(outputs[position].shape).astype(jnp.bfloat16)
            position += 1


def spectra(voltages, halo, chunks, devices, chan_local):
    folds = 2 if chan_local % 2 == 0 else 1
    inputs_here = voltages.shape[0]
    frames_dev = voltages.shape[1] // FFT
    groups = []
    for residue in range(folds):
        members = [chunk for chunk in chunks if chunk % folds == residue]
        if members:
            groups.append((residue, members))
    transforms = [jnp.asarray(build_transform(members, devices, chan_local, folds)) for _, members in groups]
    order = [chunk for _, members in groups for chunk in members]
    shape = (devices, 2, frames_dev, inputs_here)
    block = (devices, 2, FRAME_BLOCK, inputs_here)
    depth = 3 * (FFT // folds)
    most = max(transform.shape[0] for transform in transforms)
    results = pl.pallas_call(
        functools.partial(spectra_kernel, groups, folds),
        grid=(frames_dev // FRAME_BLOCK,),
        in_specs=[
            pl.BlockSpec((inputs_here, FRAME_BLOCK * FFT), lambda step: (0, step)),
            pl.BlockSpec((inputs_here, HISTORY * FFT), lambda step: (0, 0)),
            pl.BlockSpec((TAPS, FFT), lambda step: (0, 0)),
        ]
        + [pl.BlockSpec(transform.shape, lambda step: (0, 0)) for transform in transforms],
        out_specs=[pl.BlockSpec(block, lambda step: (0, 0, step, 0)) for _ in order],
        out_shape=[jax.ShapeDtypeStruct(shape, jnp.bfloat16) for _ in order],
        scratch_shapes=[
            pltpu.VMEM((inputs_here, HISTORY * FFT), jnp.float32),
            pltpu.VMEM((most * FRAME_BLOCK, inputs_here), jnp.float32),
        ]
        + [pltpu.VMEM((FRAME_BLOCK * inputs_here, depth), jnp.bfloat16) for _ in groups],
        compiler_params=pltpu.CompilerParams(vmem_limit_bytes=VMEM_LIMIT),
        cost_estimate=pl.CostEstimate(
            flops=2 * frames_dev * inputs_here * depth * sum(transform.shape[0] for transform in transforms),
            bytes_accessed=voltages.size * 4 + 2 * len(order) * int(np.prod(shape)),
            transcendentals=0,
        ),
        name="spectra",
    )(voltages, halo, jnp.asarray(build_taps().astype(np.float32)), *transforms)
    return dict(zip(order, results))


def visibility_kernel(received, *refs):
    real_out, imag_out, across, turned, swapped = refs[-5:]
    chan_count, blk_count, _, frames_dev, inputs_here = received.shape
    depth = blk_count * 2 * frames_dev
    total_frames = blk_count * frames_dev
    row_block = real_out.shape[1]

    @pl.when(pl.program_id(0) == 0)
    def _():
        for chan in range(chan_count):
            across[:, chan * inputs_here : (chan + 1) * inputs_here] = received[chan].reshape(depth, inputs_here)

    start = pl.multiple_of(pl.program_id(0) * row_block, row_block)
    turned[...] = across[:, pl.ds(start, row_block)].T
    for blk in range(blk_count):
        at = blk * 2 * frames_dev
        swapped[:, at : at + frames_dev] = turned[:, at + frames_dev : at + 2 * frames_dev]
        swapped[:, at + frames_dev : at + 2 * frames_dev] = -turned[:, at : at + frames_dev]
    everything = across[...]
    real_out[0] = jnp.dot(turned[...], everything, preferred_element_type=jnp.float32) / total_frames
    imag_out[0] = jnp.dot(swapped[...], everything, preferred_element_type=jnp.float32) / total_frames


def visibilities(received, before, chunk, chan_local):
    chan_count, blk_count, _, frames_dev, inputs_here = received.shape
    inputs = chan_count * inputs_here
    depth = blk_count * 2 * frames_dev
    row_block = 256
    shape = jax.ShapeDtypeStruct((chan_local, inputs, inputs), jnp.float32)
    out_spec = pl.BlockSpec((1, row_block, inputs), lambda step: (chunk, step, 0))
    return pl.pallas_call(
        visibility_kernel,
        grid=(inputs // row_block,),
        in_specs=[pl.BlockSpec(received.shape, lambda step: (0, 0, 0, 0, 0))]
        + [pl.BlockSpec(memory_space=pl.ANY) for _ in before],
        out_specs=[out_spec, out_spec],
        out_shape=[shape, shape],
        input_output_aliases={1 + index: index for index in range(len(before))},
        scratch_shapes=[
            pltpu.VMEM((depth, inputs), jnp.bfloat16),
            pltpu.VMEM((row_block, depth), jnp.bfloat16),
            pltpu.VMEM((row_block, depth), jnp.bfloat16),
        ],
        compiler_params=pltpu.CompilerParams(vmem_limit_bytes=VMEM_LIMIT),
        cost_estimate=pl.CostEstimate(
            flops=4 * inputs * inputs * depth,
            bytes_accessed=2 * received.size + 8 * inputs * inputs,
            transcendentals=0,
        ),
        name="visibilities",
    )(received, *before)


def local(voltages):
    inputs_here = voltages.shape[0]
    frames_dev = voltages.shape[1] // FFT
    chan_count = lax.axis_size("chan")
    blk_count = lax.axis_size("blk")
    devices = chan_count * blk_count
    chan_local = NC // devices
    tail = voltages[:, (frames_dev - HISTORY) * FFT :].astype(jnp.bfloat16)
    halo = shifted(tail, "blk", 1)
    first = [0]
    rest = list(range(1, chan_local))
    sent = spectra(voltages, halo, first, devices, chan_local)
    if rest:
        sent.update(spectra(voltages, halo, rest, devices, chan_local))
    outputs = ()
    for chunk in range(chan_local):
        received = lax.all_to_all(sent[chunk], ("chan", "blk"), split_axis=0, concat_axis=0, tiled=True)
        received = received.reshape(chan_count, blk_count, 2, frames_dev, inputs_here)
        outputs = visibilities(received, outputs, chunk, chan_local)
    return tuple(outputs)


def solution(mesh):
    return jax.shard_map(
        local,
        mesh=mesh,
        in_specs=(P("chan", "blk"),),
        out_specs=(P(("chan", "blk"), None, None), P(("chan", "blk"), None, None)),
        check_vma=False,
    )
```

time: 879 us -> 484 us (0.55)
  blocking collectives: 557 us -> 315 us
  matrix products: 141 us -> 0 us
  Pallas kernels: 0 us -> 140 us
  local copies, waits for them, and re-layouts: 124 us -> 2.11 us
  other arithmetic: 50.5 us -> 1.18 us
  starting transfers between devices: 2.38 us -> 18.9 us
    all_to_all x2 -> x6, blocking collectives: 557 us -> 315 us  [local(): lax.all_to_all(sent[chunk], ('chan', 'blk'), split_axis=0, concat_axis=0,...]
    dot_general x3 -> x0, matrix products: 141 us -> none  [the longest x1 79.3 us: to_spectra(): jnp.einsum('ifn,nk->kif', filtered, transform, precision=lax.Precision.HI...]
    pallas_call x0 -> x10, Pallas kernels: none -> 140 us  [the longest x2 71.2 us: spectra(): pl.pallas_call(functools.partial(spectra_kernel, groups, folds), grid=(fr...]
    unnamed x4 -> x6, local copies, waits for them, and re-layouts: 38.2 us -> 2.11 us
    all_to_all x3 -> x0, local copies, waits for them, and re-layouts: 35.3 us -> none  [the longest x2 33.4 us: local(): lax.all_to_all(across, 'chan', split_axis=0, concat_axis=1, tiled=True)]
    reshape x2 -> x0, local copies, waits for them, and re-layouts: 25.6 us -> none  [the longest x1 25.2 us: local(): stacked = turned.reshape(chan_local, NI, blk_count, 2, frames_dev)]
    convert_element_type x1 -> x0, local copies, waits for them, and re-layouts: 23.8 us -> none  [to_spectra(): return spectra.reshape(NC, inputs_here, 2 * frames_dev).astype(jnp.bfloat16)]
    convert_element_type x1 -> x0, other arithmetic: 22.5 us -> none  [local(): samples = voltages.astype(jnp.float32).reshape(inputs_here, frames_dev, FFT)]
  transfers between devices with their start and end apart: 1 -> 3, of which waited for: 0 -> 2; matrix products, arithmetic and copies ran while one was open for 7% -> 0% of each run, Pallas kernels for 0% -> 22%
where the time goes in v1:
time: 484 us; the launch traced here: 483 us
  blocking collectives  315 us (65%)
  Pallas kernels  140 us (29%)
  starting transfers between devices  18.9 us (4%)
    all_to_all x6, blocking collectives, local(): lax.all_to_all(sent[chunk], ('chan', 'blk'), split_axis=0, concat_axis=0,...  315 us
    pallas_call x2, Pallas kernels, spectra(): pl.pallas_call(functools.partial(spectra_kernel, groups, folds), grid=(fr...  71.2 us
    pallas_call x8, Pallas kernels, visibilities(): pl.pallas_call(visibility_kernel, grid=(inputs // row_block,), in_specs=[...  69.2 us
    all_to_all x2, starting transfers between devices, local(): lax.all_to_all(sent[chunk], ('chan', 'blk'), split_axis=0, concat_axis=0,...  16.5 us
  transfers between devices with their start and end apart: 3, of which 2 were waited for; matrix products, arithmetic and copies ran while one was open for 0% of the time, Pallas kernels for 22%

profile of v1, /device:TPU:0, one launch (start us, length us, event | category | flops | bytes accessed | tf_op | source)
XLA Modules:
  0.0 483.2 jit_solution(4856103156832921764)
XLA Ops:
  0.6 1.2 slice_convert_fusion
  1.8 2.4 collective-permute-start
  4.2 1.3 collective-permute-done.refs_1_
  5.5 0.0 copy-start.2
  5.5 0.8 copy-done.2
  6.3 25.7 %spectra.3 = bf16[32,2,128,128]{3,2,1,0:T(8,128)(2,1)} custom-call(s32[128,65536]{1,0:T(8,128)} %refs_0_.3, bf16[128,1536]{1,0:T(8,128)(2,1)} %copy-done.2, f32[4,512]{1,0:T(4,128)} %constant.9.clone.refs_2_, bf16[64,768]{1,0:T(8,128)(2,1)} %constant.8.clone.refs_3_), custom_call_target="tpu_custom_call" | custom-call | flops 1610612736 | bytes 35651584 | tf_op jit(solution)/shard_map/spectra/pallas_call | solution.py:139
  32.0 12.7 %all-to-all-start.7 = ((bf16[32,2,128,128]{3,2,1,0:T(8,128)(2,1)}), bf16[32,2,128,128]{3,2,1,0:T(8,128)(2,1)S(1)}, u32[]{:S(2)}, u32[]{:S(2)}) async-start(bf16[32,2,128,128]{3,2,1,0:T(8,128)(2,1)} %spectra.3), calls=%async_computation.7 | async-start | bytes 4194304 | tf_op jit(solution)/shard_map/all_to_all | solution.py:235
  44.7 45.5 %spectra.2 = (bf16[32,2,128,128]{3,2,1,0:T(8,128)(2,1)}, bf16[32,2,128,128]{3,2,1,0:T(8,128)(2,1)}, bf16[32,2,128,128]{3,2,1,0:T(8,128)(2,1)}, bf16[32,2,128,128...) custom-call(s32[128,65536]{1,0:T(8,128)} %refs_0_.3, ...), custom_call_target="tpu_custom_call" | custom-call | flops 11274289152 | bytes 48234496 | tf_op jit(solution)/shard_map/spectra/pallas_call | solution.py:139
  90.2 3.4 all-to-all-done.7
  93.6 0.0 copy-start.1
  93.6 52.8 %all_to_all.40 = bf16[32,2,128,128]{3,2,1,0:T(8,128)(2,1)} all-to-all(bf16[32,2,128,128]{3,2,1,0:T(8,128)(2,1)} %get-tuple-element.24), channel_id=1, replica_groups=mesh['chan'=8,'blk'=4] {'chan','blk'}, dimensions={0} | all-to-all | bytes 4194304 | tf_op jit(solution)/shard_map/all_to_all | solution.py:235
  146.4 52.5 %all_to_all.41 = bf16[32,2,128,128]{3,2,1,0:T(8,128)(2,1)} all-to-all(bf16[32,2,128,128]{3,2,1,0:T(8,128)(2,1)} %get-tuple-element.25), channel_id=1, replica_groups=mesh['chan'=8,'blk'=4] {'chan','blk'}, dimensions={0} | all-to-all | bytes 4194304 | tf_op jit(solution)/shard_map/all_to_all | solution.py:235
  198.9 52.5 %all_to_all.42 = bf16[32,2,128,128]{3,2,1,0:T(8,128)(2,1)} all-to-all(bf16[32,2,128,128]{3,2,1,0:T(8,128)(2,1)} %get-tuple-element.26), channel_id=1, replica_groups=mesh['chan'=8,'blk'=4] {'chan','blk'}, dimensions={0} | all-to-all | bytes 4194304 | tf_op jit(solution)/shard_map/all_to_all | solution.py:235
  251.4 52.5 %all_to_all.43 = bf16[32,2,128,128]{3,2,1,0:T(8,128)(2,1)} all-to-all(bf16[32,2,128,128]{3,2,1,0:T(8,128)(2,1)} %get-tuple-element.27), channel_id=1, replica_groups=mesh['chan'=8,'blk'=4] {'chan','blk'}, dimensions={0} | all-to-all | bytes 4194304 | tf_op jit(solution)/shard_map/all_to_all | solution.py:235
  303.8 52.5 %all_to_all.44 = bf16[32,2,128,128]{3,2,1,0:T(8,128)(2,1)} all-to-all(bf16[32,2,128,128]{3,2,1,0:T(8,128)(2,1)} %get-tuple-element.28), channel_id=1, replica_groups=mesh['chan'=8,'blk'=4] {'chan','blk'}, dimensions={0} | all-to-all | bytes 4194304 | tf_op jit(solution)/shard_map/all_to_all | solution.py:235
  356.3 52.5 %all_to_all.45 = bf16[32,2,128,128]{3,2,1,0:T(8,128)(2,1)} all-to-all(bf16[32,2,128,128]{3,2,1,0:T(8,128)(2,1)} %get-tuple-element.29), channel_id=1, replica_groups=mesh['chan'=8,'blk'=4] {'chan','blk'}, dimensions={0} | all-to-all | bytes 4194304 | tf_op jit(solution)/shard_map/all_to_all | solution.py:235
  408.8 0.0 copy-done.1
  408.8 3.8 all-to-all-start
  412.7 8.7 %visibilities.8 = (f32[8,1024,1024]{2,1,0:T(8,128)}, f32[8,1024,1024]{2,1,0:T(8,128)}) custom-call(bf16[8,4,2,128,128]{4,3,2,1,0:T(8,128)(2,1)} %bitcast.15), custom_call_target="tpu_custom_call" | custom-call | flops 4294967296 | bytes 10485760 | tf_op jit(solution)/shard_map/visibilities/pallas_call | solution.py:196
  421.4 8.7 %visibilities.9 = (f32[8,1024,1024]{2,1,0:T(8,128)}, f32[8,1024,1024]{2,1,0:T(8,128)}) custom-call(bf16[8,4,2,128,128]{4,3,2,1,0:T(8,128)(2,1)} %bitcast.14, f32[8,1024,1024]{2,1,0:T(8,128)} %get-tuple-element.30.refs_0_, f32[8,1024,1024]{2,1,0:T(8,128)} %get-tuple-element.31.refs_1_), custom_call_target="tpu_custom_call", output_to_operand_aliasing={{0}: (1, {}), {1}: (2, {})} | custom-call | flops 4294967296 | bytes 10485760 | tf_op jit(solution)/shard_map/visibilities/pallas_call | solution.py:196
  430.0 8.6 %visibilities.10 = (f32[8,1024,1024]{2,1,0:T(8,128)}, f32[8,1024,1024]{2,1,0:T(8,128)}) custom-call(bf16[8,4,2,128,128]{4,3,2,1,0:T(8,128)(2,1)} %bitcast.13, f32[8,1024,1024]{2,1,0:T(8,128)} %get-tuple-element.32.refs_0_, f32[8,1024,1024]{2,1,0:T(8,128)} %get-tuple-element.33.refs_1_), custom_call_target="tpu_custom_call", output_to_operand_aliasing={{0}: (1, {}), {1}: (2, {})} | custom-call | flops 4294967296 | bytes 10485760 | tf_op jit(solution)/shard_map/visibilities/pallas_call | solution.py:196
  438.7 8.6 %visibilities.11 = (f32[8,1024,1024]{2,1,0:T(8,128)}, f32[8,1024,1024]{2,1,0:T(8,128)}) custom-call(bf16[8,4,2,128,128]{4,3,2,1,0:T(8,128)(2,1)} %bitcast.12, f32[8,1024,1024]{2,1,0:T(8,128)} %get-tuple-element.34.refs_0_, f32[8,1024,1024]{2,1,0:T(8,128)} %get-tuple-element.35.refs_1_), custom_call_target="tpu_custom_call", output_to_operand_aliasing={{0}: (1, {}), {1}: (2, {})} | custom-call | flops 4294967296 | bytes 10485760 | tf_op jit(solution)/shard_map/visibilities/pallas_call | solution.py:196
  447.3 8.6 %visibilities.12 = (f32[8,1024,1024]{2,1,0:T(8,128)}, f32[8,1024,1024]{2,1,0:T(8,128)}) custom-call(bf16[8,4,2,128,128]{4,3,2,1,0:T(8,128)(2,1)} %bitcast.11, f32[8,1024,1024]{2,1,0:T(8,128)} %get-tuple-element.36.refs_0_, f32[8,1024,1024]{2,1,0:T(8,128)} %get-tuple-element.37.refs_1_), custom_call_target="tpu_custom_call", output_to_operand_aliasing={{0}: (1, {}), {1}: (2, {})} | custom-call | flops 4294967296 | bytes 10485760 | tf_op jit(solution)/shard_map/visibilities/pallas_call | solution.py:196
  456.0 8.6 %visibilities.13 = (f32[8,1024,1024]{2,1,0:T(8,128)}, f32[8,1024,1024]{2,1,0:T(8,128)}) custom-call(bf16[8,4,2,128,128]{4,3,2,1,0:T(8,128)(2,1)} %bitcast.10, f32[8,1024,1024]{2,1,0:T(8,128)} %get-tuple-element.38.refs_0_, f32[8,1024,1024]{2,1,0:T(8,128)} %get-tuple-element.39.refs_1_), custom_call_target="tpu_custom_call", output_to_operand_aliasing={{0}: (1, {}), {1}: (2, {})} | custom-call | flops 4294967296 | bytes 10485760 | tf_op jit(solution)/shard_map/visibilities/pallas_call | solution.py:196
  464.6 8.6 %visibilities.14 = (f32[8,1024,1024]{2,1,0:T(8,128)}, f32[8,1024,1024]{2,1,0:T(8,128)}) custom-call(bf16[8,4,2,128,128]{4,3,2,1,0:T(8,128)(2,1)} %bitcast.8, f32[8,1024,1024]{2,1,0:T(8,128)} %get-tuple-element.40.refs_0_, f32[8,1024,1024]{2,1,0:T(8,128)} %get-tuple-element.41.refs_1_), custom_call_target="tpu_custom_call", output_to_operand_aliasing={{0}: (1, {}), {1}: (2, {})} | custom-call | flops 4294967296 | bytes 10485760 | tf_op jit(solution)/shard_map/visibilities/pallas_call | solution.py:196
  473.3 0.0 all-to-all-done
  473.3 0.0 copy-start
  473.3 1.3 copy-done
  474.6 8.6 %visibilities.15 = (f32[8,1024,1024]{2,1,0:T(8,128)}, f32[8,1024,1024]{2,1,0:T(8,128)}) custom-call(bf16[8,4,2,128,128]{4,3,2,1,0:T(8,128)(2,1)} %bitcast.9, f32[8,1024,1024]{2,1,0:T(8,128)} %get-tuple-element.42.refs_0_, f32[8,1024,1024]{2,1,0:T(8,128)} %get-tuple-element.43.refs_1_), custom_call_target="tpu_custom_call", output_to_operand_aliasing={{0}: (1, {}), {1}: (2, {})} | custom-call | flops 4294967296 | bytes 10485760 | tf_op jit(solution)/shard_map/visibilities/pallas_call | solution.py:196
Async XLA Ops:
  1.8 3.7 collective-permute-start
  5.5 0.8 copy-start.2
  32.0 61.6 %all-to-all-start.7 = ((bf16[32,2,128,128]{3,2,1,0:T(8,128)(2,1)}), bf16[32,2,128,128]{3,2,1,0:T(8,128)(2,1)S(1)}, u32[]{:S(2)}, u32[]{:S(2)}) async-start(bf16[32,2,128,128]{3,2,1,0:T(8,128)(2,1)} %spectra.3), calls=%async_computation.7 | async-start | bytes 4194304 | tf_op jit(solution)/shard_map/all_to_all | solution.py:235
  93.6 315.3 %copy-start.1 = (bf16[32,2,128,128]{3,2,1,0:T(8,128)(2,1)}, bf16[32,2,128,128]{3,2,1,0:T(8,128)(2,1)S(1)}, u32[]{:S(2)}) copy-start(bf16[32,2,128,128]{3,2,1,0:T(8,128)(2,1)S(1)} %all-to-all-done.7) | copy-start | bytes 6291460
  408.8 64.4 %all-to-all-start = ((bf16[32,2,128,128]{3,2,1,0:T(8,128)(2,1)}), bf16[32,2,128,128]{3,2,1,0:T(8,128)(2,1)S(1)}, u32[]{:S(2)}, u32[]{:S(2)}) async-start(bf16[32,2,128,128]{3,2,1,0:T(8,128)(2,1)} %get-tuple-element.23), calls=%async_computation | async-start | bytes 4194304 | tf_op jit(solution)/shard_map/all_to_all | solution.py:235
  473.3 1.3 copy-start

commit v2 on v1

--- a/solution.py
+++ b/solution.py
@@ -35,22 +35,99 @@
     return 1.0 / (56.0 * np.sqrt(FFT * energy))
 
 
-def build_transform(chunks, devices, chan_local, folds):
-    scale = spectrum_scale(build_taps())
-    points = np.arange(FFT // folds)
+def build_dft(channels, devices, chan_local, points):
     rows = []
-    for chunk in chunks:
-        channel = np.arange(devices) * chan_local + chunk
-        angle = (channel[:, None] * points[None, :] % FFT) * (2.0 * np.pi / FFT)
+    for channel in channels:
+        whole = np.arange(devices) * chan_local + channel
+        angle = (whole[:, None] * np.arange(points)[None, :] % FFT) * (2.0 * np.pi / FFT)
         rows.append(np.stack([np.cos(angle), -np.sin(angle)], axis=1))
-    matrix = (np.concatenate(rows) * scale).reshape(-1, FFT // folds).astype(np.float32)
+    return (np.concatenate(rows) * spectrum_scale(build_taps())).reshape(-1, points)
+
+
+def split_high_low(matrix):
+    matrix = matrix.astype(np.float32)
     high = matrix.astype(jnp.bfloat16)
-    low = (matrix - high.astype(np.float32)).astype(jnp.bfloat16)
+    return high, (matrix - high.astype(np.float32)).astype(jnp.bfloat16)
+
+
+def build_transform(channels, devices, chan_local, folds):
+    high, low = split_high_low(build_dft(channels, devices, chan_local, FFT // folds))
     return np.concatenate([high, high, low], axis=1)
 
 
-def spectra_kernel(groups, folds, *refs):
-    chunk_count = sum(len(chunks) for _, chunks in groups)
+def build_direct(channel, devices, chan_local):
+    matrix = build_dft([channel], devices, chan_local, FFT)
+    high, low = split_high_low(np.concatenate([matrix * taps[None, :] for taps in build_taps()]))
+    return np.concatenate([high, low], axis=0)
+
+
+def direct_kernel(voltages, halo, transform, *refs):
+    output, products, turned = refs[-3:]
+    inputs_here = voltages.shape[0]
+    rows = turned.shape[0] // FRAME_BLOCK
+    batch = 2 if inputs_here == 128 else 1
+
+    def multiply(target, source, frames):
+        for first in range(0, frames, batch):
+            count = min(batch, frames - first)
+            frame_list = [source[:, frame * FFT : (frame + 1) * FFT] for frame in range(first, first + count)]
+            samples = jnp.concatenate(frame_list, axis=0).astype(jnp.float32).astype(jnp.bfloat16)
+            result = lax.dot_general(
+                transform[...], samples, (((1,), (1,)), ((), ())), preferred_element_type=jnp.float32
+            )
+            for frame in range(count):
+                products[target + first + frame] = result[:, frame * inputs_here : (frame + 1) * inputs_here]
+
+    @pl.when(pl.program_id(0) == 0)
+    def _():
+        multiply(0, halo, HISTORY)
+
+    multiply(HISTORY, voltages, FRAME_BLOCK)
+    for frame in range(FRAME_BLOCK):
+        total = None
+        for part in (1, 0):
+            for offset in range(TAPS):
+                start = (part * TAPS + offset) * rows
+                term = products[frame + offset, start : start + rows, :]
+                total = term if total is None else total + term
+        turned[pl.ds(frame, rows, stride=FRAME_BLOCK), :] = total
+    for frame in range(HISTORY):
+        products[frame] = products[FRAME_BLOCK + frame]
+    output[...] = turned[...].reshape(output.shape).astype(jnp.bfloat16)
+
+
+def direct_spectra(voltages, halo, before, channel, blocks, devices, chan_local):
+    inputs_here = voltages.shape[0]
+    frames_dev = voltages.shape[1] // FFT
+    transform = jnp.asarray(build_direct(channel, devices, chan_local))
+    shape = (devices, 1, 2, frames_dev, inputs_here)
+    return pl.pallas_call(
+        direct_kernel,
+        grid=(blocks,),
+        in_specs=[
+            pl.BlockSpec((inputs_here, FRAME_BLOCK * FFT), lambda step: (0, step)),
+            pl.BlockSpec((inputs_here, HISTORY * FFT), lambda step: (0, 0)),
+            pl.BlockSpec(transform.shape, lambda step: (0, 0)),
+        ]
+        + [pl.BlockSpec(memory_space=pl.ANY) for _ in before],
+        out_specs=pl.BlockSpec((devices, 1, 2, FRAME_BLOCK, inputs_here), lambda step: (0, 0, 0, step, 0)),
+        out_shape=jax.ShapeDtypeStruct(shape, jnp.bfloat16),
+        input_output_aliases={3: 0} if before else {},
+        scratch_shapes=[
+            pltpu.VMEM((HISTORY + FRAME_BLOCK, transform.shape[0], inputs_here), jnp.float32),
+            pltpu.VMEM((devices * 2 * FRAME_BLOCK, inputs_here), jnp.float32),
+        ],
+        compiler_params=pltpu.CompilerParams(vmem_limit_bytes=VMEM_LIMIT),
+        cost_estimate=pl.CostEstimate(
+            flops=2 * blocks * FRAME_BLOCK * inputs_here * FFT * transform.shape[0],
+            bytes_accessed=blocks * FRAME_BLOCK * inputs_here * (4 * FFT + 4 * devices),
+            transcendentals=0,
+        ),
+        name="direct_spectra",
+    )(voltages, halo, transform, *before)
+
+
+def spectra_kernel(groups, folds, places, chunk_count, *refs):
     voltages, halo, taps = refs[:3]
     transforms = refs[3 : 3 + len(groups)]
     outputs = refs[3 + len(groups) : 3 + len(groups) + chunk_count]
@@ -99,9 +176,8 @@
 
     lax.fori_loop(0, inputs_here // ROWS, filter_rows, 0)
 
-    position = 0
-    for (_, chunks), transform, source in zip(groups, transforms, folded):
-        per_chunk = transform.shape[0] // len(chunks)
+    for (_, channels), transform, source in zip(groups, transforms, folded):
+        per_channel = transform.shape[0] // len(channels)
         batch = max(1, min(FRAME_BLOCK, 256 // inputs_here)) if inputs_here >= lanes else 1
         for first in range(0, FRAME_BLOCK, batch):
             result = lax.dot_general(
@@ -114,30 +190,29 @@
                 turned[pl.ds(first + frame, transform.shape[0], stride=FRAME_BLOCK), :] = result[
                     :, frame * inputs_here : (frame + 1) * inputs_here
                 ]
-        for index in range(len(chunks)):
-            start = index * per_chunk * FRAME_BLOCK
-            block = turned[start : start + per_chunk * FRAME_BLOCK, :]
-            outputs[position][...] = block.reshape(outputs[position].shape).astype(jnp.bfloat16)
-            position += 1
+        for index, channel in enumerate(channels):
+            start = index * per_channel * FRAME_BLOCK
+            block = turned[start : start + per_channel * FRAME_BLOCK, :]
+            chunk, slot = places[channel]
+            block = block.reshape(per_channel // 2, 2, FRAME_BLOCK, inputs_here)
+            outputs[chunk][:, slot] = block.astype(jnp.bfloat16)
 
 
 def spectra(voltages, halo, chunks, devices, chan_local):
     folds = 2 if chan_local % 2 == 0 else 1
     inputs_here = voltages.shape[0]
     frames_dev = voltages.shape[1] // FFT
+    places = {channel: (index, slot) for index, chunk in enumerate(chunks) for slot, channel in enumerate(chunk)}
     groups = []
     for residue in range(folds):
-        members = [chunk for chunk in chunks if chunk % folds == residue]
+        members = [channel for channel in sorted(places) if channel % folds == residue]
         if members:
             groups.append((residue, members))
     transforms = [jnp.asarray(build_transform(members, devices, chan_local, folds)) for _, members in groups]
-    order = [chunk for _, members in groups for chunk in members]
-    shape = (devices, 2, frames_dev, inputs_here)
-    block = (devices, 2, FRAME_BLOCK, inputs_here)
     depth = 3 * (FFT // folds)
     most = max(transform.shape[0] for transform in transforms)
-    results = pl.pallas_call(
-        functools.partial(spectra_kernel, groups, folds),
+    return pl.pallas_call(
+        functools.partial(spectra_kernel, groups, folds, places, len(chunks)),
         grid=(frames_dev // FRAME_BLOCK,),
         in_specs=[
             pl.BlockSpec((inputs_here, FRAME_BLOCK * FFT), lambda step: (0, step)),
@@ -145,8 +220,13 @@
             pl.BlockSpec((TAPS, FFT), lambda step: (0, 0)),
         ]
         + [pl.BlockSpec(transform.shape, lambda step: (0, 0)) for transform in transforms],
-        out_specs=[pl.BlockSpec(block, lambda step: (0, 0, step, 0)) for _ in order],
-        out_shape=[jax.ShapeDtypeStruct(shape, jnp.bfloat16) for _ in order],
+        out_specs=[
+            pl.BlockSpec((devices, len(chunk), 2, FRAME_BLOCK, inputs_here), lambda step: (0, 0, 0, step, 0))
+            for chunk in chunks
+        ],
+        out_shape=[
+            jax.ShapeDtypeStruct((devices, len(chunk), 2, frames_dev, inputs_here), jnp.bfloat16) for chunk in chunks
+        ],
         scratch_shapes=[
             pltpu.VMEM((inputs_here, HISTORY * FFT), jnp.float32),
             pltpu.VMEM((most * FRAME_BLOCK, inputs_here), jnp.float32),
@@ -155,27 +235,27 @@
         compiler_params=pltpu.CompilerParams(vmem_limit_bytes=VMEM_LIMIT),
         cost_estimate=pl.CostEstimate(
             flops=2 * frames_dev * inputs_here * depth * sum(transform.shape[0] for transform in transforms),
-            bytes_accessed=voltages.size * 4 + 2 * len(order) * int(np.prod(shape)),
+            bytes_accessed=frames_dev * inputs_here * (4 * FFT + 4 * devices * len(places)),
             transcendentals=0,
         ),
         name="spectra",
     )(voltages, halo, jnp.asarray(build_taps().astype(np.float32)), *transforms)
-    return dict(zip(order, results))
-
-
-def visibility_kernel(received, *refs):
-    real_out, imag_out, across, turned, swapped = refs[-5:]
-    chan_count, blk_count, _, frames_dev, inputs_here = received.shape
+
+
+def visibility_kernel(carried, received, *refs):
+    across, turned, swapped = refs[-3:]
+    real_out, imag_out = refs[-5 - carried : -3 - carried]
+    chan_count, blk_count, _, _, frames_dev, inputs_here = received.shape
     depth = blk_count * 2 * frames_dev
     total_frames = blk_count * frames_dev
     row_block = real_out.shape[1]
 
-    @pl.when(pl.program_id(0) == 0)
+    @pl.when(pl.program_id(1) == 0)
     def _():
         for chan in range(chan_count):
             across[:, chan * inputs_here : (chan + 1) * inputs_here] = received[chan].reshape(depth, inputs_here)
 
-    start = pl.multiple_of(pl.program_id(0) * row_block, row_block)
+    start = pl.multiple_of(pl.program_id(1) * row_block, row_block)
     turned[...] = across[:, pl.ds(start, row_block)].T
     for blk in range(blk_count):
         at = blk * 2 * frames_dev
@@ -186,21 +266,29 @@
     imag_out[0] = jnp.dot(swapped[...], everything, preferred_element_type=jnp.float32) / total_frames
 
 
-def visibilities(received, before, chunk, chan_local):
-    chan_count, blk_count, _, frames_dev, inputs_here = received.shape
+def visibilities(received, before, carry, chunk, chan_local):
+    chan_count, blk_count, channels, _, frames_dev, inputs_here = received.shape
     inputs = chan_count * inputs_here
     depth = blk_count * 2 * frames_dev
     row_block = 256
     shape = jax.ShapeDtypeStruct((chan_local, inputs, inputs), jnp.float32)
-    out_spec = pl.BlockSpec((1, row_block, inputs), lambda step: (chunk, step, 0))
-    return pl.pallas_call(
-        visibility_kernel,
-        grid=(inputs // row_block,),
-        in_specs=[pl.BlockSpec(received.shape, lambda step: (0, 0, 0, 0, 0))]
-        + [pl.BlockSpec(memory_space=pl.ANY) for _ in before],
-        out_specs=[out_spec, out_spec],
-        out_shape=[shape, shape],
-        input_output_aliases={1 + index: index for index in range(len(before))},
+    out_spec = pl.BlockSpec((1, row_block, inputs), lambda channel, step: (chunk[0] + channel, step, 0))
+    anywhere = pl.BlockSpec(memory_space=pl.ANY)
+    aliases = {1 + index: index for index in range(len(before))}
+    aliases.update({1 + len(before) + index: 2 + index for index in range(len(carry))})
+    results = pl.pallas_call(
+        functools.partial(visibility_kernel, len(carry)),
+        grid=(channels, inputs // row_block),
+        in_specs=[
+            pl.BlockSpec(
+                (chan_count, blk_count, 1, 2, frames_dev, inputs_here), lambda channel, step: (0, 0, channel, 0, 0, 0)
+            )
+        ]
+        + [anywhere for _ in before]
+        + [anywhere for _ in carry],
+        out_specs=[out_spec, out_spec] + [anywhere for _ in carry],
+        out_shape=[shape, shape] + [jax.ShapeDtypeStruct(array.shape, array.dtype) for array in carry],
+        input_output_aliases=aliases,
         scratch_shapes=[
             pltpu.VMEM((depth, inputs), jnp.bfloat16),
             pltpu.VMEM((row_block, depth), jnp.bfloat16),
@@ -208,12 +296,20 @@
         ],
         compiler_params=pltpu.CompilerParams(vmem_limit_bytes=VMEM_LIMIT),
         cost_estimate=pl.CostEstimate(
-            flops=4 * inputs * inputs * depth,
-            bytes_accessed=2 * received.size + 8 * inputs * inputs,
+            flops=4 * channels * inputs * inputs * depth,
+            bytes_accessed=2 * received.size + 8 * channels * inputs * inputs,
             transcendentals=0,
         ),
         name="visibilities",
-    )(received, *before)
+    )(received, *before, *carry)
+    return tuple(results[:2]), list(results[2:])
+
+
+def split_channels(chan_local):
+    if chan_local < 4:
+        return [[channel] for channel in range(chan_local)]
+    middle = list(range(1, chan_local - 1))
+    return [[0]] + [middle[start : start + 2] for start in range(0, len(middle), 2)] + [[chan_local - 1]]
 
 
 def local(voltages):
@@ -225,16 +321,24 @@
     chan_local = NC // devices
     tail = voltages[:, (frames_dev - HISTORY) * FFT :].astype(jnp.bfloat16)
     halo = shifted(tail, "blk", 1)
-    first = [0]
-    rest = list(range(1, chan_local))
-    sent = spectra(voltages, halo, first, devices, chan_local)
-    if rest:
-        sent.update(spectra(voltages, halo, rest, devices, chan_local))
+    chunks = split_channels(chan_local)
+    if len(chunks) > 1:
+        nothing = jnp.zeros_like(tail)
+        early = direct_spectra(voltages, nothing, [], 0, frames_dev // FRAME_BLOCK, devices, chan_local)
+        sent = [direct_spectra(voltages, halo, [early], 0, 1, devices, chan_local)]
+        sent += spectra(voltages, halo, chunks[1:], devices, chan_local)
+    else:
+        sent = spectra(voltages, halo, chunks, devices, chan_local)
     outputs = ()
-    for chunk in range(chan_local):
-        received = lax.all_to_all(sent[chunk], ("chan", "blk"), split_axis=0, concat_axis=0, tiled=True)
-        received = received.reshape(chan_count, blk_count, 2, frames_dev, inputs_here)
-        outputs = visibilities(received, outputs, chunk, chan_local)
+    received = []
+    for index, chunk in enumerate(chunks):
+        if index >= 2:
+            outputs, carried = visibilities(received[index - 2], outputs, [sent[index]], chunks[index - 2], chan_local)
+            sent[index] = carried[0]
+        arrived = lax.all_to_all(sent[index], ("chan", "blk"), split_axis=0, concat_axis=0, tiled=True)
+        received.append(arrived.reshape(chan_count, blk_count, len(chunk), 2, frames_dev, inputs_here))
+    for index in range(max(0, len(chunks) - 2), len(chunks)):
+        outputs, _ = visibilities(received[index], outputs, [], chunks[index], chan_local)
     return tuple(outputs)
 
 

time: 484 us -> 444 us (0.917)
  blocking collectives: 315 us -> 0 us
  waiting for transfers between devices: 4.68 us -> 278 us
  starting transfers between devices: 18.9 us -> 26 us
  Pallas kernels: 140 us -> 133 us
    all_to_all x6 -> x0, blocking collectives: 315 us -> none  [local(): lax.all_to_all(sent[chunk], ('chan', 'blk'), split_axis=0, concat_axis=0,...]
    all_to_all x2 -> x5, waiting for transfers between devices: 3.37 us -> 278 us  [local(): lax.all_to_all(sent[index], ('chan', 'blk'), split_axis=0, concat_axis=0,...]
    pallas_call x10 -> x8, Pallas kernels: 140 us -> 133 us  [the longest x5 64.7 us: visibilities(): pl.pallas_call(functools.partial(visibility_kernel, len(carry)), grid=(ch...]
    all_to_all x2 -> x5, starting transfers between devices: 16.5 us -> 23.6 us  [local(): lax.all_to_all(sent[index], ('chan', 'blk'), split_axis=0, concat_axis=0,...]
  transfers between devices with their start and end apart: 3 -> 6, of which waited for: 2 -> 5; matrix products, arithmetic and copies ran while one was open for 0% -> 0% of each run, Pallas kernels for 22% -> 27%
where the time goes in v2:
time: 444 us; the launch traced here: 443 us
  waiting for transfers between devices  278 us (63%)
  Pallas kernels  133 us (30%)
  starting transfers between devices  26 us (6%)
    all_to_all x5, waiting for transfers between devices, local(): lax.all_to_all(sent[index], ('chan', 'blk'), split_axis=0, concat_axis=0,...  278 us
    pallas_call x5, Pallas kernels, visibilities(): pl.pallas_call(functools.partial(visibility_kernel, len(carry)), grid=(ch...  64.7 us
    pallas_call x1, Pallas kernels, spectra(): pl.pallas_call(functools.partial(spectra_kernel, groups, folds, places, l...  45.6 us
    all_to_all x5, starting transfers between devices, local(): lax.all_to_all(sent[index], ('chan', 'blk'), split_axis=0, concat_axis=0,...  23.6 us
    pallas_call x2, Pallas kernels, direct_spectra(): pl.pallas_call(direct_kernel, grid=(blocks,), in_specs=[pl.BlockSpec((inp...  23.1 us
  transfers between devices with their start and end apart: 6, of which 5 were waited for; matrix products, arithmetic and copies ran while one was open for 0% of the time, Pallas kernels for 27%

profile of v2, /device:TPU:0, one launch (start us, length us, event | category | flops | bytes accessed | tf_op | source)
XLA Modules:
  0.0 443.0 jit_solution(12369342115057844396)
XLA Ops:
  0.6 1.2 slice_convert_fusion
  1.8 2.4 collective-permute-start
  4.2 0.8 broadcast_in_dim.3.halo
  5.0 18.3 %direct_spectra.2.refs_0_ = bf16[32,1,2,128,128]{4,3,2,1,0:T(8,128)(2,1)} custom-call(s32[128,65536]{1,0:T(8,128)} %refs_0_.1, bf16[128,1536]{1,0:T(8,128)(2,1)} %broadcast_in_dim.3.halo, bf16[512,512]{1,0:T(8,128)(2,1)} %constant.10.clone.transform), custom_call_target="tpu_custom_call" | custom-call | flops 8589934592 | bytes 35651584 | tf_op jit(solution)/shard_map/direct_spectra/pallas_call | solution.py:104
  23.3 0.0 collective-permute-done.halo.refs_1_
  23.3 0.0 copy-start.2
  23.3 0.7 copy-done.2
  24.0 4.8 %direct_spectra.3 = bf16[32,1,2,128,128]{4,3,2,1,0:T(8,128)(2,1)} custom-call(s32[128,65536]{1,0:T(8,128)} %refs_0_.1, bf16[128,1536]{1,0:T(8,128)(2,1)} %copy-done.2, bf16[512,512]{1,0:T(8,128)(2,1)} %constant.10.clone.transform, bf16[32,1,2,128,128]{4,3,2,1,0:T(8,128)(2,1)} %direct_spectra.2.refs_0_), custom_call_target="tpu_custom_call", output_to_operand_aliasing={{}: (3, {})} | custom-call | flops 1073741824 | bytes 4456448 | tf_op jit(solution)/shard_map/direct_spectra/pallas_call | solution.py:104
  28.8 7.1 %all-to-all-start = ((bf16[32,1,2,128,128]{4,3,2,1,0:T(8,128)(2,1)}), bf16[32,1,2,128,128]{4,3,2,1,0:T(8,128)(2,1)S(1)}, u32[]{:S(2)}, u32[]{:S(2)}) async-start(bf16[32,1,2,128,128]{4,3,2,1,0:T(8,128)(2,1)} %direct_spectra.3), calls=%async_computation | async-start | bytes 4194304 | tf_op jit(solution)/shard_map/all_to_all | solution.py:338
  35.9 45.6 %spectra.1 = (bf16[32,2,2,128,128]{4,3,2,1,0:T(8,128)(2,1)}, bf16[32,2,2,128,128]{4,3,2,1,0:T(8,128)(2,1)}, bf16[32,2,2,128,128]{4,3,2,1,0:T(8,128)(2,1)}, bf16[32,1,2,128,128]{4,3,2,1,0:T(8,128)(2,1)}) custom-call(s32[128,65536]{1,0:T(8,128)} %refs_0_.1, bf16[128,1536]{1,0:T(8,128)(2,1)} %copy-done.2, f32[4,512]{1,0:T(4,128)} %constant.13.clone.refs_2_, ...), custom_call_target="tpu_custom_call" | custom-call | flops 11274289152 | bytes 48234496 | tf_op jit(solution)/shard_map/spectra/pallas_call | solution.py:214
  81.5 3.3 all-to-all-done
  84.8 0.0 copy-start.1
  84.8 1.3 copy-done.1
  86.1 4.1 all-to-all-start.2
  90.3 8.7 %visibilities.5 = (f32[8,1024,1024]{2,1,0:T(8,128)}, f32[8,1024,1024]{2,1,0:T(8,128)}, bf16[32,2,2,128,128]{4,3,2,1,0:T(8,128)(2,1)}) custom-call(bf16[8,4,1,2,128,128]{5,4,3,2,1,0:T(8,128)(2,1)} %bitcast.6, bf16[32,2,2,128,128]{4,3,2,1,0:T(8,128)(2,1)} %get-tuple-element.17.refs_0_), custom_call_target="tpu_custom_call", output_to_operand_aliasing={{2}: (1, {})} | custom-call | flops 4294967296 | bytes 10485760 | tf_op jit(solution)/shard_map/visibilities/pallas_call | solution.py:279
  99.0 85.2 %all-to-all-done.2 = bf16[32,2,2,128,128]{4,3,2,1,0:T(8,128)(2,1)} async-done(((bf16[32,2,2,128,128]{4,3,2,1,0:T(8,128)(2,1)}), bf16[32,2,2,128,128]{4,3,2,1,0:T(8,128)(2,1)}, u32[]{:S(2)}, u32[]{:S(2)}) %all-to-all-start.2) | async-done | bytes 4194336 | tf_op jit(solution)/shard_map/all_to_all | solution.py:338
  184.2 4.1 all-to-all-start.1
  188.3 15.8 %visibilities.6 = (f32[8,1024,1024]{2,1,0:T(8,128)}, f32[8,1024,1024]{2,1,0:T(8,128)}, bf16[32,2,2,128,128]{4,3,2,1,0:T(8,128)(2,1)}) custom-call(bf16[8,4,2,2,128,128]{5,4,3,2,1,0:T(8,128)(2,1)} %bitcast.2.received, f32[8,1024,1024]{2,1,0:T(8,128)} %get-tuple-element.20.refs_0_, ...), custom_call_target="tpu_custom_call", output_to_operand_aliasing={{0}: (1, {}), {1}: (2, {}), {2}: (3, {})} | custom-call | flops 8589934592 | bytes 20971520 | tf_op jit(solution)/shard_map/visibilities/pallas_call | solution.py:279
  204.0 78.1 %all-to-all-done.1 = bf16[32,2,2,128,128]{4,3,2,1,0:T(8,128)(2,1)} async-done(((bf16[32,2,2,128,128]{4,3,2,1,0:T(8,128)(2,1)}), bf16[32,2,2,128,128]{4,3,2,1,0:T(8,128)(2,1)}, u32[]{:S(2)}, u32[]{:S(2)}) %all-to-all-start.1) | async-done | bytes 4194336 | tf_op jit(solution)/shard_map/all_to_all | solution.py:338
  282.1 4.1 all-to-all-start.4
  286.2 15.8 %visibilities.7 = (f32[8,1024,1024]{2,1,0:T(8,128)}, f32[8,1024,1024]{2,1,0:T(8,128)}, bf16[32,1,2,128,128]{4,3,2,1,0:T(8,128)(2,1)}) custom-call(bf16[8,4,2,2,128,128]{5,4,3,2,1,0:T(8,128)(2,1)} %bitcast.1.received, f32[8,1024,1024]{2,1,0:T(8,128)} %get-tuple-element.23.refs_0_, ...), custom_call_target="tpu_custom_call", output_to_operand_aliasing={{0}: (1, {}), {1}: (2, {}), {2}: (3, {})} | custom-call | flops 8589934592 | bytes 20971520 | tf_op jit(solution)/shard_map/visibilities/pallas_call | solution.py:279
  302.0 78.1 %all-to-all-done.4 = bf16[32,2,2,128,128]{4,3,2,1,0:T(8,128)(2,1)} async-done(((bf16[32,2,2,128,128]{4,3,2,1,0:T(8,128)(2,1)}), bf16[32,2,2,128,128]{4,3,2,1,0:T(8,128)(2,1)}, u32[]{:S(2)}, u32[]{:S(2)}) %all-to-all-start.4) | async-done | bytes 4194336 | tf_op jit(solution)/shard_map/all_to_all | solution.py:338
  380.1 4.1 all-to-all-start.3
  384.3 15.8 %visibilities.8 = (f32[8,1024,1024]{2,1,0:T(8,128)}, f32[8,1024,1024]{2,1,0:T(8,128)}) custom-call(bf16[8,4,2,2,128,128]{5,4,3,2,1,0:T(8,128)(2,1)} %bitcast.4.received, f32[8,1024,1024]{2,1,0:T(8,128)} %get-tuple-element.28.refs_0_, f32[8,1024,1024]{2,1,0:T(8,128)} %get-tuple-element.29.refs_1_), custom_call_target="tpu_custom_call", output_to_operand_aliasing={{0}: (1, {}), {1}: (2, {})} | custom-call | flops 8589934592 | bytes 20971520 | tf_op jit(solution)/shard_map/visibilities/pallas_call | solution.py:279
  400.0 33.0 %all-to-all-done.3 = bf16[32,1,2,128,128]{4,3,2,1,0:T(8,128)(2,1)S(1)} async-done(((bf16[32,1,2,128,128]{4,3,2,1,0:T(8,128)(2,1)}), bf16[32,1,2,128,128]{4,3,2,1,0:T(8,128)(2,1)S(1)}, u32[]{:S(2)}, u32[]{:S(2)}) %all-to-all-start.3) | async-done | bytes 2097184 | tf_op jit(solution)/shard_map/all_to_all | solution.py:338
  433.0 0.0 copy-start
  433.0 1.3 copy-done
  434.4 8.7 %visibilities.9 = (f32[8,1024,1024]{2,1,0:T(8,128)}, f32[8,1024,1024]{2,1,0:T(8,128)}) custom-call(bf16[8,4,1,2,128,128]{5,4,3,2,1,0:T(8,128)(2,1)} %bitcast.5, f32[8,1024,1024]{2,1,0:T(8,128)} %get-tuple-element.30.refs_0_, f32[8,1024,1024]{2,1,0:T(8,128)} %get-tuple-element.31.refs_1_), custom_call_target="tpu_custom_call", output_to_operand_aliasing={{0}: (1, {}), {1}: (2, {})} | custom-call | flops 4294967296 | bytes 10485760 | tf_op jit(solution)/shard_map/visibilities/pallas_call | solution.py:279
Async XLA Ops:
  1.8 21.5 %collective-permute-start = (bf16[128,1536]{1,0:T(8,128)(2,1)S(1)}, bf16[128,1536]{1,0:T(8,128)(2,1)S(1)}, u32[]{:S(2)}, u32[]{:S(2)}) collective-permute-start(bf16[128,1536]{1,0:T(8,128)(2,1)S(1)} %slice_convert_fusion), channel_id=1, source_target_pairs={{0,1},{1,2},{2,3},{4,5},{5,6},{6,7},{8,9},{9,10},{10,11},{12,13},{... | collective-permute-start | bytes 1179656 | tf_op jit(solution)/shard_map/ppermute | solution.py:23
  23.3 0.7 copy-start.2
  28.8 56.0 %all-to-all-start = ((bf16[32,1,2,128,128]{4,3,2,1,0:T(8,128)(2,1)}), bf16[32,1,2,128,128]{4,3,2,1,0:T(8,128)(2,1)S(1)}, u32[]{:S(2)}, u32[]{:S(2)}) async-start(bf16[32,1,2,128,128]{4,3,2,1,0:T(8,128)(2,1)} %direct_spectra.3), calls=%async_computation | async-start | bytes 4194304 | tf_op jit(solution)/shard_map/all_to_all | solution.py:338
  84.8 1.3 copy-start.1
  86.1 98.0 %all-to-all-start.2 = ((bf16[32,2,2,128,128]{4,3,2,1,0:T(8,128)(2,1)}), bf16[32,2,2,128,128]{4,3,2,1,0:T(8,128)(2,1)}, u32[]{:S(2)}, u32[]{:S(2)}) async-start(bf16[32,2,2,128,128]{4,3,2,1,0:T(8,128)(2,1)} %get-tuple-element.19), calls=%async_computation.2 | async-start | bytes 8388608 | tf_op jit(solution)/shard_map/all_to_all | solution.py:338
  184.2 98.0 %all-to-all-start.1 = ((bf16[32,2,2,128,128]{4,3,2,1,0:T(8,128)(2,1)}), bf16[32,2,2,128,128]{4,3,2,1,0:T(8,128)(2,1)}, u32[]{:S(2)}, u32[]{:S(2)}) async-start(bf16[32,2,2,128,128]{4,3,2,1,0:T(8,128)(2,1)} %get-tuple-element.18), calls=%async_computation.1 | async-start | bytes 8388608 | tf_op jit(solution)/shard_map/all_to_all | solution.py:338
  282.1 98.0 %all-to-all-start.4 = ((bf16[32,2,2,128,128]{4,3,2,1,0:T(8,128)(2,1)}), bf16[32,2,2,128,128]{4,3,2,1,0:T(8,128)(2,1)}, u32[]{:S(2)}, u32[]{:S(2)}) async-start(bf16[32,2,2,128,128]{4,3,2,1,0:T(8,128)(2,1)} %get-tuple-element.27), calls=%async_computation.4 | async-start | bytes 8388608 | tf_op jit(solution)/shard_map/all_to_all | solution.py:338
  380.1 52.9 %all-to-all-start.3 = ((bf16[32,1,2,128,128]{4,3,2,1,0:T(8,128)(2,1)}), bf16[32,1,2,128,128]{4,3,2,1,0:T(8,128)(2,1)S(1)}, u32[]{:S(2)}, u32[]{:S(2)}) async-start(bf16[32,1,2,128,128]{4,3,2,1,0:T(8,128)(2,1)} %get-tuple-element.26), calls=%async_computation.3 | async-start | bytes 4194304 | tf_op jit(solution)/shard_map/all_to_all | solution.py:338
  433.0 1.3 copy-start

commit v3 on v2

v3 whole, which is shorter than its diff:
```python
import functools

import jax
import jax.numpy as jnp
import numpy as np
from jax import lax
from jax.experimental import pallas as pl
from jax.experimental.pallas import tpu as pltpu
from jax.sharding import PartitionSpec as P

NC = 256
TAPS = 4
FFT = 512
HISTORY = TAPS - 1
FRAME_BLOCK = 16
ROWS = 16
VMEM_LIMIT = 56 * 1024 * 1024
VISIBILITY_LIMIT = 40 * 1024 * 1024


def shifted(value, axis, steps):
    count = lax.axis_size(axis)
    leading, last = (max(0, -steps), min(count, count - steps))
    return lax.ppermute(value, axis, [(source, source + steps) for source in range(leading, last)])


def build_taps():
    length = TAPS * FFT
    points = np.arange(length, dtype=np.float64)
    window = 0.54 - 0.46 * np.cos(2.0 * np.pi * points / (length - 1))
    return (np.sinc((points - (length - 1) / 2.0) / FFT) * window).reshape(TAPS, FFT)


def spectrum_scale(filter_taps):
    energy = np.mean(np.sum(filter_taps * filter_taps, axis=0))
    return 1.0 / (56.0 * np.sqrt(FFT * energy))


def build_dft(channels, devices, chan_local, points):
    rows = []
    for channel in channels:
        whole = np.arange(devices) * chan_local + channel
        angle = (whole[:, None] * np.arange(points)[None, :] % FFT) * (2.0 * np.pi / FFT)
        rows.append(np.stack([np.cos(angle), -np.sin(angle)], axis=1))
    return (np.concatenate(rows) * spectrum_scale(build_taps())).reshape(-1, points)


def split_high_low(matrix):
    matrix = matrix.astype(np.float32)
    high = matrix.astype(jnp.bfloat16)
    return high, (matrix - high.astype(np.float32)).astype(jnp.bfloat16)


def build_transform(channels, devices, chan_local, folds):
    high, low = split_high_low(build_dft(channels, devices, chan_local, FFT // folds))
    return np.concatenate([high, high, low], axis=1)


def build_direct(channel, devices, chan_local):
    matrix = build_dft([channel], devices, chan_local, FFT)
    high, low = split_high_low(np.concatenate([matrix * taps[None, :] for taps in build_taps()]))
    return np.concatenate([high, low], axis=0)


def history_specs(history, inputs_here, first_block):
    if len(history) == 1:
        return [pl.BlockSpec((inputs_here, HISTORY * FFT), lambda step: (0, 0))]
    before = first_block * FRAME_BLOCK - HISTORY
    return [pl.BlockSpec((inputs_here, FFT), functools.partial(lambda at, step: (0, at), before + k)) for k in range(HISTORY)]


def direct_kernel(history_count, voltages, *refs):
    history = refs[:history_count]
    transform, output, tail, products, turned = refs[history_count:]
    inputs_here = voltages.shape[0]
    rows = turned.shape[0] // FRAME_BLOCK
    batch = 2 if inputs_here == 128 else 1

    def multiply(target, frames):
        for first in range(0, len(frames), batch):
            group = [source[:, at : at + FFT] for source, at in frames[first : first + batch]]
            samples = jnp.concatenate(group, axis=0).astype(jnp.float32).astype(jnp.bfloat16)
            result = lax.dot_general(
                transform[...], samples, (((1,), (1,)), ((), ())), preferred_element_type=jnp.float32
            )
            for frame in range(len(group)):
                products[target + first + frame] = result[:, frame * inputs_here : (frame + 1) * inputs_here]

    @pl.when(pl.program_id(0) == 0)
    def _():
        multiply(0, [(source, 0) for source in history])

    multiply(HISTORY, [(voltages, frame * FFT) for frame in range(FRAME_BLOCK)])
    for frame in range(FRAME_BLOCK):
        total = None
        for part in (1, 0):
            for offset in range(TAPS):
                start = (part * TAPS + offset) * rows
                term = products[frame + offset, start : start + rows, :]
                total = term if total is None else total + term
        turned[pl.ds(frame, rows, stride=FRAME_BLOCK), :] = total
    for frame in range(HISTORY):
        products[frame] = products[FRAME_BLOCK + frame]
    output[...] = turned[...].reshape(output.shape).astype(jnp.bfloat16)

    @pl.when(pl.program_id(0) == pl.num_programs(0) - 1)
    def _():
        tail[...] = voltages[:, (FRAME_BLOCK - HISTORY) * FFT :].astype(jnp.float32).astype(jnp.bfloat16)


def direct_spectra(voltages, channel, first_block, devices, chan_local):
    inputs_here = voltages.shape[0]
    frames = voltages.shape[1] // FFT - first_block * FRAME_BLOCK
    transform = jnp.asarray(build_direct(channel, devices, chan_local))
    history = [voltages] * HISTORY
    return pl.pallas_call(
        functools.partial(direct_kernel, len(history)),
        grid=(frames // FRAME_BLOCK,),
        in_specs=[pl.BlockSpec((inputs_here, FRAME_BLOCK * FFT), lambda step: (0, first_block + step))]
        + history_specs(history, inputs_here, first_block)
        + [pl.BlockSpec(transform.shape, lambda step: (0, 0))],
        out_specs=[
            pl.BlockSpec((devices, 1, 2, FRAME_BLOCK, inputs_here), lambda step: (0, 0, 0, step, 0)),
            pl.BlockSpec((inputs_here, HISTORY * FFT), lambda step: (0, 0)),
        ],
        out_shape=[
            jax.ShapeDtypeStruct((devices, 1, 2, frames, inputs_here), jnp.bfloat16),
            jax.ShapeDtypeStruct((inputs_here, HISTORY * FFT), jnp.bfloat16),
        ],
        scratch_shapes=[
            pltpu.VMEM((HISTORY + FRAME_BLOCK, transform.shape[0], inputs_here), jnp.float32),
            pltpu.VMEM((devices * 2 * FRAME_BLOCK, inputs_here), jnp.float32),
        ],
        compiler_params=pltpu.CompilerParams(vmem_limit_bytes=VMEM_LIMIT),
        cost_estimate=pl.CostEstimate(
            flops=2 * frames * inputs_here * FFT * transform.shape[0],
            bytes_accessed=frames * inputs_here * (4 * FFT + 4 * devices),
            transcendentals=0,
        ),
        name="direct_spectra",
    )(voltages, *history, transform)


def spectra_kernel(groups, folds, places, history_count, array_count, voltages, *refs):
    before = refs[:history_count]
    taps = refs[history_count]
    transforms = refs[history_count + 1 : history_count + 1 + len(groups)]
    history, turned = refs[-2 - len(groups) : len(refs) - len(groups)]
    folded = refs[len(refs) - len(groups) :]
    outputs = refs[-2 - len(groups) - array_count : -2 - len(groups)]
    inputs_here = voltages.shape[0]
    part = FFT // folds
    lanes = 128

    @pl.when(pl.program_id(0) == 0)
    def _():
        at = 0
        for source in before:
            history[:, at : at + source.shape[1]] = source[...].astype(jnp.float32)
            at += source.shape[1]

    def filter_rows(step, carry):
        rows = pl.ds(pl.multiple_of(step * ROWS, ROWS), ROWS)
        for start in range(0, part, lanes):
            pieces = []
            for fold in range(folds):
                column = fold * part + start
                weights = [taps[offset : offset + 1, column : column + lanes] for offset in range(TAPS)]
                past = [history[rows, frame * FFT + column : frame * FFT + column + lanes] for frame in range(HISTORY)]
                filtered = []
                for frame in range(FRAME_BLOCK):
                    at = frame * FFT + column
                    past.append(voltages[rows, at : at + lanes].astype(jnp.float32))
                    value = weights[0] * past[0]
                    for offset in range(1, TAPS):
                        value = value + weights[offset] * past[offset]
                    filtered.append(value)
                    past = past[1:]
                for frame in range(HISTORY):
                    history[rows, frame * FFT + column : frame * FFT + column + lanes] = past[frame]
                pieces.append(filtered)
            for frame in range(FRAME_BLOCK):
                for (residue, _), target in zip(groups, folded):
                    value = pieces[0][frame]
                    if folds == 2:
                        value = value + pieces[1][frame] if residue == 0 else value - pieces[1][frame]
                    high = value.astype(jnp.bfloat16)
                    low = (value - high.astype(jnp.float32)).astype(jnp.bfloat16)
                    at = pl.ds(pl.multiple_of(frame * inputs_here + step * ROWS, ROWS), ROWS)
                    target[at, start : start + lanes] = high
                    target[at, part + start : part + start + lanes] = low
                    target[at, 2 * part + start : 2 * part + start + lanes] = high
        return carry

    lax.fori_loop(0, inputs_here // ROWS, filter_rows, 0)

    for (_, channels), transform, source in zip(groups, transforms, folded):
        per_channel = transform.shape[0] // len(channels)
        batch = max(1, min(FRAME_BLOCK, 256 // inputs_here)) if inputs_here >= lanes else 1
        for first in range(0, FRAME_BLOCK, batch):
            result = lax.dot_general(
                transform[...],
                source[first * inputs_here : (first + batch) * inputs_here, :],
                (((1,), (1,)), ((), ())),
                preferred_element_type=jnp.float32,
            )
            for frame in range(batch):
                turned[pl.ds(first + frame, transform.shape[0], stride=FRAME_BLOCK), :] = result[
                    :, frame * inputs_here : (frame + 1) * inputs_here
                ]
        for index, channel in enumerate(channels):
            start = index * per_channel * FRAME_BLOCK
            block = turned[start : start + per_channel * FRAME_BLOCK, :]
            chunk, slot = places[channel]
            block = block.reshape(per_channel // 2, 2, FRAME_BLOCK, inputs_here)
            outputs[chunk][:, slot] = block.astype(jnp.bfloat16)


def spectra(voltages, history, first_block, blocks, arrays, devices, chan_local):
    folds = 2 if chan_local % 2 == 0 else 1
    inputs_here = voltages.shape[0]
    places = {}
    groups = []
    for index, (channels, _, _, _, _) in enumerate(arrays):
        places.update({channel: (index, slot) for slot, channel in enumerate(channels)})
    for residue in range(folds):
        members = [channel for channel in sorted(places) if channel % folds == residue]
        if members:
            groups.append((residue, members))
    transforms = [jnp.asarray(build_transform(members, devices, chan_local, folds)) for _, members in groups]
    depth = 3 * (FFT // folds)
    most = max(transform.shape[0] for transform in transforms)
    existing = [(index, array[4]) for index, array in enumerate(arrays) if array[4] is not None]
    operand_count = 2 + len(history) + len(transforms)
    frames = blocks * FRAME_BLOCK
    return pl.pallas_call(
        functools.partial(spectra_kernel, groups, folds, places, len(history), len(arrays)),
        grid=(blocks,),
        in_specs=[pl.BlockSpec((inputs_here, FRAME_BLOCK * FFT), lambda step: (0, first_block + step))]
        + history_specs(history, inputs_here, first_block)
        + [pl.BlockSpec((TAPS, FFT), lambda step: (0, 0))]
        + [pl.BlockSpec(transform.shape, lambda step: (0, 0)) for transform in transforms]
        + [pl.BlockSpec(memory_space=pl.ANY) for _ in existing],
        out_specs=[
            pl.BlockSpec(
                (devices, len(channels), 2, FRAME_BLOCK, inputs_here),
                functools.partial(lambda at, step: (0, at, 0, step, 0), slot_block),
            )
            for channels, _, _, slot_block, _ in arrays
        ],
        out_shape=[
            jax.ShapeDtypeStruct((devices, slots, 2, array_frames, inputs_here), jnp.bfloat16)
            for _, slots, array_frames, _, _ in arrays
        ],
        input_output_aliases={operand_count + k: index for k, (index, _) in enumerate(existing)},
        scratch_shapes=[
            pltpu.VMEM((inputs_here, HISTORY * FFT), jnp.float32),
            pltpu.VMEM((most * FRAME_BLOCK, inputs_here), jnp.float32),
        ]
        + [pltpu.VMEM((FRAME_BLOCK * inputs_here, depth), jnp.bfloat16) for _ in groups],
        compiler_params=pltpu.CompilerParams(vmem_limit_bytes=VMEM_LIMIT),
        cost_estimate=pl.CostEstimate(
            flops=2 * frames * inputs_here * depth * sum(transform.shape[0] for transform in transforms),
            bytes_accessed=frames * inputs_here * (4 * FFT + 4 * devices * len(places)),
            transcendentals=0,
        ),
        name="spectra",
    )(
        voltages,
        *history,
        jnp.asarray(build_taps().astype(np.float32)),
        *transforms,
        *[array for _, array in existing],
    )


def visibility_kernel(piece_count, carried, *refs):
    pieces = refs[:piece_count]
    across, turned, swapped = refs[-3:]
    real_out, imag_out = refs[-5 - carried : -3 - carried][:2]
    depth = across.shape[0]
    total_frames = depth // 2
    row_block = real_out.shape[1]

    @pl.when(pl.program_id(1) == 0)
    def _():
        top = 0
        for piece in pieces:
            chan_count, blk_count, _, _, frames, inputs_here = piece.shape
            rows = blk_count * 2 * frames
            for chan in range(chan_count):
                columns = slice(chan * inputs_here, (chan + 1) * inputs_here)
                across[top : top + rows, columns] = piece[chan].reshape(rows, inputs_here)
            top += rows

    start = pl.multiple_of(pl.program_id(1) * row_block, row_block)
    turned[...] = across[:, pl.ds(start, row_block)].T
    top = 0
    for piece in pieces:
        frames = piece.shape[4]
        for at in range(top, top + piece.shape[1] * 2 * frames, 2 * frames):
            swapped[:, at : at + frames] = turned[:, at + frames : at + 2 * frames]
            swapped[:, at + frames : at + 2 * frames] = -turned[:, at : at + frames]
        top += piece.shape[1] * 2 * frames
    everything = across[...]
    real_out[0] = jnp.dot(turned[...], everything, preferred_element_type=jnp.float32) / total_frames
    imag_out[0] = jnp.dot(swapped[...], everything, preferred_element_type=jnp.float32) / total_frames


def visibilities(pieces, channels, before, carry, chan_local, in_vmem=False):
    arrays = [array for array, _ in pieces]
    chan_count, blk_count, _, _, _, inputs_here = arrays[0].shape
    inputs = chan_count * inputs_here
    depth = sum(blk_count * 2 * array.shape[4] for array in arrays)
    row_block = 256
    shape = jax.ShapeDtypeStruct((chan_local, inputs, inputs), jnp.float32)
    out_spec = pl.BlockSpec((1, row_block, inputs), lambda channel, step: (channels[0] + channel, step, 0))
    anywhere = pl.BlockSpec(memory_space=pl.ANY)
    aliases = {len(arrays) + index: index for index in range(len(before))}
    aliases.update({len(arrays) + len(before) + index: 2 + index for index in range(len(carry))})
    if in_vmem:
        piece_specs = [pl.BlockSpec(memory_space=pltpu.VMEM) for _ in arrays]
    else:
        piece_specs = [
            pl.BlockSpec(
                (chan_count, blk_count, 1, 2, array.shape[4], inputs_here),
                functools.partial(lambda slot, channel, step: (0, 0, slot + channel, 0, 0, 0), slot),
            )
            for array, slot in pieces
        ]
    results = pl.pallas_call(
        functools.partial(visibility_kernel, len(arrays), len(carry)),
        grid=(len(channels), inputs // row_block),
        in_specs=piece_specs + [anywhere for _ in before] + [anywhere for _ in carry],
        out_specs=[out_spec, out_spec] + [anywhere for _ in carry],
        out_shape=[shape, shape] + [jax.ShapeDtypeStruct(array.shape, array.dtype) for array in carry],
        input_output_aliases=aliases,
        scratch_shapes=[
            pltpu.VMEM((depth, inputs), jnp.bfloat16),
            pltpu.VMEM((row_block, depth), jnp.bfloat16),
            pltpu.VMEM((row_block, depth), jnp.bfloat16),
        ],
        compiler_params=pltpu.CompilerParams(vmem_limit_bytes=VISIBILITY_LIMIT),
        cost_estimate=pl.CostEstimate(
            flops=4 * len(channels) * inputs * inputs * depth,
            bytes_accessed=len(channels) * (2 * depth * inputs + 8 * inputs * inputs),
            transcendentals=0,
        ),
        name="visibilities",
    )(*arrays, *before, *carry)
    return tuple(results[:2]), list(results[2:])


def local(voltages):
    inputs_here = voltages.shape[0]
    frames_dev = voltages.shape[1] // FFT
    chan_count = lax.axis_size("chan")
    blk_count = lax.axis_size("blk")
    devices = chan_count * blk_count
    chan_local = NC // devices
    blocks = frames_dev // FRAME_BLOCK
    half = blocks // 2

    def exchange(array):
        arrived = lax.all_to_all(array, ("chan", "blk"), split_axis=0, concat_axis=0, tiled=True)
        return arrived.reshape(chan_count, blk_count, *array.shape[1:])

    if chan_local < 4 or chan_local % 2 or blocks % 2:
        tail = voltages[:, (frames_dev - HISTORY) * FFT :].astype(jnp.bfloat16)
        halo = shifted(tail, "blk", 1)
        outputs = ()
        arrays = [([channel], 1, frames_dev, 0, None) for channel in range(chan_local)]
        for channel, array in enumerate(spectra(voltages, [halo], 0, blocks, arrays, devices, chan_local)):
            outputs, _ = visibilities([(exchange(array), 0)], [channel], outputs, [], chan_local)
        return outputs

    first, second, last = 0, 2, 1
    rest = list(range(3, chan_local))
    early, tail = direct_spectra(voltages, first, half, devices, chan_local)
    halo = shifted(tail, "blk", 1)
    half_frames = half * FRAME_BLOCK
    (pair,) = spectra(
        voltages, [voltages] * HISTORY, half, half, [([second], 3, half_frames, 2, None)], devices, chan_local
    )
    (pair,) = spectra(voltages, [halo], 0, half, [([first, second], 3, half_frames, 0, pair)], devices, chan_local)
    many, final = spectra(
        voltages,
        [halo],
        0,
        blocks,
        [(rest, len(rest), frames_dev, 0, None), ([last], 1, frames_dev, 0, None)],
        devices,
        chan_local,
    )
    early = exchange(early)
    pair = exchange(pair)
    many = exchange(many)
    outputs, _ = visibilities([(early, 0), (pair, 0)], [first], (), [], chan_local)
    outputs, (final,) = visibilities([(pair, 1), (pair, 2)], [second], outputs, [final], chan_local)
    final = exchange(final)
    outputs, _ = visibilities([(many, 0)], rest, outputs, [], chan_local)
    outputs, _ = visibilities([(final, 0)], [last], outputs, [], chan_local, in_vmem=True)
    return outputs


def solution(mesh):
    return jax.shard_map(
        local,
        mesh=mesh,
        in_specs=(P("chan", "blk"),),
        out_specs=(P(("chan", "blk"), None, None), P(("chan", "blk"), None, None)),
        check_vma=False,
    )
```

time: 444 us -> 426 us (0.959)
  waiting for transfers between devices: 278 us -> 253 us
  Pallas kernels: 133 us -> 143 us
    pallas_call x1 -> x3, Pallas kernels: 45.6 us -> 74.2 us  [spectra(): pl.pallas_call(functools.partial(spectra_kernel, groups, folds, places, l...]
    all_to_all x5 -> x4, waiting for transfers between devices: 278 us -> 253 us  [exchange(): lax.all_to_all(array, ('chan', 'blk'), split_axis=0, concat_axis=0, tiled...]
    pallas_call x7 -> x5, Pallas kernels: 87.7 us -> 68.9 us  [the longest x4 58.1 us: visibilities(): pl.pallas_call(functools.partial(visibility_kernel, len(arrays), len(carr...]
    all_to_all x5 -> x4, starting transfers between devices: 23.6 us -> 20.1 us  [exchange(): lax.all_to_all(array, ('chan', 'blk'), split_axis=0, concat_axis=0, tiled...]
  transfers between devices with their start and end apart: 6 -> 5, of which waited for: 5 -> 3; matrix products, arithmetic and copies ran while one was open for 0% -> 0% of each run, Pallas kernels for 27% -> 29%
where the time goes in v3:
time: 426 us; the launch traced here: 425 us
  waiting for transfers between devices  253 us (59%)
  Pallas kernels  143 us (34%)
  starting transfers between devices  22.3 us (5%)
  local copies, waits for them, and re-layouts  5.89 us (1%)
    all_to_all x4, waiting for transfers between devices, exchange(): lax.all_to_all(array, ('chan', 'blk'), split_axis=0, concat_axis=0, tiled...  253 us
    pallas_call x3, Pallas kernels, spectra(): pl.pallas_call(functools.partial(spectra_kernel, groups, folds, places, l...  74.2 us
    pallas_call x4, Pallas kernels, visibilities(): pl.pallas_call(functools.partial(visibility_kernel, len(arrays), len(carr...  58.1 us
    all_to_all x4, starting transfers between devices, exchange(): lax.all_to_all(array, ('chan', 'blk'), split_axis=0, concat_axis=0, tiled...  20.1 us
    pallas_call x1, Pallas kernels, direct_spectra(): pl.pallas_call(functools.partial(direct_kernel, len(history)), grid=(fram...  10.8 us
  transfers between devices with their start and end apart: 5, of which 3 were waited for; matrix products, arithmetic and copies ran while one was open for 0% of the time, Pallas kernels for 29%

profile of v3, /device:TPU:0, one launch (start us, length us, event | category | flops | bytes accessed | tf_op | source)
XLA Modules:
  0.0 425.1 jit_solution(1164181530105460607)
XLA Ops:
  0.6 10.8 %direct_spectra.1 = (bf16[32,1,2,64,128]{4,3,2,1,0:T(8,128)(2,1)}, bf16[128,1536]{1,0:T(8,128)(2,1)}) custom-call(s32[128,65536]{1,0:T(8,128)} %voltages.7, s32[128,65536]{1,0:T(8,128)} %voltages.7, s32[128,65536]{1,0:T(8,128)} %voltages.7, s32[128,65536]{1,0:T(8,128)} %voltages.7, bf16[512,512]{1,0:T(8,128)(2,1)} %constant.12.clone.refs_3_), custom_call_target="tpu_custom_call" | custom-call | flops 4294967296 | bytes 17825792 | tf_op jit(solution)/shard_map/direct_spectra/pallas_call | solution.py:116
  11.5 7.3 %all-to-all-start.1 = ((bf16[32,1,2,64,128]{4,3,2,1,0:T(8,128)(2,1)}), bf16[32,1,2,64,128]{4,3,2,1,0:T(8,128)(2,1)S(1)}, u32[]{:S(2)}, u32[]{:S(2)}) async-start(bf16[32,1,2,64,128]{4,3,2,1,0:T(8,128)(2,1)} %get-tuple-element.14), calls=%async_computation.1 | async-start | bytes 2097152 | tf_op jit(solution)/shard_map/all_to_all | solution.py:365
  18.8 2.2 collective-permute-start
  21.0 14.5 %spectra.3.refs_3_ = bf16[32,3,2,64,128]{4,3,2,1,0:T(8,128)(2,1)} custom-call(s32[128,65536]{1,0:T(8,128)} %voltages.7, s32[128,65536]{1,0:T(8,128)} %voltages.7, s32[128,65536]{1,0:T(8,128)} %voltages.7, s32[128,65536]{1,0:T(8,128)} %voltages.7, f32[4,512]{1,0:T(4,128)} %constant.14.clone.refs_3_.refs_1_, bf16[64,768]{1,0:T(8,128)(2,1)} %constant.13.clone.refs_4_), custom_call_target="tpu_custom_call" | custom-call | flops 805306368 | bytes 17825792 | tf_op jit(solution)/shard_map/spectra/pallas_call | solution.py:236
  35.5 0.0 collective-permute-done.refs_0_
  35.5 0.0 copy-start.4
  35.5 0.7 copy-done.4
  36.2 15.3 %spectra.4 = bf16[32,3,2,64,128]{4,3,2,1,0:T(8,128)(2,1)} custom-call(s32[128,65536]{1,0:T(8,128)} %voltages.7, bf16[128,1536]{1,0:T(8,128)(2,1)} %copy-done.4, f32[4,512]{1,0:T(4,128)} %constant.14.clone.refs_3_.refs_1_, bf16[128,768]{1,0:T(8,128)(2,1)} %constant.15.clone.refs_2_, ...), custom_call_target="tpu_custom_call", output_to_operand_aliasing={{}: (4, {})} | custom-call | flops 1610612736 | bytes 18874368 | tf_op jit(solution)/shard_map/spectra/pallas_call | solution.py:236
  51.6 0.0 all-to-all-done.1
  51.6 0.0 copy-start.2
  51.6 1.0 copy-done.2
  52.5 5.8 %all-to-all-start = ((bf16[32,3,2,64,128]{4,3,2,1,0:T(8,128)(2,1)}), bf16[32,3,2,64,128]{4,3,2,1,0:T(8,128)(2,1)S(1)}, u32[]{:S(2)}, u32[]{:S(2)}) async-start(bf16[32,3,2,64,128]{4,3,2,1,0:T(8,128)(2,1)} %spectra.4), calls=%async_computation | async-start | bytes 6291456 | tf_op jit(solution)/shard_map/all_to_all | solution.py:365
  58.4 44.3 %spectra.5 = (bf16[32,5,2,128,128]{4,3,2,1,0:T(8,128)(2,1)}, bf16[32,1,2,128,128]{4,3,2,1,0:T(8,128)(2,1)}) custom-call(s32[128,65536]{1,0:T(8,128)} %voltages.7, bf16[128,1536]{1,0:T(8,128)(2,1)} %copy-done.4, f32[4,512]{1,0:T(4,128)} %constant.14.clone.refs_3_.refs_1_, bf16[128,768]{1,0:T(8,128)(2,1)} %constant.16.clone.refs_2_, ...), custom_call_target="tpu_custom_call" | custom-call | flops 9663676416 | bytes 46137344 | tf_op jit(solution)/shard_map/spectra/pallas_call | solution.py:236
  102.7 27.1 %all-to-all-done = bf16[32,3,2,64,128]{4,3,2,1,0:T(8,128)(2,1)S(1)} async-done(((bf16[32,3,2,64,128]{4,3,2,1,0:T(8,128)(2,1)}), bf16[32,3,2,64,128]{4,3,2,1,0:T(8,128)(2,1)S(1)}, u32[]{:S(2)}, u32[]{:S(2)}) %all-to-all-start) | async-done | bytes 3145760 | tf_op jit(solution)/shard_map/all_to_all | solution.py:365
  129.9 4.0 all-to-all-start.3
  133.9 0.0 copy-start.3
  133.9 1.2 copy-done.3
  135.1 7.0 %visibilities.4 = (f32[8,1024,1024]{2,1,0:T(8,128)}, f32[8,1024,1024]{2,1,0:T(8,128)}) custom-call(bf16[8,4,1,2,64,128]{5,4,3,2,1,0:T(8,128)(2,1)S(1)} %bitcast.8, bf16[8,4,3,2,64,128]{5,4,3,2,1,0:T(8,128)(2,1)S(1)} %bitcast.4), custom_call_target="tpu_custom_call" | custom-call | flops 4294967296 | bytes 10485760 | tf_op jit(solution)/shard_map/visibilities/pallas_call | solution.py:331
  142.2 0.0 copy-start
  142.2 1.6 copy-done
  143.7 7.1 %visibilities.5 = (f32[8,1024,1024]{2,1,0:T(8,128)}, f32[8,1024,1024]{2,1,0:T(8,128)}, bf16[32,1,2,128,128]{4,3,2,1,0:T(8,128)(2,1)S(1)}) custom-call(bf16[8,4,3,2,64,128]{5,4,3,2,1,0:T(8,128)(2,1)S(1)} %bitcast.5, bf16[8,4,3,2,64,128]{5,4,3,2,1,0:T(8,128)(2,1)S(1)} %bitcast.6, ...), custom_call_target="tpu_custom_call", output_to_operand_aliasing={{0}: (2, {}), {1}: (3, {}), {2}: (4, {})} | custom-call | flops 4294967296 | bytes 10485760 | tf_op jit(solution)/shard_map/visibilities/pallas_call | solution.py:331
  150.8 0.0 copy-start.1
  150.8 1.4 copy-done.1
  152.2 214.0 %all-to-all-done.3 = bf16[32,5,2,128,128]{4,3,2,1,0:T(8,128)(2,1)} async-done(((bf16[32,5,2,128,128]{4,3,2,1,0:T(8,128)(2,1)}), bf16[32,5,2,128,128]{4,3,2,1,0:T(8,128)(2,1)}, u32[]{:S(2)}, u32[]{:S(2)}) %all-to-all-start.3) | async-done | bytes 10485792 | tf_op jit(solution)/shard_map/all_to_all | solution.py:365
  366.2 2.9 all-to-all-start.2
  369.1 36.9 %visibilities.6 = (f32[8,1024,1024]{2,1,0:T(8,128)}, f32[8,1024,1024]{2,1,0:T(8,128)}) custom-call(bf16[8,4,5,2,128,128]{5,4,3,2,1,0:T(8,128)(2,1)} %bitcast.3.refs_0_, f32[8,1024,1024]{2,1,0:T(8,128)} %get-tuple-element.20.refs_1_, f32[8,1024,1024]{2,1,0:T(8,128)} %get-tuple-element.21.refs_2_), custom_call_target="tpu_custom_call", output_to_operand_aliasing={{0}: (1, {}), {1}: (2, {})} | custom-call | flops 21474836480 | bytes 52428800 | tf_op jit(solution)/shard_map/visibilities/pallas_call | solution.py:331
  406.0 12.0 %all-to-all-done.2 = bf16[32,1,2,128,128]{4,3,2,1,0:T(8,128)(2,1)S(1)} async-done(((bf16[32,1,2,128,128]{4,3,2,1,0:T(8,128)(2,1)}), bf16[32,1,2,128,128]{4,3,2,1,0:T(8,128)(2,1)S(1)}, u32[]{:S(2)}, u32[]{:S(2)}) %all-to-all-start.2) | async-done | bytes 2097184 | tf_op jit(solution)/shard_map/all_to_all | solution.py:365
  418.0 7.1 %visibilities.7 = (f32[8,1024,1024]{2,1,0:T(8,128)}, f32[8,1024,1024]{2,1,0:T(8,128)}) custom-call(bf16[8,4,1,2,128,128]{5,4,3,2,1,0:T(8,128)(2,1)S(1)} %bitcast.7, f32[8,1024,1024]{2,1,0:T(8,128)} %get-tuple-element.22.refs_1_, f32[8,1024,1024]{2,1,0:T(8,128)} %get-tuple-element.23.refs_2_), custom_call_target="tpu_custom_call", output_to_operand_aliasing={{0}: (1, {}), {1}: (2, {})} | custom-call | flops 4294967296 | bytes 10485760 | tf_op jit(solution)/shard_map/visibilities/pallas_call | solution.py:331
Async XLA Ops:
  11.5 40.1 %all-to-all-start.1 = ((bf16[32,1,2,64,128]{4,3,2,1,0:T(8,128)(2,1)}), bf16[32,1,2,64,128]{4,3,2,1,0:T(8,128)(2,1)S(1)}, u32[]{:S(2)}, u32[]{:S(2)}) async-start(bf16[32,1,2,64,128]{4,3,2,1,0:T(8,128)(2,1)} %get-tuple-element.14), calls=%async_computation.1 | async-start | bytes 2097152 | tf_op jit(solution)/shard_map/all_to_all | solution.py:365
  18.8 16.7 %collective-permute-start = (bf16[128,1536]{1,0:T(8,128)(2,1)}, bf16[128,1536]{1,0:T(8,128)(2,1)S(1)}, u32[]{:S(2)}, u32[]{:S(2)}) collective-permute-start(bf16[128,1536]{1,0:T(8,128)(2,1)} %get-tuple-element.13), channel_id=1, source_target_pairs={{0,1},{1,2},{2,3},{4,5},{5,6},{6,7},{8,9},{9,10},{10,11},{12,13},{... | collective-permute-start | bytes 1179656 | tf_op jit(solution)/shard_map/ppermute | solution.py:24
  35.5 0.7 copy-start.4
  51.6 1.0 copy-start.2
  52.5 77.3 %all-to-all-start = ((bf16[32,3,2,64,128]{4,3,2,1,0:T(8,128)(2,1)}), bf16[32,3,2,64,128]{4,3,2,1,0:T(8,128)(2,1)S(1)}, u32[]{:S(2)}, u32[]{:S(2)}) async-start(bf16[32,3,2,64,128]{4,3,2,1,0:T(8,128)(2,1)} %spectra.4), calls=%async_computation | async-start | bytes 6291456 | tf_op jit(solution)/shard_map/all_to_all | solution.py:365
  129.9 236.3 %all-to-all-start.3 = ((bf16[32,5,2,128,128]{4,3,2,1,0:T(8,128)(2,1)}), bf16[32,5,2,128,128]{4,3,2,1,0:T(8,128)(2,1)}, u32[]{:S(2)}, u32[]{:S(2)}) async-start(bf16[32,5,2,128,128]{4,3,2,1,0:T(8,128)(2,1)} %get-tuple-element.19), calls=%async_computation.3 | async-start | bytes 20971520 | tf_op jit(solution)/shard_map/all_to_all | solution.py:365
  133.9 1.2 copy-start.3
  142.2 1.6 copy-start
  150.8 1.4 copy-start.1
  366.2 51.8 %all-to-all-start.2 = ((bf16[32,1,2,128,128]{4,3,2,1,0:T(8,128)(2,1)}), bf16[32,1,2,128,128]{4,3,2,1,0:T(8,128)(2,1)S(1)}, u32[]{:S(2)}, u32[]{:S(2)}) async-start(bf16[32,1,2,128,128]{4,3,2,1,0:T(8,128)(2,1)} %copy-done.1), calls=%async_computation.2 | async-start | bytes 4194304 | tf_op jit(solution)/shard_map/all_to_all | solution.py:365

commit v4 on v3

--- a/solution.py
+++ b/solution.py
@@ -162,34 +162,31 @@
     def filter_rows(step, carry):
         rows = pl.ds(pl.multiple_of(step * ROWS, ROWS), ROWS)
         for start in range(0, part, lanes):
-            pieces = []
-            for fold in range(folds):
-                column = fold * part + start
-                weights = [taps[offset : offset + 1, column : column + lanes] for offset in range(TAPS)]
-                past = [history[rows, frame * FFT + column : frame * FFT + column + lanes] for frame in range(HISTORY)]
+            columns = [fold * part + start for fold in range(folds)]
+            weights = [[taps[offset : offset + 1, at : at + lanes] for offset in range(TAPS)] for at in columns]
+            past = [[history[rows, k * FFT + at : k * FFT + at + lanes] for k in range(HISTORY)] for at in columns]
+            for frame in range(FRAME_BLOCK):
                 filtered = []
-                for frame in range(FRAME_BLOCK):
+                for fold, column in enumerate(columns):
                     at = frame * FFT + column
-                    past.append(voltages[rows, at : at + lanes].astype(jnp.float32))
-                    value = weights[0] * past[0]
+                    past[fold].append(voltages[rows, at : at + lanes].astype(jnp.float32))
+                    value = weights[fold][0] * past[fold].pop(0)
                     for offset in range(1, TAPS):
-                        value = value + weights[offset] * past[offset]
+                        value = value + weights[fold][offset] * past[fold][offset - 1]
                     filtered.append(value)
-                    past = past[1:]
-                for frame in range(HISTORY):
-                    history[rows, frame * FFT + column : frame * FFT + column + lanes] = past[frame]
-                pieces.append(filtered)
-            for frame in range(FRAME_BLOCK):
                 for (residue, _), target in zip(groups, folded):
-                    value = pieces[0][frame]
+                    value = filtered[0]
                     if folds == 2:
-                        value = value + pieces[1][frame] if residue == 0 else value - pieces[1][frame]
+                        value = value + filtered[1] if residue == 0 else value - filtered[1]
                     high = value.astype(jnp.bfloat16)
                     low = (value - high.astype(jnp.float32)).astype(jnp.bfloat16)
                     at = pl.ds(pl.multiple_of(frame * inputs_here + step * ROWS, ROWS), ROWS)
                     target[at, start : start + lanes] = high
                     target[at, part + start : part + start + lanes] = low
                     target[at, 2 * part + start : 2 * part + start + lanes] = high
+            for fold, at in enumerate(columns):
+                for k in range(HISTORY):
+                    history[rows, k * FFT + at : k * FFT + at + lanes] = past[fold][k]
         return carry
 
     lax.fori_loop(0, inputs_here // ROWS, filter_rows, 0)
@@ -244,13 +241,13 @@
         out_specs=[
             pl.BlockSpec(
                 (devices, len(channels), 2, FRAME_BLOCK, inputs_here),
-                functools.partial(lambda at, step: (0, at, 0, step, 0), slot_block),
+                place,
             )
-            for channels, _, _, slot_block, _ in arrays
+            for channels, _, _, place, _ in arrays
         ],
         out_shape=[
-            jax.ShapeDtypeStruct((devices, slots, 2, array_frames, inputs_here), jnp.bfloat16)
-            for _, slots, array_frames, _, _ in arrays
+            jax.ShapeDtypeStruct((devices, units, 2, unit_frames, inputs_here), jnp.bfloat16)
+            for _, units, unit_frames, _, _ in arrays
         ],
         input_output_aliases={operand_count + k: index for k, (index, _) in enumerate(existing)},
         scratch_shapes=[
@@ -274,34 +271,31 @@
     )
 
 
-def visibility_kernel(piece_count, carried, *refs):
-    pieces = refs[:piece_count]
+def visibility_kernel(piece_units, carried, *refs):
+    pieces = refs[: len(piece_units)]
     across, turned, swapped = refs[-3:]
     real_out, imag_out = refs[-5 - carried : -3 - carried][:2]
-    depth = across.shape[0]
-    total_frames = depth // 2
+    total_frames = across.shape[0] // 2
     row_block = real_out.shape[1]
 
     @pl.when(pl.program_id(1) == 0)
     def _():
         top = 0
-        for piece in pieces:
+        for piece, units in zip(pieces, piece_units):
             chan_count, blk_count, _, _, frames, inputs_here = piece.shape
-            rows = blk_count * 2 * frames
-            for chan in range(chan_count):
-                columns = slice(chan * inputs_here, (chan + 1) * inputs_here)
-                across[top : top + rows, columns] = piece[chan].reshape(rows, inputs_here)
-            top += rows
+            for blk in range(blk_count):
+                for unit in units:
+                    for part in range(2):
+                        rows = slice(part * total_frames + top, part * total_frames + top + frames)
+                        for chan in range(chan_count):
+                            columns = slice(chan * inputs_here, (chan + 1) * inputs_here)
+                            across[rows, columns] = piece[chan, blk, unit, part]
+                    top += frames
 
     start = pl.multiple_of(pl.program_id(1) * row_block, row_block)
     turned[...] = across[:, pl.ds(start, row_block)].T
-    top = 0
-    for piece in pieces:
-        frames = piece.shape[4]
-        for at in range(top, top + piece.shape[1] * 2 * frames, 2 * frames):
-            swapped[:, at : at + frames] = turned[:, at + frames : at + 2 * frames]
-            swapped[:, at + frames : at + 2 * frames] = -turned[:, at : at + frames]
-        top += piece.shape[1] * 2 * frames
+    swapped[:, :total_frames] = turned[:, total_frames:]
+    swapped[:, total_frames:] = -turned[:, :total_frames]
     everything = across[...]
     real_out[0] = jnp.dot(turned[...], everything, preferred_element_type=jnp.float32) / total_frames
     imag_out[0] = jnp.dot(swapped[...], everything, preferred_element_type=jnp.float32) / total_frames
@@ -309,27 +303,27 @@
 
 def visibilities(pieces, channels, before, carry, chan_local, in_vmem=False):
     arrays = [array for array, _ in pieces]
+    piece_units = [units or [0] for _, units in pieces]
     chan_count, blk_count, _, _, _, inputs_here = arrays[0].shape
     inputs = chan_count * inputs_here
-    depth = sum(blk_count * 2 * array.shape[4] for array in arrays)
+    depth = sum(blk_count * 2 * array.shape[4] * len(units) for array, units in zip(arrays, piece_units))
     row_block = 256
     shape = jax.ShapeDtypeStruct((chan_local, inputs, inputs), jnp.float32)
     out_spec = pl.BlockSpec((1, row_block, inputs), lambda channel, step: (channels[0] + channel, step, 0))
     anywhere = pl.BlockSpec(memory_space=pl.ANY)
     aliases = {len(arrays) + index: index for index in range(len(before))}
     aliases.update({len(arrays) + len(before) + index: 2 + index for index in range(len(carry))})
-    if in_vmem:
-        piece_specs = [pl.BlockSpec(memory_space=pltpu.VMEM) for _ in arrays]
-    else:
-        piece_specs = [
-            pl.BlockSpec(
-                (chan_count, blk_count, 1, 2, array.shape[4], inputs_here),
-                functools.partial(lambda slot, channel, step: (0, 0, slot + channel, 0, 0, 0), slot),
-            )
-            for array, slot in pieces
-        ]
+    piece_specs = []
+    for array, units in pieces:
+        if in_vmem:
+            piece_specs.append(pl.BlockSpec(memory_space=pltpu.VMEM))
+        elif units:
+            piece_specs.append(pl.BlockSpec(array.shape, lambda channel, step: (0, 0, 0, 0, 0, 0)))
+        else:
+            block = (chan_count, blk_count, 1) + array.shape[3:]
+            piece_specs.append(pl.BlockSpec(block, lambda channel, step: (0, 0, channel, 0, 0, 0)))
     results = pl.pallas_call(
-        functools.partial(visibility_kernel, len(arrays), len(carry)),
+        functools.partial(visibility_kernel, piece_units, len(carry)),
         grid=(len(channels), inputs // row_block),
         in_specs=piece_specs + [anywhere for _ in before] + [anywhere for _ in carry],
         out_specs=[out_spec, out_spec] + [anywhere for _ in carry],
@@ -359,47 +353,66 @@
     devices = chan_count * blk_count
     chan_local = NC // devices
     blocks = frames_dev // FRAME_BLOCK
-    half = blocks // 2
+    upper = blocks * 3 // 8
+    lower = blocks - upper
 
     def exchange(array):
         arrived = lax.all_to_all(array, ("chan", "blk"), split_axis=0, concat_axis=0, tiled=True)
         return arrived.reshape(chan_count, blk_count, *array.shape[1:])
 
-    if chan_local < 4 or chan_local % 2 or blocks % 2:
+    def frame_by_frame(step):
+        return (0, 0, 0, step, 0)
+
+    def unit_by_unit(first, step):
+        return (0, first + step, 0, 0, 0)
+
+    if chan_local < 4 or chan_local % 2 or upper == 0:
         tail = voltages[:, (frames_dev - HISTORY) * FFT :].astype(jnp.bfloat16)
         halo = shifted(tail, "blk", 1)
         outputs = ()
-        arrays = [([channel], 1, frames_dev, 0, None) for channel in range(chan_local)]
+        arrays = [([channel], 1, frames_dev, frame_by_frame, None) for channel in range(chan_local)]
         for channel, array in enumerate(spectra(voltages, [halo], 0, blocks, arrays, devices, chan_local)):
-            outputs, _ = visibilities([(exchange(array), 0)], [channel], outputs, [], chan_local)
+            outputs, _ = visibilities([(exchange(array), None)], [channel], outputs, [], chan_local)
         return outputs
 
     first, second, last = 0, 2, 1
     rest = list(range(3, chan_local))
-    early, tail = direct_spectra(voltages, first, half, devices, chan_local)
+    early, tail = direct_spectra(voltages, first, lower, devices, chan_local)
     halo = shifted(tail, "blk", 1)
-    half_frames = half * FRAME_BLOCK
+    units = 2 * lower + upper
+    above = functools.partial(unit_by_unit, 2 * lower)
+    below = functools.partial(unit_by_unit, 0)
     (pair,) = spectra(
-        voltages, [voltages] * HISTORY, half, half, [([second], 3, half_frames, 2, None)], devices, chan_local
+        voltages,
+        [voltages] * HISTORY,
+        lower,
+        upper,
+        [([second], units, FRAME_BLOCK, above, None)],
+        devices,
+        chan_local,
     )
-    (pair,) = spectra(voltages, [halo], 0, half, [([first, second], 3, half_frames, 0, pair)], devices, chan_local)
+    (pair,) = spectra(
+        voltages, [halo], 0, lower, [([first, second], units, FRAME_BLOCK, below, pair)], devices, chan_local
+    )
     many, final = spectra(
         voltages,
         [halo],
         0,
         blocks,
-        [(rest, len(rest), frames_dev, 0, None), ([last], 1, frames_dev, 0, None)],
+        [(rest, len(rest), frames_dev, frame_by_frame, None), ([last], 1, frames_dev, frame_by_frame, None)],
         devices,
         chan_local,
     )
     early = exchange(early)
     pair = exchange(pair)
     many = exchange(many)
-    outputs, _ = visibilities([(early, 0), (pair, 0)], [first], (), [], chan_local)
-    outputs, (final,) = visibilities([(pair, 1), (pair, 2)], [second], outputs, [final], chan_local)
+    first_units = list(range(0, 2 * lower, 2))
+    second_units = list(range(1, 2 * lower, 2)) + list(range(2 * lower, units))
+    outputs, _ = visibilities([(early, [0]), (pair, first_units)], [first], (), [], chan_local)
+    outputs, (final,) = visibilities([(pair, second_units)], [second], outputs, [final], chan_local)
     final = exchange(final)
-    outputs, _ = visibilities([(many, 0)], rest, outputs, [], chan_local)
-    outputs, _ = visibilities([(final, 0)], [last], outputs, [], chan_local, in_vmem=True)
+    outputs, _ = visibilities([(many, None)], rest, outputs, [], chan_local)
+    outputs, _ = visibilities([(final, None)], [last], outputs, [], chan_local, in_vmem=True)
     return outputs
 
 

time: 426 us -> 430 us (level)
  waiting for transfers between devices: 253 us -> 261 us
    all_to_all x4, waiting for transfers between devices: 253 us -> 261 us  [exchange(): lax.all_to_all(array, ('chan', 'blk'), split_axis=0, concat_axis=0, tiled...]
where the time goes in v4:
time: 430 us; the launch traced here: 429 us
  waiting for transfers between devices  261 us (61%)
  Pallas kernels  139 us (32%)
  starting transfers between devices  22.3 us (5%)
  local copies, waits for them, and re-layouts  5.71 us (1%)
    all_to_all x4, waiting for transfers between devices, exchange(): lax.all_to_all(array, ('chan', 'blk'), split_axis=0, concat_axis=0, tiled...  261 us
    pallas_call x3, Pallas kernels, spectra(): pl.pallas_call(functools.partial(spectra_kernel, groups, folds, places, l...  74 us
    pallas_call x4, Pallas kernels, visibilities(): pl.pallas_call(functools.partial(visibility_kernel, piece_units, len(carr...  55.7 us
    all_to_all x4, starting transfers between devices, exchange(): lax.all_to_all(array, ('chan', 'blk'), split_axis=0, concat_axis=0, tiled...  20.1 us
    pallas_call x1, Pallas kernels, direct_spectra(): pl.pallas_call(functools.partial(direct_kernel, len(history)), grid=(fram...  9.15 us
  transfers between devices with their start and end apart: 5, of which 3 were waited for; matrix products, arithmetic and copies ran while one was open for 0% of the time, Pallas kernels for 29%

profile of v4, /device:TPU:0, one launch (start us, length us, event | category | flops | bytes accessed | tf_op | source)
XLA Modules:
  0.0 428.8 jit_solution(13003286594652284734)
XLA Ops:
  0.6 9.1 %direct_spectra.1 = (bf16[32,1,2,48,128]{4,3,2,1,0:T(8,128)(2,1)}, bf16[128,1536]{1,0:T(8,128)(2,1)}) custom-call(s32[128,65536]{1,0:T(8,128)} %voltages.7, s32[128,65536]{1,0:T(8,128)} %voltages.7, s32[128,65536]{1,0:T(8,128)} %voltages.7, s32[128,65536]{1,0:T(8,128)} %voltages.7, bf16[512,512]{1,0:T(8,128)(2,1)} %constant.12.clone.refs_3_), custom_call_target="tpu_custom_call" | custom-call | flops 3221225472 | bytes 13369344 | tf_op jit(solution)/shard_map/direct_spectra/pallas_call | solution.py:116
  9.8 7.3 %all-to-all-start.1 = ((bf16[32,1,2,48,128]{4,3,2,1,0:T(8,128)(2,1)}), bf16[32,1,2,48,128]{4,3,2,1,0:T(8,128)(2,1)S(1)}, u32[]{:S(2)}, u32[]{:S(2)}) async-start(bf16[32,1,2,48,128]{4,3,2,1,0:T(8,128)(2,1)} %get-tuple-element.14), calls=%async_computation.1 | async-start | bytes 1572864 | tf_op jit(solution)/shard_map/all_to_all | solution.py:360
  17.1 2.2 collective-permute-start
  19.3 11.7 %spectra.3.refs_3_ = bf16[32,13,2,16,128]{4,3,2,1,0:T(8,128)(2,1)} custom-call(s32[128,65536]{1,0:T(8,128)} %voltages.7, s32[128,65536]{1,0:T(8,128)} %voltages.7, s32[128,65536]{1,0:T(8,128)} %voltages.7, s32[128,65536]{1,0:T(8,128)} %voltages.7, f32[4,512]{1,0:T(4,128)} %constant.14.clone.refs_3_.refs_1_, bf16[64,768]{1,0:T(8,128)(2,1)} %constant.13.clone.refs_4_), custom_call_target="tpu_custom_call" | custom-call | flops 603979776 | bytes 13369344 | tf_op jit(solution)/shard_map/spectra/pallas_call | solution.py:233
  30.9 0.0 collective-permute-done.refs_0_
  30.9 0.0 copy-start.4
  31.0 0.7 copy-done.4
  31.7 18.4 %spectra.4 = bf16[32,13,2,16,128]{4,3,2,1,0:T(8,128)(2,1)} custom-call(s32[128,65536]{1,0:T(8,128)} %voltages.7, bf16[128,1536]{1,0:T(8,128)(2,1)} %copy-done.4, f32[4,512]{1,0:T(4,128)} %constant.14.clone.refs_3_.refs_1_, bf16[128,768]{1,0:T(8,128)(2,1)} %constant.15.clone.refs_2_, ...), custom_call_target="tpu_custom_call", output_to_operand_aliasing={{}: (4, {})} | custom-call | flops 2013265920 | bytes 23592960 | tf_op jit(solution)/shard_map/spectra/pallas_call | solution.py:233
  50.1 0.0 all-to-all-done.1
  50.1 0.0 copy-start.2
  50.1 0.9 copy-done.2
  51.0 5.8 %all-to-all-start = ((bf16[32,13,2,16,128]{4,3,2,1,0:T(8,128)(2,1)}), bf16[32,13,2,16,128]{4,3,2,1,0:T(8,128)(2,1)S(1)}, u32[]{:S(2)}, u32[]{:S(2)}) async-start(bf16[32,13,2,16,128]{4,3,2,1,0:T(8,128)(2,1)} %spectra.4), calls=%async_computation | async-start | bytes 6815744 | tf_op jit(solution)/shard_map/all_to_all | solution.py:360
  56.8 43.9 %spectra.5 = (bf16[32,5,2,128,128]{4,3,2,1,0:T(8,128)(2,1)}, bf16[32,1,2,128,128]{4,3,2,1,0:T(8,128)(2,1)}) custom-call(s32[128,65536]{1,0:T(8,128)} %voltages.7, bf16[128,1536]{1,0:T(8,128)(2,1)} %copy-done.4, f32[4,512]{1,0:T(4,128)} %constant.14.clone.refs_3_.refs_1_, bf16[128,768]{1,0:T(8,128)(2,1)} %constant.16.clone.refs_2_, ...), custom_call_target="tpu_custom_call" | custom-call | flops 9663676416 | bytes 46137344 | tf_op jit(solution)/shard_map/spectra/pallas_call | solution.py:233
  100.7 33.1 %all-to-all-done = bf16[32,13,2,16,128]{4,3,2,1,0:T(8,128)(2,1)S(1)} async-done(((bf16[32,13,2,16,128]{4,3,2,1,0:T(8,128)(2,1)}), bf16[32,13,2,16,128]{4,3,2,1,0:T(8,128)(2,1)S(1)}, u32[]{:S(2)}, u32[]{:S(2)}) %all-to-all-start) | async-done | bytes 3407904 | tf_op jit(solution)/shard_map/all_to_all | solution.py:360
  133.9 4.1 all-to-all-start.3
  138.0 0.0 copy-start.3
  138.0 1.1 copy-done.3
  139.1 6.6 %visibilities.4 = (f32[8,1024,1024]{2,1,0:T(8,128)}, f32[8,1024,1024]{2,1,0:T(8,128)}) custom-call(bf16[8,4,1,2,48,128]{5,4,3,2,1,0:T(8,128)(2,1)S(1)} %bitcast.7, bf16[8,4,13,2,16,128]{5,4,3,2,1,0:T(8,128)(2,1)S(1)} %bitcast.4), custom_call_target="tpu_custom_call" | custom-call | flops 4294967296 | bytes 10485760 | tf_op jit(solution)/shard_map/visibilities/pallas_call | solution.py:325
  145.7 0.0 copy-start
  145.7 1.6 copy-done
  147.3 6.6 %visibilities.5 = (f32[8,1024,1024]{2,1,0:T(8,128)}, f32[8,1024,1024]{2,1,0:T(8,128)}, bf16[32,1,2,128,128]{4,3,2,1,0:T(8,128)(2,1)S(1)}) custom-call(bf16[8,4,13,2,16,128]{5,4,3,2,1,0:T(8,128)(2,1)S(1)} %bitcast.5, f32[8,1024,1024]{2,1,0:T(8,128)} %get-tuple-element.15.refs_1_, ...), custom_call_target="tpu_custom_call", output_to_operand_aliasing={{0}: (1, {}), {1}: (2, {}), {2}: (3, {})} | custom-call | flops 4294967296 | bytes 10485760 | tf_op jit(solution)/shard_map/visibilities/pallas_call | solution.py:325
  153.8 0.0 copy-start.1
  153.8 1.4 copy-done.1
  155.2 215.0 %all-to-all-done.3 = bf16[32,5,2,128,128]{4,3,2,1,0:T(8,128)(2,1)} async-done(((bf16[32,5,2,128,128]{4,3,2,1,0:T(8,128)(2,1)}), bf16[32,5,2,128,128]{4,3,2,1,0:T(8,128)(2,1)}, u32[]{:S(2)}, u32[]{:S(2)}) %all-to-all-start.3) | async-done | bytes 10485792 | tf_op jit(solution)/shard_map/all_to_all | solution.py:360
  370.2 2.9 all-to-all-start.2
  373.2 35.8 %visibilities.6 = (f32[8,1024,1024]{2,1,0:T(8,128)}, f32[8,1024,1024]{2,1,0:T(8,128)}) custom-call(bf16[8,4,5,2,128,128]{5,4,3,2,1,0:T(8,128)(2,1)} %bitcast.3.refs_0_, f32[8,1024,1024]{2,1,0:T(8,128)} %get-tuple-element.20.refs_1_, f32[8,1024,1024]{2,1,0:T(8,128)} %get-tuple-element.21.refs_2_), custom_call_target="tpu_custom_call", output_to_operand_aliasing={{0}: (1, {}), {1}: (2, {})} | custom-call | flops 21474836480 | bytes 52428800 | tf_op jit(solution)/shard_map/visibilities/pallas_call | solution.py:325
  409.0 13.1 %all-to-all-done.2 = bf16[32,1,2,128,128]{4,3,2,1,0:T(8,128)(2,1)S(1)} async-done(((bf16[32,1,2,128,128]{4,3,2,1,0:T(8,128)(2,1)}), bf16[32,1,2,128,128]{4,3,2,1,0:T(8,128)(2,1)S(1)}, u32[]{:S(2)}, u32[]{:S(2)}) %all-to-all-start.2) | async-done | bytes 2097184 | tf_op jit(solution)/shard_map/all_to_all | solution.py:360
  422.1 6.7 %visibilities.7 = (f32[8,1024,1024]{2,1,0:T(8,128)}, f32[8,1024,1024]{2,1,0:T(8,128)}) custom-call(bf16[8,4,1,2,128,128]{5,4,3,2,1,0:T(8,128)(2,1)S(1)} %bitcast.6, f32[8,1024,1024]{2,1,0:T(8,128)} %get-tuple-element.22.refs_1_, f32[8,1024,1024]{2,1,0:T(8,128)} %get-tuple-element.23.refs_2_), custom_call_target="tpu_custom_call", output_to_operand_aliasing={{0}: (1, {}), {1}: (2, {})} | custom-call | flops 4294967296 | bytes 10485760 | tf_op jit(solution)/shard_map/visibilities/pallas_call | solution.py:325
Async XLA Ops:
  9.8 40.3 %all-to-all-start.1 = ((bf16[32,1,2,48,128]{4,3,2,1,0:T(8,128)(2,1)}), bf16[32,1,2,48,128]{4,3,2,1,0:T(8,128)(2,1)S(1)}, u32[]{:S(2)}, u32[]{:S(2)}) async-start(bf16[32,1,2,48,128]{4,3,2,1,0:T(8,128)(2,1)} %get-tuple-element.14), calls=%async_computation.1 | async-start | bytes 1572864 | tf_op jit(solution)/shard_map/all_to_all | solution.py:360
  17.1 13.9 %collective-permute-start = (bf16[128,1536]{1,0:T(8,128)(2,1)}, bf16[128,1536]{1,0:T(8,128)(2,1)S(1)}, u32[]{:S(2)}, u32[]{:S(2)}) collective-permute-start(bf16[128,1536]{1,0:T(8,128)(2,1)} %get-tuple-element.13), channel_id=1, source_target_pairs={{0,1},{1,2},{2,3},{4,5},{5,6},{6,7},{8,9},{9,10},{10,11},{12,13},{... | collective-permute-start | bytes 1179656 | tf_op jit(solution)/shard_map/ppermute | solution.py:24
  30.9 0.7 copy-start.4
  50.1 0.9 copy-start.2
  51.0 82.9 %all-to-all-start = ((bf16[32,13,2,16,128]{4,3,2,1,0:T(8,128)(2,1)}), bf16[32,13,2,16,128]{4,3,2,1,0:T(8,128)(2,1)S(1)}, u32[]{:S(2)}, u32[]{:S(2)}) async-start(bf16[32,13,2,16,128]{4,3,2,1,0:T(8,128)(2,1)} %spectra.4), calls=%async_computation | async-start | bytes 6815744 | tf_op jit(solution)/shard_map/all_to_all | solution.py:360
  133.9 236.4 %all-to-all-start.3 = ((bf16[32,5,2,128,128]{4,3,2,1,0:T(8,128)(2,1)}), bf16[32,5,2,128,128]{4,3,2,1,0:T(8,128)(2,1)}, u32[]{:S(2)}, u32[]{:S(2)}) async-start(bf16[32,5,2,128,128]{4,3,2,1,0:T(8,128)(2,1)} %get-tuple-element.19), calls=%async_computation.3 | async-start | bytes 20971520 | tf_op jit(solution)/shard_map/all_to_all | solution.py:360
  138.0 1.1 copy-start.3
  145.7 1.6 copy-start
  153.8 1.4 copy-start.1
  370.2 51.8 %all-to-all-start.2 = ((bf16[32,1,2,128,128]{4,3,2,1,0:T(8,128)(2,1)}), bf16[32,1,2,128,128]{4,3,2,1,0:T(8,128)(2,1)S(1)}, u32[]{:S(2)}, u32[]{:S(2)}) async-start(bf16[32,1,2,128,128]{4,3,2,1,0:T(8,128)(2,1)} %copy-done.1), calls=%async_computation.2 | async-start | bytes 4194304 | tf_op jit(solution)/shard_map/all_to_all | solution.py:360

commit v5 on v4

--- a/solution.py
+++ b/solution.py
@@ -108,7 +108,7 @@
         tail[...] = voltages[:, (FRAME_BLOCK - HISTORY) * FFT :].astype(jnp.float32).astype(jnp.bfloat16)
 
 
-def direct_spectra(voltages, channel, first_block, devices, chan_local):
+def direct_spectra(voltages, channel, first_block, units, unit_frames, place, devices, chan_local):
     inputs_here = voltages.shape[0]
     frames = voltages.shape[1] // FFT - first_block * FRAME_BLOCK
     transform = jnp.asarray(build_direct(channel, devices, chan_local))
@@ -120,11 +120,11 @@
         + history_specs(history, inputs_here, first_block)
         + [pl.BlockSpec(transform.shape, lambda step: (0, 0))],
         out_specs=[
-            pl.BlockSpec((devices, 1, 2, FRAME_BLOCK, inputs_here), lambda step: (0, 0, 0, step, 0)),
+            pl.BlockSpec((devices, 1, 2, FRAME_BLOCK, inputs_here), place),
             pl.BlockSpec((inputs_here, HISTORY * FFT), lambda step: (0, 0)),
         ],
         out_shape=[
-            jax.ShapeDtypeStruct((devices, 1, 2, frames, inputs_here), jnp.bfloat16),
+            jax.ShapeDtypeStruct((devices, units, 2, unit_frames, inputs_here), jnp.bfloat16),
             jax.ShapeDtypeStruct((inputs_here, HISTORY * FFT), jnp.bfloat16),
         ],
         scratch_shapes=[
@@ -273,10 +273,10 @@
 
 def visibility_kernel(piece_units, carried, *refs):
     pieces = refs[: len(piece_units)]
-    across, turned, swapped = refs[-3:]
-    real_out, imag_out = refs[-5 - carried : -3 - carried][:2]
+    across, turned, swapped, above = refs[-4:]
+    real_out, imag_out = refs[-6 - carried : -4 - carried][:2]
     total_frames = across.shape[0] // 2
-    row_block = real_out.shape[1]
+    row_block, inputs = real_out.shape[1:]
 
     @pl.when(pl.program_id(1) == 0)
     def _():
@@ -292,13 +292,23 @@
                             across[rows, columns] = piece[chan, blk, unit, part]
                     top += frames
 
-    start = pl.multiple_of(pl.program_id(1) * row_block, row_block)
-    turned[...] = across[:, pl.ds(start, row_block)].T
-    swapped[:, :total_frames] = turned[:, total_frames:]
-    swapped[:, total_frames:] = -turned[:, :total_frames]
-    everything = across[...]
-    real_out[0] = jnp.dot(turned[...], everything, preferred_element_type=jnp.float32) / total_frames
-    imag_out[0] = jnp.dot(swapped[...], everything, preferred_element_type=jnp.float32) / total_frames
+    def one_block(step):
+        start = step * row_block
+        turned[...] = across[:, start : start + row_block].T
+        swapped[:, :total_frames] = turned[:, total_frames:]
+        swapped[:, total_frames:] = -turned[:, :total_frames]
+        columns = across[:, start:]
+        for index, (rows, output) in enumerate(((turned, real_out), (swapped, imag_out))):
+            result = jnp.dot(rows[...], columns, preferred_element_type=jnp.float32) / total_frames
+            output[0, :, start:] = result
+            if start + row_block < inputs:
+                above[index, start : start + row_block, start + row_block :] = result[:, row_block:]
+            for left in range(0, start, row_block):
+                mirrored = above[index, left : left + row_block, start : start + row_block].T
+                output[0, :, left : left + row_block] = mirrored if index == 0 else -mirrored
+
+    for step in range(inputs // row_block):
+        pl.when(pl.program_id(1) == step)(functools.partial(one_block, step))
 
 
 def visibilities(pieces, channels, before, carry, chan_local, in_vmem=False):
@@ -333,6 +343,7 @@
             pltpu.VMEM((depth, inputs), jnp.bfloat16),
             pltpu.VMEM((row_block, depth), jnp.bfloat16),
             pltpu.VMEM((row_block, depth), jnp.bfloat16),
+            pltpu.VMEM((2, inputs, inputs), jnp.float32),
         ],
         compiler_params=pltpu.CompilerParams(vmem_limit_bytes=VISIBILITY_LIMIT),
         cost_estimate=pl.CostEstimate(
@@ -353,7 +364,7 @@
     devices = chan_count * blk_count
     chan_local = NC // devices
     blocks = frames_dev // FRAME_BLOCK
-    upper = blocks * 3 // 8
+    upper = blocks * 5 // 8
     lower = blocks - upper
 
     def exchange(array):
@@ -377,20 +388,14 @@
 
     first, second, last = 0, 2, 1
     rest = list(range(3, chan_local))
-    early, tail = direct_spectra(voltages, first, lower, devices, chan_local)
+    early, tail = direct_spectra(
+        voltages, first, lower, 1, upper * FRAME_BLOCK, frame_by_frame, devices, chan_local
+    )
     halo = shifted(tail, "blk", 1)
     units = 2 * lower + upper
     above = functools.partial(unit_by_unit, 2 * lower)
     below = functools.partial(unit_by_unit, 0)
-    (pair,) = spectra(
-        voltages,
-        [voltages] * HISTORY,
-        lower,
-        upper,
-        [([second], units, FRAME_BLOCK, above, None)],
-        devices,
-        chan_local,
-    )
+    pair, _ = direct_spectra(voltages, second, lower, units, FRAME_BLOCK, above, devices, chan_local)
     (pair,) = spectra(
         voltages, [halo], 0, lower, [([first, second], units, FRAME_BLOCK, below, pair)], devices, chan_local
     )

time: 430 us -> 418 us (0.972)
  Pallas kernels: 139 us -> 133 us
    pallas_call x3 -> x2, Pallas kernels: 74 us -> 56.2 us  [spectra(): pl.pallas_call(functools.partial(spectra_kernel, groups, folds, places, l...]
    pallas_call x1 -> x2, Pallas kernels: 9.15 us -> 25.9 us  [direct_spectra(): pl.pallas_call(functools.partial(direct_kernel, len(history)), grid=(fram...]
    pallas_call x4, Pallas kernels: 55.7 us -> 50.8 us  [visibilities(): pl.pallas_call(functools.partial(visibility_kernel, piece_units, len(carr...]
  transfers between devices with their start and end apart: 5 -> 5, of which waited for: 3 -> 4; matrix products, arithmetic and copies ran while one was open for 0% -> 0% of each run, Pallas kernels for 29% -> 27%
where the time goes in v5:
time: 418 us
  waiting for transfers between devices  259 us (62%)
  Pallas kernels  133 us (32%)
  starting transfers between devices  20.2 us (5%)
  local copies, waits for them, and re-layouts  4.62 us (1%)
    all_to_all x4, waiting for transfers between devices, exchange(): lax.all_to_all(array, ('chan', 'blk'), split_axis=0, concat_axis=0, tiled...  259 us
    pallas_call x2, Pallas kernels, spectra(): pl.pallas_call(functools.partial(spectra_kernel, groups, folds, places, l...  56.2 us
    pallas_call x4, Pallas kernels, visibilities(): pl.pallas_call(functools.partial(visibility_kernel, piece_units, len(carr...  50.8 us
    pallas_call x2, Pallas kernels, direct_spectra(): pl.pallas_call(functools.partial(direct_kernel, len(history)), grid=(fram...  25.9 us
    all_to_all x4, starting transfers between devices, exchange(): lax.all_to_all(array, ('chan', 'blk'), split_axis=0, concat_axis=0, tiled...  18.1 us
  transfers between devices with their start and end apart: 5, of which 4 were waited for; matrix products, arithmetic and copies ran while one was open for 0% of the time, Pallas kernels for 27%

profile of v5, /device:TPU:0, one launch (start us, length us, event | category | flops | bytes accessed | tf_op | source)
XLA Modules:
  0.0 417.5 jit_solution(18064256272995411052)
XLA Ops:
  0.6 13.0 %direct_spectra.2 = (bf16[32,1,2,80,128]{4,3,2,1,0:T(8,128)(2,1)}, bf16[128,1536]{1,0:T(8,128)(2,1)}) custom-call(s32[128,65536]{1,0:T(8,128)} %voltages.7, s32[128,65536]{1,0:T(8,128)} %voltages.7, s32[128,65536]{1,0:T(8,128)} %voltages.7, s32[128,65536]{1,0:T(8,128)} %voltages.7, bf16[512,512]{1,0:T(8,128)(2,1)} %constant.12.clone.refs_3_), custom_call_target="tpu_custom_call" | custom-call | flops 5368709120 | bytes 22282240 | tf_op jit(solution)/shard_map/direct_spectra/pallas_call | solution.py:116
  13.6 7.3 %all-to-all-start.1 = ((bf16[32,1,2,80,128]{4,3,2,1,0:T(8,128)(2,1)}), bf16[32,1,2,80,128]{4,3,2,1,0:T(8,128)(2,1)S(1)}, u32[]{:S(2)}, u32[]{:S(2)}) async-start(bf16[32,1,2,80,128]{4,3,2,1,0:T(8,128)(2,1)} %get-tuple-element.16), calls=%async_computation.1 | async-start | bytes 2621440 | tf_op jit(solution)/shard_map/all_to_all | solution.py:371
  20.9 2.2 collective-permute-start
  23.1 12.9 %direct_spectra.3 = (bf16[32,11,2,16,128]{4,3,2,1,0:T(8,128)(2,1)}, bf16[128,1536]{1,0:T(8,128)(2,1)}) custom-call(s32[128,65536]{1,0:T(8,128)} %voltages.7, s32[128,65536]{1,0:T(8,128)} %voltages.7, s32[128,65536]{1,0:T(8,128)} %voltages.7, s32[128,65536]{1,0:T(8,128)} %voltages.7, bf16[512,512]{1,0:T(8,128)(2,1)} %constant.13.clone.refs_3_), custom_call_target="tpu_custom_call" | custom-call | flops 5368709120 | bytes 22282240 | tf_op jit(solution)/shard_map/direct_spectra/pallas_call | solution.py:116
  36.0 0.0 collective-permute-done.refs_0_
  36.0 0.0 copy-start.4
  36.0 0.7 copy-done.4
  36.8 12.3 %spectra.2 = bf16[32,11,2,16,128]{4,3,2,1,0:T(8,128)(2,1)} custom-call(s32[128,65536]{1,0:T(8,128)} %voltages.7, bf16[128,1536]{1,0:T(8,128)(2,1)} %copy-done.4, f32[4,512]{1,0:T(4,128)} %constant.15.clone.refs_1_, bf16[128,768]{1,0:T(8,128)(2,1)} %constant.14.clone.refs_2_, ...), custom_call_target="tpu_custom_call", output_to_operand_aliasing={{}: (4, {})} | custom-call | flops 1207959552 | bytes 14155776 | tf_op jit(solution)/shard_map/spectra/pallas_call | solution.py:233
  49.1 3.9 all-to-all-done.1
  53.0 0.0 copy-start.2
  53.0 1.1 copy-done.2
  54.1 3.6 all-to-all-start
  57.7 43.9 %spectra.3 = (bf16[32,5,2,128,128]{4,3,2,1,0:T(8,128)(2,1)}, bf16[32,1,2,128,128]{4,3,2,1,0:T(8,128)(2,1)}) custom-call(s32[128,65536]{1,0:T(8,128)} %voltages.7, bf16[128,1536]{1,0:T(8,128)(2,1)} %copy-done.4, f32[4,512]{1,0:T(4,128)} %constant.15.clone.refs_1_, bf16[128,768]{1,0:T(8,128)(2,1)} %constant.16.clone.refs_2_, ...), custom_call_target="tpu_custom_call" | custom-call | flops 9663676416 | bytes 46137344 | tf_op jit(solution)/shard_map/spectra/pallas_call | solution.py:233
  101.6 21.9 %all-to-all-done = bf16[32,11,2,16,128]{4,3,2,1,0:T(8,128)(2,1)S(1)} async-done(((bf16[32,11,2,16,128]{4,3,2,1,0:T(8,128)(2,1)}), bf16[32,11,2,16,128]{4,3,2,1,0:T(8,128)(2,1)S(1)}, u32[]{:S(2)}, u32[]{:S(2)}) %all-to-all-start) | async-done | bytes 2883616 | tf_op jit(solution)/shard_map/all_to_all | solution.py:371
  123.5 4.2 %all-to-all-start.3 = ((bf16[32,5,2,128,128]{4,3,2,1,0:T(8,128)(2,1)}), bf16[32,5,2,128,128]{4,3,2,1,0:T(8,128)(2,1)}, u32[]{:S(2)}, u32[]{:S(2)}) async-start(bf16[32,5,2,128,128]{4,3,2,1,0:T(8,128)(2,1)} %get-tuple-element.21), calls=%async_computation.3 | async-start | bytes 20971520 | tf_op jit(solution)/shard_map/all_to_all | solution.py:371
  127.7 0.0 copy-start
  127.7 0.0 copy-start.3
  127.8 1.5 copy-done.3
  129.2 5.7 %visibilities.4 = (f32[8,1024,1024]{2,1,0:T(8,128)}, f32[8,1024,1024]{2,1,0:T(8,128)}) custom-call(bf16[8,4,1,2,80,128]{5,4,3,2,1,0:T(8,128)(2,1)S(1)} %bitcast.7, bf16[8,4,11,2,16,128]{5,4,3,2,1,0:T(8,128)(2,1)S(1)} %bitcast.4), custom_call_target="tpu_custom_call" | custom-call | flops 4294967296 | bytes 10485760 | tf_op jit(solution)/shard_map/visibilities/pallas_call | solution.py:335
  135.0 0.0 copy-done
  135.0 5.8 %visibilities.5 = (f32[8,1024,1024]{2,1,0:T(8,128)}, f32[8,1024,1024]{2,1,0:T(8,128)}, bf16[32,1,2,128,128]{4,3,2,1,0:T(8,128)(2,1)S(1)}) custom-call(bf16[8,4,11,2,16,128]{5,4,3,2,1,0:T(8,128)(2,1)S(1)} %bitcast.5, f32[8,1024,1024]{2,1,0:T(8,128)} %get-tuple-element.17.refs_1_, ...), custom_call_target="tpu_custom_call", output_to_operand_aliasing={{0}: (1, {}), {1}: (2, {}), {2}: (3, {})} | custom-call | flops 4294967296 | bytes 10485760 | tf_op jit(solution)/shard_map/visibilities/pallas_call | solution.py:335
  140.7 0.0 copy-start.1
  140.7 1.4 copy-done.1
  142.1 217.8 %all-to-all-done.3 = bf16[32,5,2,128,128]{4,3,2,1,0:T(8,128)(2,1)} async-done(((bf16[32,5,2,128,128]{4,3,2,1,0:T(8,128)(2,1)}), bf16[32,5,2,128,128]{4,3,2,1,0:T(8,128)(2,1)}, u32[]{:S(2)}, u32[]{:S(2)}) %all-to-all-start.3) | async-done | bytes 10485792 | tf_op jit(solution)/shard_map/all_to_all | solution.py:371
  359.9 2.9 all-to-all-start.2
  362.9 33.5 %visibilities.6 = (f32[8,1024,1024]{2,1,0:T(8,128)}, f32[8,1024,1024]{2,1,0:T(8,128)}) custom-call(bf16[8,4,5,2,128,128]{5,4,3,2,1,0:T(8,128)(2,1)} %bitcast.3.refs_0_, f32[8,1024,1024]{2,1,0:T(8,128)} %get-tuple-element.22.refs_1_, f32[8,1024,1024]{2,1,0:T(8,128)} %get-tuple-element.23.refs_2_), custom_call_target="tpu_custom_call", output_to_operand_aliasing={{0}: (1, {}), {1}: (2, {})} | custom-call | flops 21474836480 | bytes 52428800 | tf_op jit(solution)/shard_map/visibilities/pallas_call | solution.py:335
  396.4 15.4 %all-to-all-done.2 = bf16[32,1,2,128,128]{4,3,2,1,0:T(8,128)(2,1)S(1)} async-done(((bf16[32,1,2,128,128]{4,3,2,1,0:T(8,128)(2,1)}), bf16[32,1,2,128,128]{4,3,2,1,0:T(8,128)(2,1)S(1)}, u32[]{:S(2)}, u32[]{:S(2)}) %all-to-all-start.2) | async-done | bytes 2097184 | tf_op jit(solution)/shard_map/all_to_all | solution.py:371
  411.8 5.8 %visibilities.7 = (f32[8,1024,1024]{2,1,0:T(8,128)}, f32[8,1024,1024]{2,1,0:T(8,128)}) custom-call(bf16[8,4,1,2,128,128]{5,4,3,2,1,0:T(8,128)(2,1)S(1)} %bitcast.6, f32[8,1024,1024]{2,1,0:T(8,128)} %get-tuple-element.24.refs_1_, f32[8,1024,1024]{2,1,0:T(8,128)} %get-tuple-element.25.refs_2_), custom_call_target="tpu_custom_call", output_to_operand_aliasing={{0}: (1, {}), {1}: (2, {})} | custom-call | flops 4294967296 | bytes 10485760 | tf_op jit(solution)/shard_map/visibilities/pallas_call | solution.py:335
Async XLA Ops:
  13.6 39.4 %all-to-all-start.1 = ((bf16[32,1,2,80,128]{4,3,2,1,0:T(8,128)(2,1)}), bf16[32,1,2,80,128]{4,3,2,1,0:T(8,128)(2,1)S(1)}, u32[]{:S(2)}, u32[]{:S(2)}) async-start(bf16[32,1,2,80,128]{4,3,2,1,0:T(8,128)(2,1)} %get-tuple-element.16), calls=%async_computation.1 | async-start | bytes 2621440 | tf_op jit(solution)/shard_map/all_to_all | solution.py:371
  20.9 15.1 %collective-permute-start = (bf16[128,1536]{1,0:T(8,128)(2,1)}, bf16[128,1536]{1,0:T(8,128)(2,1)S(1)}, u32[]{:S(2)}, u32[]{:S(2)}) collective-permute-start(bf16[128,1536]{1,0:T(8,128)(2,1)} %get-tuple-element.14), channel_id=1, source_target_pairs={{0,1},{1,2},{2,3},{4,5},{5,6},{6,7},{8,9},{9,10},{10,11},{12,13},{... | collective-permute-start | bytes 1179656 | tf_op jit(solution)/shard_map/ppermute | solution.py:24
  36.0 0.8 copy-start.4
  53.0 1.1 copy-start.2
  54.1 69.4 %all-to-all-start = ((bf16[32,11,2,16,128]{4,3,2,1,0:T(8,128)(2,1)}), bf16[32,11,2,16,128]{4,3,2,1,0:T(8,128)(2,1)S(1)}, u32[]{:S(2)}, u32[]{:S(2)}) async-start(bf16[32,11,2,16,128]{4,3,2,1,0:T(8,128)(2,1)} %spectra.2), calls=%async_computation | async-start | bytes 5767168 | tf_op jit(solution)/shard_map/all_to_all | solution.py:371
  123.5 236.4 %all-to-all-start.3 = ((bf16[32,5,2,128,128]{4,3,2,1,0:T(8,128)(2,1)}), bf16[32,5,2,128,128]{4,3,2,1,0:T(8,128)(2,1)}, u32[]{:S(2)}, u32[]{:S(2)}) async-start(bf16[32,5,2,128,128]{4,3,2,1,0:T(8,128)(2,1)} %get-tuple-element.21), calls=%async_computation.3 | async-start | bytes 20971520 | tf_op jit(solution)/shard_map/all_to_all | solution.py:371
  127.7 7.2 %copy-start = (bf16[32,1,2,128,128]{4,3,2,1,0:T(8,128)(2,1)S(1)}, bf16[32,1,2,128,128]{4,3,2,1,0:T(8,128)(2,1)}, u32[]{:S(2)}) copy-start(bf16[32,1,2,128,128]{4,3,2,1,0:T(8,128)(2,1)} %get-tuple-element.19.refs_3_) | copy-start | bytes 6291460
  127.7 1.5 copy-start.3
  140.7 1.4 copy-start.1
  359.9 51.9 %all-to-all-start.2 = ((bf16[32,1,2,128,128]{4,3,2,1,0:T(8,128)(2,1)}), bf16[32,1,2,128,128]{4,3,2,1,0:T(8,128)(2,1)S(1)}, u32[]{:S(2)}, u32[]{:S(2)}) async-start(bf16[32,1,2,128,128]{4,3,2,1,0:T(8,128)(2,1)} %copy-done.1), calls=%async_computation.2 | async-start | bytes 4194304 | tf_op jit(solution)/shard_map/all_to_all | solution.py:371

commit v6 on v5

--- a/solution.py
+++ b/solution.py
@@ -14,7 +14,7 @@
 HISTORY = TAPS - 1
 FRAME_BLOCK = 16
 ROWS = 16
-VMEM_LIMIT = 56 * 1024 * 1024
+VMEM_LIMIT = 40 * 1024 * 1024
 VISIBILITY_LIMIT = 40 * 1024 * 1024
 
 
@@ -76,29 +76,42 @@
     rows = turned.shape[0] // FRAME_BLOCK
     batch = 2 if inputs_here == 128 else 1
 
-    def multiply(target, frames):
-        for first in range(0, len(frames), batch):
-            group = [source[:, at : at + FFT] for source, at in frames[first : first + batch]]
-            samples = jnp.concatenate(group, axis=0).astype(jnp.float32).astype(jnp.bfloat16)
-            result = lax.dot_general(
-                transform[...], samples, (((1,), (1,)), ((), ())), preferred_element_type=jnp.float32
-            )
-            for frame in range(len(group)):
-                products[target + first + frame] = result[:, frame * inputs_here : (frame + 1) * inputs_here]
+    newest = TAPS - 1
+
+    def multiply(frames):
+        samples = jnp.concatenate([source[:, at : at + FFT] for source, at in frames], axis=0)
+        result = lax.dot_general(
+            transform[...],
+            samples.astype(jnp.float32).astype(jnp.bfloat16),
+            (((1,), (1,)), ((), ())),
+            preferred_element_type=jnp.float32,
+        )
+        return [result[:, k * inputs_here : (k + 1) * inputs_here] for k in range(len(frames))]
+
+    def keep(place, product):
+        for part in range(2):
+            start = part * TAPS * rows
+            kept = slice(part * newest * rows, (part + 1) * newest * rows)
+            products[place, kept, :] = product[start : start + newest * rows]
 
     @pl.when(pl.program_id(0) == 0)
     def _():
-        multiply(0, [(source, 0) for source in history])
-
-    multiply(HISTORY, [(voltages, frame * FFT) for frame in range(FRAME_BLOCK)])
-    for frame in range(FRAME_BLOCK):
-        total = None
-        for part in (1, 0):
-            for offset in range(TAPS):
-                start = (part * TAPS + offset) * rows
-                term = products[frame + offset, start : start + rows, :]
+        for k, source in enumerate(history):
+            keep(k, multiply([(source, 0)])[0])
+
+    for first in range(0, FRAME_BLOCK, batch):
+        frames = range(first, first + batch)
+        for frame, product in zip(frames, multiply([(voltages, frame * FFT) for frame in frames])):
+            keep(HISTORY + frame, product)
+            total = None
+            for part in (1, 0):
+                start = (part * TAPS + newest) * rows
+                term = product[start : start + rows]
                 total = term if total is None else total + term
-        turned[pl.ds(frame, rows, stride=FRAME_BLOCK), :] = total
+                for offset in range(newest):
+                    start = (part * newest + offset) * rows
+                    total = total + products[frame + offset, start : start + rows, :]
+            turned[pl.ds(frame, rows, stride=FRAME_BLOCK), :] = total
     for frame in range(HISTORY):
         products[frame] = products[FRAME_BLOCK + frame]
     output[...] = turned[...].reshape(output.shape).astype(jnp.bfloat16)
@@ -128,7 +141,7 @@
             jax.ShapeDtypeStruct((inputs_here, HISTORY * FFT), jnp.bfloat16),
         ],
         scratch_shapes=[
-            pltpu.VMEM((HISTORY + FRAME_BLOCK, transform.shape[0], inputs_here), jnp.float32),
+            pltpu.VMEM((HISTORY + FRAME_BLOCK, transform.shape[0] // TAPS * (TAPS - 1), inputs_here), jnp.float32),
             pltpu.VMEM((devices * 2 * FRAME_BLOCK, inputs_here), jnp.float32),
         ],
         compiler_params=pltpu.CompilerParams(vmem_limit_bytes=VMEM_LIMIT),

time: 418 us -> 419 us (level)
  waiting for transfers between devices: 259 us -> 251 us
  local copies, waits for them, and re-layouts: 4.62 us -> 12.1 us
    all_to_all x4, waiting for transfers between devices: 259 us -> 251 us  [exchange(): lax.all_to_all(array, ('chan', 'blk'), split_axis=0, concat_axis=0, tiled...]
    unnamed x10 -> x26, local copies, waits for them, and re-layouts: 4.62 us -> 12.1 us
  transfers between devices with their start and end apart: 5 -> 5, of which waited for: 4 -> 4; matrix products, arithmetic and copies ran while one was open for 0% -> 0% of each run, Pallas kernels for 27% -> 28%
where the time goes in v6:
time: 419 us; the launch traced here: 418 us
  waiting for transfers between devices  251 us (60%)
  Pallas kernels  134 us (32%)
  starting transfers between devices  21 us (5%)
  local copies, waits for them, and re-layouts  12.1 us (3%)
    all_to_all x4, waiting for transfers between devices, exchange(): lax.all_to_all(array, ('chan', 'blk'), split_axis=0, concat_axis=0, tiled...  251 us
    pallas_call x2, Pallas kernels, spectra(): pl.pallas_call(functools.partial(spectra_kernel, groups, folds, places, l...  55.9 us
    pallas_call x4, Pallas kernels, visibilities(): pl.pallas_call(functools.partial(visibility_kernel, piece_units, len(carr...  52.3 us
    pallas_call x2, Pallas kernels, direct_spectra(): pl.pallas_call(functools.partial(direct_kernel, len(history)), grid=(fram...  25.7 us
    all_to_all x4, starting transfers between devices, exchange(): lax.all_to_all(array, ('chan', 'blk'), split_axis=0, concat_axis=0, tiled...  18.7 us
    unnamed x26, local copies, waits for them, and re-layouts  12.1 us
  transfers between devices with their start and end apart: 5, of which 4 were waited for; matrix products, arithmetic and copies ran while one was open for 0% of the time, Pallas kernels for 28%

profile of v6, /device:TPU:0, one launch (start us, length us, event | category | flops | bytes accessed | tf_op | source)
XLA Modules:
  0.0 418.3 jit_solution(4849922006531535564)
XLA Ops:
  0.6 0.0 copy-start.5
  0.6 0.0 copy-start.6
  0.7 1.1 copy-done.6
  1.7 12.9 %direct_spectra.2 = (bf16[32,1,2,80,128]{4,3,2,1,0:T(8,128)(2,1)}, bf16[128,1536]{1,0:T(8,128)(2,1)}) custom-call(s32[128,65536]{1,0:T(8,128)} %voltages.7, s32[128,65536]{1,0:T(8,128)} %voltages.7, s32[128,65536]{1,0:T(8,128)} %voltages.7, s32[128,65536]{1,0:T(8,128)} %voltages.7, bf16[512,512]{1,0:T(8,128)(2,1)S(1)} %copy-done.6), custom_call_target="tpu_custom_call" | custom-call | flops 5368709120 | bytes 22282240 | tf_op jit(solution)/shard_map/direct_spectra/pallas_call | solution.py:129
  14.7 7.4 %all-to-all-start.1 = ((bf16[32,1,2,80,128]{4,3,2,1,0:T(8,128)(2,1)}), bf16[32,1,2,80,128]{4,3,2,1,0:T(8,128)(2,1)}, u32[]{:S(2)}, u32[]{:S(2)}) async-start(bf16[32,1,2,80,128]{4,3,2,1,0:T(8,128)(2,1)} %get-tuple-element.16), calls=%async_computation.1 | async-start | bytes 2621440 | tf_op jit(solution)/shard_map/all_to_all | solution.py:384
  22.1 0.0 copy-start.9
  22.1 0.0 copy-start.10
  22.1 2.2 collective-permute-start
  24.4 0.0 copy-done.5
  24.4 12.8 %direct_spectra.3 = (bf16[32,11,2,16,128]{4,3,2,1,0:T(8,128)(2,1)S(1)}, bf16[128,1536]{1,0:T(8,128)(2,1)}) custom-call(s32[128,65536]{1,0:T(8,128)} %voltages.7, s32[128,65536]{1,0:T(8,128)} %voltages.7, s32[128,65536]{1,0:T(8,128)} %voltages.7, s32[128,65536]{1,0:T(8,128)} %voltages.7, bf16[512,512]{1,0:T(8,128)(2,1)S(1)} %copy-done.5), custom_call_target="tpu_custom_call" | custom-call | flops 5368709120 | bytes 22282240 | tf_op jit(solution)/shard_map/direct_spectra/pallas_call | solution.py:129
  37.2 0.0 collective-permute-done.refs_0_
  37.2 0.0 copy-done.9
  37.2 0.0 copy-done.10
  37.2 0.0 copy-start.11
  37.2 11.7 %spectra.2 = bf16[32,11,2,16,128]{4,3,2,1,0:T(8,128)(2,1)S(1)} custom-call(s32[128,65536]{1,0:T(8,128)} %voltages.7, bf16[128,1536]{1,0:T(8,128)(2,1)S(1)} %collective-permute-done.refs_0_, f32[4,512]{1,0:T(4,128)S(1)} %copy-done.10, bf16[128,768]{1,0:T(8,128)(2,1)S(1)} %copy-done.9, ...), custom_call_target="tpu_custom_call", output_to_operand_aliasing={{}: (4, {})} | custom-call | flops 1207959552 | bytes 14155776 | tf_op jit(solution)/shard_map/spectra/pallas_call | solution.py:246
  48.9 0.0 copy-start
  48.9 1.6 copy-done
  50.5 0.0 copy-start.7
  50.5 0.7 copy-done.7
  51.3 3.0 all-to-all-done.1
  54.2 4.2 all-to-all-start
  58.4 0.0 copy-done.11
  58.4 0.0 copy-start.8
  58.4 1.0 copy-done.8
  59.4 0.0 copy-start.12
  59.4 0.9 copy-done.12
  60.3 44.1 %spectra.3 = (bf16[32,5,2,128,128]{4,3,2,1,0:T(8,128)(2,1)S(1)}, bf16[32,1,2,128,128]{4,3,2,1,0:T(8,128)(2,1)S(1)}) custom-call(s32[128,65536]{1,0:T(8,128)} %voltages.7, bf16[128,1536]{1,0:T(8,128)(2,1)S(1)} %copy-done.8, f32[4,512]{1,0:T(4,128)S(1)} %copy-done.10, bf16[128,768]{1,0:T(8,128)(2,1)S(1)} %copy-done.12, bf16[256,768]{1,0:T(8,128)(2,1)S(1)} %copy-done.11), custom_call_target="tpu_custom_call" | custom-call | flops 9663676416 | bytes 46137344 | tf_op jit(solution)/shard_map/spectra/pallas_call | solution.py:246
  104.5 0.0 copy-start.1
  104.5 4.0 copy-done.1
  108.5 0.0 copy-start.2
  108.5 1.4 copy-done.2
  109.8 14.4 %all-to-all-done = bf16[32,11,2,16,128]{4,3,2,1,0:T(8,128)(2,1)S(1)} async-done(((bf16[32,11,2,16,128]{4,3,2,1,0:T(8,128)(2,1)}), bf16[32,11,2,16,128]{4,3,2,1,0:T(8,128)(2,1)S(1)}, u32[]{:S(2)}, u32[]{:S(2)}) %all-to-all-start) | async-done | bytes 2883616 | tf_op jit(solution)/shard_map/all_to_all | solution.py:384
  124.2 4.2 %all-to-all-start.3 = ((bf16[32,5,2,128,128]{4,3,2,1,0:T(8,128)(2,1)}), bf16[32,5,2,128,128]{4,3,2,1,0:T(8,128)(2,1)}, u32[]{:S(2)}, u32[]{:S(2)}) async-start(bf16[32,5,2,128,128]{4,3,2,1,0:T(8,128)(2,1)} %copy-done.1), calls=%async_computation.3 | async-start | bytes 20971520 | tf_op jit(solution)/shard_map/all_to_all | solution.py:384
  128.5 0.0 copy-start.3
  128.5 7.3 %visibilities.4 = (f32[8,1024,1024]{2,1,0:T(8,128)}, f32[8,1024,1024]{2,1,0:T(8,128)}) custom-call(bf16[8,4,1,2,80,128]{5,4,3,2,1,0:T(8,128)(2,1)} %bitcast.1.refs_0_, bf16[8,4,11,2,16,128]{5,4,3,2,1,0:T(8,128)(2,1)S(1)} %bitcast.4), custom_call_target="tpu_custom_call" | custom-call | flops 4294967296 | bytes 10485760 | tf_op jit(solution)/shard_map/visibilities/pallas_call | solution.py:348
  135.7 0.0 copy-done.3
  135.7 5.8 %visibilities.5 = (f32[8,1024,1024]{2,1,0:T(8,128)}, f32[8,1024,1024]{2,1,0:T(8,128)}, bf16[32,1,2,128,128]{4,3,2,1,0:T(8,128)(2,1)S(1)}) custom-call(bf16[8,4,11,2,16,128]{5,4,3,2,1,0:T(8,128)(2,1)S(1)} %bitcast.5, f32[8,1024,1024]{2,1,0:T(8,128)} %get-tuple-element.17.refs_1_, ...), custom_call_target="tpu_custom_call", output_to_operand_aliasing={{0}: (1, {}), {1}: (2, {}), {2}: (3, {})} | custom-call | flops 4294967296 | bytes 10485760 | tf_op jit(solution)/shard_map/visibilities/pallas_call | solution.py:348
  141.5 0.0 copy-start.4
  141.5 1.4 copy-done.4
  142.9 217.8 %all-to-all-done.3 = bf16[32,5,2,128,128]{4,3,2,1,0:T(8,128)(2,1)} async-done(((bf16[32,5,2,128,128]{4,3,2,1,0:T(8,128)(2,1)}), bf16[32,5,2,128,128]{4,3,2,1,0:T(8,128)(2,1)}, u32[]{:S(2)}, u32[]{:S(2)}) %all-to-all-start.3) | async-done | bytes 10485792 | tf_op jit(solution)/shard_map/all_to_all | solution.py:384
  360.7 2.9 all-to-all-start.2
  363.6 33.5 %visibilities.6 = (f32[8,1024,1024]{2,1,0:T(8,128)}, f32[8,1024,1024]{2,1,0:T(8,128)}) custom-call(bf16[8,4,5,2,128,128]{5,4,3,2,1,0:T(8,128)(2,1)} %bitcast.3.refs_0_, f32[8,1024,1024]{2,1,0:T(8,128)} %get-tuple-element.22.refs_1_, f32[8,1024,1024]{2,1,0:T(8,128)} %get-tuple-element.23.refs_2_), custom_call_target="tpu_custom_call", output_to_operand_aliasing={{0}: (1, {}), {1}: (2, {})} | custom-call | flops 21474836480 | bytes 52428800 | tf_op jit(solution)/shard_map/visibilities/pallas_call | solution.py:348
  397.1 15.4 %all-to-all-done.2 = bf16[32,1,2,128,128]{4,3,2,1,0:T(8,128)(2,1)S(1)} async-done(((bf16[32,1,2,128,128]{4,3,2,1,0:T(8,128)(2,1)}), bf16[32,1,2,128,128]{4,3,2,1,0:T(8,128)(2,1)S(1)}, u32[]{:S(2)}, u32[]{:S(2)}) %all-to-all-start.2) | async-done | bytes 2097184 | tf_op jit(solution)/shard_map/all_to_all | solution.py:384
  412.5 5.7 %visibilities.7 = (f32[8,1024,1024]{2,1,0:T(8,128)}, f32[8,1024,1024]{2,1,0:T(8,128)}) custom-call(bf16[8,4,1,2,128,128]{5,4,3,2,1,0:T(8,128)(2,1)S(1)} %bitcast.6, f32[8,1024,1024]{2,1,0:T(8,128)} %get-tuple-element.24.refs_1_, f32[8,1024,1024]{2,1,0:T(8,128)} %get-tuple-element.25.refs_2_), custom_call_target="tpu_custom_call", output_to_operand_aliasing={{0}: (1, {}), {1}: (2, {})} | custom-call | flops 4294967296 | bytes 10485760 | tf_op jit(solution)/shard_map/visibilities/pallas_call | solution.py:348
Async XLA Ops:
  0.6 23.8 %copy-start.5 = (bf16[512,512]{1,0:T(8,128)(2,1)S(1)}, bf16[512,512]{1,0:T(8,128)(2,1)}, u32[]{:S(2)}) copy-start(bf16[512,512]{1,0:T(8,128)(2,1)} %constant.13.clone.refs_3_) | copy-start | bytes 1572868
  0.6 1.1 copy-start.6
  14.7 39.5 %all-to-all-start.1 = ((bf16[32,1,2,80,128]{4,3,2,1,0:T(8,128)(2,1)}), bf16[32,1,2,80,128]{4,3,2,1,0:T(8,128)(2,1)}, u32[]{:S(2)}, u32[]{:S(2)}) async-start(bf16[32,1,2,80,128]{4,3,2,1,0:T(8,128)(2,1)} %get-tuple-element.16), calls=%async_computation.1 | async-start | bytes 2621440 | tf_op jit(solution)/shard_map/all_to_all | solution.py:384
  22.1 15.0 %copy-start.9 = (bf16[128,768]{1,0:T(8,128)(2,1)S(1)}, bf16[128,768]{1,0:T(8,128)(2,1)}, u32[]{:S(2)}) copy-start(bf16[128,768]{1,0:T(8,128)(2,1)} %constant.14.clone.refs_2_) | copy-start | bytes 589828
  22.1 15.0 %copy-start.10 = (f32[4,512]{1,0:T(4,128)S(1)}, f32[4,512]{1,0:T(4,128)}, u32[]{:S(2)}) copy-start(f32[4,512]{1,0:T(4,128)} %constant.15.clone.refs_1_) | copy-start | bytes 24580
  22.1 15.0 %collective-permute-start = (bf16[128,1536]{1,0:T(8,128)(2,1)}, bf16[128,1536]{1,0:T(8,128)(2,1)S(1)}, u32[]{:S(2)}, u32[]{:S(2)}) collective-permute-start(bf16[128,1536]{1,0:T(8,128)(2,1)} %get-tuple-element.14), channel_id=1, source_target_pairs={{0,1},{1,2},{2,3},{4,5},{5,6},{6,7},{8,9},{9,10},{10,11},{12,13},{... | collective-permute-start | bytes 1179656 | tf_op jit(solution)/shard_map/ppermute | solution.py:24
  37.2 21.2 %copy-start.11 = (bf16[256,768]{1,0:T(8,128)(2,1)S(1)}, bf16[256,768]{1,0:T(8,128)(2,1)}, u32[]{:S(2)}) copy-start(bf16[256,768]{1,0:T(8,128)(2,1)} %constant.17.clone.refs_3_) | copy-start | bytes 1179652
  48.9 1.6 copy-start
  50.5 0.7 copy-start.7
  54.2 70.0 %all-to-all-start = ((bf16[32,11,2,16,128]{4,3,2,1,0:T(8,128)(2,1)}), bf16[32,11,2,16,128]{4,3,2,1,0:T(8,128)(2,1)S(1)}, u32[]{:S(2)}, u32[]{:S(2)}) async-start(bf16[32,11,2,16,128]{4,3,2,1,0:T(8,128)(2,1)} %copy-done), calls=%async_computation | async-start | bytes 5767168 | tf_op jit(solution)/shard_map/all_to_all | solution.py:384
  58.4 1.0 copy-start.8
  59.4 0.9 copy-start.12
  104.5 4.0 copy-start.1
  108.5 1.4 copy-start.2
  124.2 236.4 %all-to-all-start.3 = ((bf16[32,5,2,128,128]{4,3,2,1,0:T(8,128)(2,1)}), bf16[32,5,2,128,128]{4,3,2,1,0:T(8,128)(2,1)}, u32[]{:S(2)}, u32[]{:S(2)}) async-start(bf16[32,5,2,128,128]{4,3,2,1,0:T(8,128)(2,1)} %copy-done.1), calls=%async_computation.3 | async-start | bytes 20971520 | tf_op jit(solution)/shard_map/all_to_all | solution.py:384
  128.5 7.3 %copy-start.3 = (bf16[32,1,2,128,128]{4,3,2,1,0:T(8,128)(2,1)S(1)}, bf16[32,1,2,128,128]{4,3,2,1,0:T(8,128)(2,1)}, u32[]{:S(2)}) copy-start(bf16[32,1,2,128,128]{4,3,2,1,0:T(8,128)(2,1)} %copy-done.2) | copy-start | bytes 6291460
  141.5 1.4 copy-start.4
  360.7 51.9 %all-to-all-start.2 = ((bf16[32,1,2,128,128]{4,3,2,1,0:T(8,128)(2,1)}), bf16[32,1,2,128,128]{4,3,2,1,0:T(8,128)(2,1)S(1)}, u32[]{:S(2)}, u32[]{:S(2)}) async-start(bf16[32,1,2,128,128]{4,3,2,1,0:T(8,128)(2,1)} %copy-done.4), calls=%async_computation.2 | async-start | bytes 4194304 | tf_op jit(solution)/shard_map/all_to_all | solution.py:384

commit v7 on v6

--- a/solution.py
+++ b/solution.py
@@ -14,7 +14,7 @@
 HISTORY = TAPS - 1
 FRAME_BLOCK = 16
 ROWS = 16
-VMEM_LIMIT = 40 * 1024 * 1024
+VMEM_LIMIT = 56 * 1024 * 1024
 VISIBILITY_LIMIT = 40 * 1024 * 1024
 
 
@@ -62,6 +62,16 @@
     return np.concatenate([high, low], axis=0)
 
 
+def row_groups(inputs_here):
+    return 4 if inputs_here % (4 * ROWS) == 0 else 1
+
+
+def sample_specs(inputs_here, first_block):
+    count = row_groups(inputs_here)
+    block = (inputs_here // count, FRAME_BLOCK * FFT)
+    return [pl.BlockSpec(block, functools.partial(lambda at, step: (at, first_block + step), k)) for k in range(count)]
+
+
 def history_specs(history, inputs_here, first_block):
     if len(history) == 1:
         return [pl.BlockSpec((inputs_here, HISTORY * FFT), lambda step: (0, 0))]
@@ -69,17 +79,19 @@
     return [pl.BlockSpec((inputs_here, FFT), functools.partial(lambda at, step: (0, at), before + k)) for k in range(HISTORY)]
 
 
-def direct_kernel(history_count, voltages, *refs):
-    history = refs[:history_count]
-    transform, output, tail, products, turned = refs[history_count:]
-    inputs_here = voltages.shape[0]
+def direct_kernel(group_count, history_count, *refs):
+    voltages = refs[:group_count]
+    history = refs[group_count : group_count + history_count]
+    transform, output, tail, products, turned = refs[group_count + history_count :]
+    inputs_here = tail.shape[0]
     rows = turned.shape[0] // FRAME_BLOCK
     batch = 2 if inputs_here == 128 else 1
 
     newest = TAPS - 1
 
     def multiply(frames):
-        samples = jnp.concatenate([source[:, at : at + FFT] for source, at in frames], axis=0)
+        pieces = [source[:, at : at + FFT] for sources, at in frames for source in sources]
+        samples = jnp.concatenate(pieces, axis=0)
         result = lax.dot_general(
             transform[...],
             samples.astype(jnp.float32).astype(jnp.bfloat16),
@@ -97,7 +109,7 @@
     @pl.when(pl.program_id(0) == 0)
     def _():
         for k, source in enumerate(history):
-            keep(k, multiply([(source, 0)])[0])
+            keep(k, multiply([([source], 0)])[0])
 
     for first in range(0, FRAME_BLOCK, batch):
         frames = range(first, first + batch)
@@ -118,7 +130,9 @@
 
     @pl.when(pl.program_id(0) == pl.num_programs(0) - 1)
     def _():
-        tail[...] = voltages[:, (FRAME_BLOCK - HISTORY) * FFT :].astype(jnp.float32).astype(jnp.bfloat16)
+        for k, source in enumerate(voltages):
+            rows = slice(k * source.shape[0], (k + 1) * source.shape[0])
+            tail[rows] = source[:, (FRAME_BLOCK - HISTORY) * FFT :].astype(jnp.float32).astype(jnp.bfloat16)
 
 
 def direct_spectra(voltages, channel, first_block, units, unit_frames, place, devices, chan_local):
@@ -127,9 +141,9 @@
     transform = jnp.asarray(build_direct(channel, devices, chan_local))
     history = [voltages] * HISTORY
     return pl.pallas_call(
-        functools.partial(direct_kernel, len(history)),
+        functools.partial(direct_kernel, row_groups(inputs_here), len(history)),
         grid=(frames // FRAME_BLOCK,),
-        in_specs=[pl.BlockSpec((inputs_here, FRAME_BLOCK * FFT), lambda step: (0, first_block + step))]
+        in_specs=sample_specs(inputs_here, first_block)
         + history_specs(history, inputs_here, first_block)
         + [pl.BlockSpec(transform.shape, lambda step: (0, 0))],
         out_specs=[
@@ -151,17 +165,19 @@
             transcendentals=0,
         ),
         name="direct_spectra",
-    )(voltages, *history, transform)
-
-
-def spectra_kernel(groups, folds, places, history_count, array_count, voltages, *refs):
+    )(*[voltages] * row_groups(inputs_here), *history, transform)
+
+
+def spectra_kernel(groups, folds, places, group_count, history_count, array_count, *refs):
+    sources = refs[:group_count]
+    refs = refs[group_count:]
     before = refs[:history_count]
     taps = refs[history_count]
     transforms = refs[history_count + 1 : history_count + 1 + len(groups)]
     history, turned = refs[-2 - len(groups) : len(refs) - len(groups)]
     folded = refs[len(refs) - len(groups) :]
     outputs = refs[-2 - len(groups) - array_count : -2 - len(groups)]
-    inputs_here = voltages.shape[0]
+    inputs_here = history.shape[0]
     part = FFT // folds
     lanes = 128
 
@@ -172,8 +188,9 @@
             history[:, at : at + source.shape[1]] = source[...].astype(jnp.float32)
             at += source.shape[1]
 
-    def filter_rows(step, carry):
-        rows = pl.ds(pl.multiple_of(step * ROWS, ROWS), ROWS)
+    def filter_rows(voltages, top, step, carry):
+        here = pl.ds(pl.multiple_of(step * ROWS, ROWS), ROWS)
+        rows = pl.ds(pl.multiple_of(top + step * ROWS, ROWS), ROWS)
         for start in range(0, part, lanes):
             columns = [fold * part + start for fold in range(folds)]
             weights = [[taps[offset : offset + 1, at : at + lanes] for offset in range(TAPS)] for at in columns]
@@ -182,7 +199,7 @@
                 filtered = []
                 for fold, column in enumerate(columns):
                     at = frame * FFT + column
-                    past[fold].append(voltages[rows, at : at + lanes].astype(jnp.float32))
+                    past[fold].append(voltages[here, at : at + lanes].astype(jnp.float32))
                     value = weights[fold][0] * past[fold].pop(0)
                     for offset in range(1, TAPS):
                         value = value + weights[fold][offset] * past[fold][offset - 1]
@@ -193,7 +210,7 @@
                         value = value + filtered[1] if residue == 0 else value - filtered[1]
                     high = value.astype(jnp.bfloat16)
                     low = (value - high.astype(jnp.float32)).astype(jnp.bfloat16)
-                    at = pl.ds(pl.multiple_of(frame * inputs_here + step * ROWS, ROWS), ROWS)
+                    at = pl.ds(pl.multiple_of(frame * inputs_here + top + step * ROWS, ROWS), ROWS)
                     target[at, start : start + lanes] = high
                     target[at, part + start : part + start + lanes] = low
                     target[at, 2 * part + start : 2 * part + start + lanes] = high
@@ -202,7 +219,9 @@
                     history[rows, k * FFT + at : k * FFT + at + lanes] = past[fold][k]
         return carry
 
-    lax.fori_loop(0, inputs_here // ROWS, filter_rows, 0)
+    for index, source in enumerate(sources):
+        height = source.shape[0]
+        lax.fori_loop(0, height // ROWS, functools.partial(filter_rows, source, index * height), 0)
 
     for (_, channels), transform, source in zip(groups, transforms, folded):
         per_channel = transform.shape[0] // len(channels)
@@ -241,12 +260,14 @@
     depth = 3 * (FFT // folds)
     most = max(transform.shape[0] for transform in transforms)
     existing = [(index, array[4]) for index, array in enumerate(arrays) if array[4] is not None]
-    operand_count = 2 + len(history) + len(transforms)
+    operand_count = 1 + row_groups(inputs_here) + len(history) + len(transforms)
     frames = blocks * FRAME_BLOCK
     return pl.pallas_call(
-        functools.partial(spectra_kernel, groups, folds, places, len(history), len(arrays)),
+        functools.partial(
+            spectra_kernel, groups, folds, places, row_groups(inputs_here), len(history), len(arrays)
+        ),
         grid=(blocks,),
-        in_specs=[pl.BlockSpec((inputs_here, FRAME_BLOCK * FFT), lambda step: (0, first_block + step))]
+        in_specs=sample_specs(inputs_here, first_block)
         + history_specs(history, inputs_here, first_block)
         + [pl.BlockSpec((TAPS, FFT), lambda step: (0, 0))]
         + [pl.BlockSpec(transform.shape, lambda step: (0, 0)) for transform in transforms]
@@ -276,7 +297,7 @@
         ),
         name="spectra",
     )(
-        voltages,
+        *[voltages] * row_groups(inputs_here),
         *history,
         jnp.asarray(build_taps().astype(np.float32)),
         *transforms,

time: 419 us -> 419 us (level)
  local copies, waits for them, and re-layouts: 12.1 us -> 4.62 us
  waiting for transfers between devices: 251 us -> 258 us
    unnamed x26 -> x10, local copies, waits for them, and re-layouts: 12.1 us -> 4.62 us
    all_to_all x4, waiting for transfers between devices: 251 us -> 258 us  [exchange(): lax.all_to_all(array, ('chan', 'blk'), split_axis=0, concat_axis=0, tiled...]
where the time goes in v7:
time: 419 us; the launch traced here: 418 us
  waiting for transfers between devices  258 us (62%)
  Pallas kernels  134 us (32%)
  starting transfers between devices  20.2 us (5%)
  local copies, waits for them, and re-layouts  4.62 us (1%)
    all_to_all x4, waiting for transfers between devices, exchange(): lax.all_to_all(array, ('chan', 'blk'), split_axis=0, concat_axis=0, tiled...  258 us
    pallas_call x2, Pallas kernels, spectra(): pl.pallas_call(functools.partial(spectra_kernel, groups, folds, places, r...  56.9 us
    pallas_call x4, Pallas kernels, visibilities(): pl.pallas_call(functools.partial(visibility_kernel, piece_units, len(carr...  50.8 us
    pallas_call x2, Pallas kernels, direct_spectra(): pl.pallas_call(functools.partial(direct_kernel, row_groups(inputs_here),...  26.8 us
    all_to_all x4, starting transfers between devices, exchange(): lax.all_to_all(array, ('chan', 'blk'), split_axis=0, concat_axis=0, tiled...  18.1 us
  transfers between devices with their start and end apart: 5, of which 4 were waited for; matrix products, arithmetic and copies ran while one was open for 0% of the time, Pallas kernels for 28%

profile of v7, /device:TPU:0, one launch (start us, length us, event | category | flops | bytes accessed | tf_op | source)
XLA Modules:
  0.0 418.0 jit_solution(10266771512415455904)
XLA Ops:
  0.6 13.4 %direct_spectra.2 = (bf16[32,1,2,80,128]{4,3,2,1,0:T(8,128)(2,1)}, bf16[128,1536]{1,0:T(8,128)(2,1)}) custom-call(s32[128,65536]{1,0:T(8,128)} %refs_3_.7, s32[128,65536]{1,0:T(8,128)} %refs_3_.7, s32[128,65536]{1,0:T(8,128)} %refs_3_.7, s32[128,65536]{1,0:T(8,128)} %refs_3_.7, s32[128,65536]{1,0:T(8,128)} %refs_3_.7, s32[128,65536]{1,0:T(8,128)} %refs_3_.7, ...), custom_call_target="tpu_custom_call" | custom-call | flops 5368709120 | bytes 22282240 | tf_op jit(solution)/shard_map/direct_spectra/pallas_call | solution.py:143
  14.0 7.3 %all-to-all-start.1 = ((bf16[32,1,2,80,128]{4,3,2,1,0:T(8,128)(2,1)}), bf16[32,1,2,80,128]{4,3,2,1,0:T(8,128)(2,1)S(1)}, u32[]{:S(2)}, u32[]{:S(2)}) async-start(bf16[32,1,2,80,128]{4,3,2,1,0:T(8,128)(2,1)} %get-tuple-element.16), calls=%async_computation.1 | async-start | bytes 2621440 | tf_op jit(solution)/shard_map/all_to_all | solution.py:405
  21.3 2.2 collective-permute-start
  23.5 13.4 %direct_spectra.3 = (bf16[32,11,2,16,128]{4,3,2,1,0:T(8,128)(2,1)}, bf16[128,1536]{1,0:T(8,128)(2,1)}) custom-call(s32[128,65536]{1,0:T(8,128)} %refs_3_.7, s32[128,65536]{1,0:T(8,128)} %refs_3_.7, s32[128,65536]{1,0:T(8,128)} %refs_3_.7, s32[128,65536]{1,0:T(8,128)} %refs_3_.7, s32[128,65536]{1,0:T(8,128)} %refs_3_.7, s32[128,65536]{1,0:T(8,128)} %refs_3_.7, ...), custom_call_target="tpu_custom_call" | custom-call | flops 5368709120 | bytes 22282240 | tf_op jit(solution)/shard_map/direct_spectra/pallas_call | solution.py:143
  36.9 0.0 collective-permute-done.refs_4_
  36.9 0.0 copy-start.4
  36.9 0.7 copy-done.4
  37.6 12.6 %spectra.2 = bf16[32,11,2,16,128]{4,3,2,1,0:T(8,128)(2,1)} custom-call(s32[128,65536]{1,0:T(8,128)} %refs_3_.7, s32[128,65536]{1,0:T(8,128)} %refs_3_.7, s32[128,65536]{1,0:T(8,128)} %refs_3_.7, s32[128,65536]{1,0:T(8,128)} %refs_3_.7, bf16[128,1536]{1,0:T(8,128)(2,1)} %copy-done.4, ...), custom_call_target="tpu_custom_call", output_to_operand_aliasing={{}: (7, {})} | custom-call | flops 1207959552 | bytes 14155776 | tf_op jit(solution)/shard_map/spectra/pallas_call | solution.py:265
  50.2 3.2 all-to-all-done.1
  53.5 0.0 copy-start.2
  53.5 1.1 copy-done.2
  54.5 3.6 all-to-all-start
  58.1 44.3 %spectra.3 = (bf16[32,5,2,128,128]{4,3,2,1,0:T(8,128)(2,1)}, bf16[32,1,2,128,128]{4,3,2,1,0:T(8,128)(2,1)}) custom-call(s32[128,65536]{1,0:T(8,128)} %refs_3_.7, s32[128,65536]{1,0:T(8,128)} %refs_3_.7, s32[128,65536]{1,0:T(8,128)} %refs_3_.7, s32[128,65536]{1,0:T(8,128)} %refs_3_.7, bf16[128,1536]{1,0:T(8,128)(2,1)} %copy-done.4, ...), custom_call_target="tpu_custom_call" | custom-call | flops 9663676416 | bytes 46137344 | tf_op jit(solution)/shard_map/spectra/pallas_call | solution.py:265
  102.4 21.6 %all-to-all-done = bf16[32,11,2,16,128]{4,3,2,1,0:T(8,128)(2,1)S(1)} async-done(((bf16[32,11,2,16,128]{4,3,2,1,0:T(8,128)(2,1)}), bf16[32,11,2,16,128]{4,3,2,1,0:T(8,128)(2,1)S(1)}, u32[]{:S(2)}, u32[]{:S(2)}) %all-to-all-start) | async-done | bytes 2883616 | tf_op jit(solution)/shard_map/all_to_all | solution.py:405
  123.9 4.2 %all-to-all-start.3 = ((bf16[32,5,2,128,128]{4,3,2,1,0:T(8,128)(2,1)}), bf16[32,5,2,128,128]{4,3,2,1,0:T(8,128)(2,1)}, u32[]{:S(2)}, u32[]{:S(2)}) async-start(bf16[32,5,2,128,128]{4,3,2,1,0:T(8,128)(2,1)} %get-tuple-element.21), calls=%async_computation.3 | async-start | bytes 20971520 | tf_op jit(solution)/shard_map/all_to_all | solution.py:405
  128.2 0.0 copy-start
  128.2 0.0 copy-start.3
  128.2 1.5 copy-done.3
  129.6 5.8 %visibilities.4 = (f32[8,1024,1024]{2,1,0:T(8,128)}, f32[8,1024,1024]{2,1,0:T(8,128)}) custom-call(bf16[8,4,1,2,80,128]{5,4,3,2,1,0:T(8,128)(2,1)S(1)} %bitcast.7, bf16[8,4,11,2,16,128]{5,4,3,2,1,0:T(8,128)(2,1)S(1)} %bitcast.4), custom_call_target="tpu_custom_call" | custom-call | flops 4294967296 | bytes 10485760 | tf_op jit(solution)/shard_map/visibilities/pallas_call | solution.py:369
  135.4 0.0 copy-done
  135.4 5.8 %visibilities.5 = (f32[8,1024,1024]{2,1,0:T(8,128)}, f32[8,1024,1024]{2,1,0:T(8,128)}, bf16[32,1,2,128,128]{4,3,2,1,0:T(8,128)(2,1)S(1)}) custom-call(bf16[8,4,11,2,16,128]{5,4,3,2,1,0:T(8,128)(2,1)S(1)} %bitcast.5, f32[8,1024,1024]{2,1,0:T(8,128)} %get-tuple-element.17.refs_1_, ...), custom_call_target="tpu_custom_call", output_to_operand_aliasing={{0}: (1, {}), {1}: (2, {}), {2}: (3, {})} | custom-call | flops 4294967296 | bytes 10485760 | tf_op jit(solution)/shard_map/visibilities/pallas_call | solution.py:369
  141.2 0.0 copy-start.1
  141.2 1.4 copy-done.1
  142.5 217.8 %all-to-all-done.3 = bf16[32,5,2,128,128]{4,3,2,1,0:T(8,128)(2,1)} async-done(((bf16[32,5,2,128,128]{4,3,2,1,0:T(8,128)(2,1)}), bf16[32,5,2,128,128]{4,3,2,1,0:T(8,128)(2,1)}, u32[]{:S(2)}, u32[]{:S(2)}) %all-to-all-start.3) | async-done | bytes 10485792 | tf_op jit(solution)/shard_map/all_to_all | solution.py:405
  360.4 2.9 all-to-all-start.2
  363.3 33.5 %visibilities.6 = (f32[8,1024,1024]{2,1,0:T(8,128)}, f32[8,1024,1024]{2,1,0:T(8,128)}) custom-call(bf16[8,4,5,2,128,128]{5,4,3,2,1,0:T(8,128)(2,1)} %bitcast.3.refs_0_, f32[8,1024,1024]{2,1,0:T(8,128)} %get-tuple-element.22.refs_1_, f32[8,1024,1024]{2,1,0:T(8,128)} %get-tuple-element.23.refs_2_), custom_call_target="tpu_custom_call", output_to_operand_aliasing={{0}: (1, {}), {1}: (2, {})} | custom-call | flops 21474836480 | bytes 52428800 | tf_op jit(solution)/shard_map/visibilities/pallas_call | solution.py:369
  396.8 15.4 %all-to-all-done.2 = bf16[32,1,2,128,128]{4,3,2,1,0:T(8,128)(2,1)S(1)} async-done(((bf16[32,1,2,128,128]{4,3,2,1,0:T(8,128)(2,1)}), bf16[32,1,2,128,128]{4,3,2,1,0:T(8,128)(2,1)S(1)}, u32[]{:S(2)}, u32[]{:S(2)}) %all-to-all-start.2) | async-done | bytes 2097184 | tf_op jit(solution)/shard_map/all_to_all | solution.py:405
  412.2 5.7 %visibilities.7 = (f32[8,1024,1024]{2,1,0:T(8,128)}, f32[8,1024,1024]{2,1,0:T(8,128)}) custom-call(bf16[8,4,1,2,128,128]{5,4,3,2,1,0:T(8,128)(2,1)S(1)} %bitcast.6, f32[8,1024,1024]{2,1,0:T(8,128)} %get-tuple-element.24.refs_1_, f32[8,1024,1024]{2,1,0:T(8,128)} %get-tuple-element.25.refs_2_), custom_call_target="tpu_custom_call", output_to_operand_aliasing={{0}: (1, {}), {1}: (2, {})} | custom-call | flops 4294967296 | bytes 10485760 | tf_op jit(solution)/shard_map/visibilities/pallas_call | solution.py:369
Async XLA Ops:
  14.0 39.4 %all-to-all-start.1 = ((bf16[32,1,2,80,128]{4,3,2,1,0:T(8,128)(2,1)}), bf16[32,1,2,80,128]{4,3,2,1,0:T(8,128)(2,1)S(1)}, u32[]{:S(2)}, u32[]{:S(2)}) async-start(bf16[32,1,2,80,128]{4,3,2,1,0:T(8,128)(2,1)} %get-tuple-element.16), calls=%async_computation.1 | async-start | bytes 2621440 | tf_op jit(solution)/shard_map/all_to_all | solution.py:405
  21.3 15.6 %collective-permute-start = (bf16[128,1536]{1,0:T(8,128)(2,1)}, bf16[128,1536]{1,0:T(8,128)(2,1)S(1)}, u32[]{:S(2)}, u32[]{:S(2)}) collective-permute-start(bf16[128,1536]{1,0:T(8,128)(2,1)} %get-tuple-element.14), channel_id=1, source_target_pairs={{0,1},{1,2},{2,3},{4,5},{5,6},{6,7},{8,9},{9,10},{10,11},{12,13},{... | collective-permute-start | bytes 1179656 | tf_op jit(solution)/shard_map/ppermute | solution.py:24
  36.9 0.8 copy-start.4
  53.5 1.1 copy-start.2
  54.5 69.4 %all-to-all-start = ((bf16[32,11,2,16,128]{4,3,2,1,0:T(8,128)(2,1)}), bf16[32,11,2,16,128]{4,3,2,1,0:T(8,128)(2,1)S(1)}, u32[]{:S(2)}, u32[]{:S(2)}) async-start(bf16[32,11,2,16,128]{4,3,2,1,0:T(8,128)(2,1)} %spectra.2), calls=%async_computation | async-start | bytes 5767168 | tf_op jit(solution)/shard_map/all_to_all | solution.py:405
  123.9 236.4 %all-to-all-start.3 = ((bf16[32,5,2,128,128]{4,3,2,1,0:T(8,128)(2,1)}), bf16[32,5,2,128,128]{4,3,2,1,0:T(8,128)(2,1)}, u32[]{:S(2)}, u32[]{:S(2)}) async-start(bf16[32,5,2,128,128]{4,3,2,1,0:T(8,128)(2,1)} %get-tuple-element.21), calls=%async_computation.3 | async-start | bytes 20971520 | tf_op jit(solution)/shard_map/all_to_all | solution.py:405
  128.2 7.2 %copy-start = (bf16[32,1,2,128,128]{4,3,2,1,0:T(8,128)(2,1)S(1)}, bf16[32,1,2,128,128]{4,3,2,1,0:T(8,128)(2,1)}, u32[]{:S(2)}) copy-start(bf16[32,1,2,128,128]{4,3,2,1,0:T(8,128)(2,1)} %get-tuple-element.19.refs_3_) | copy-start | bytes 6291460
  128.2 1.5 copy-start.3
  141.2 1.4 copy-start.1
  360.4 51.9 %all-to-all-start.2 = ((bf16[32,1,2,128,128]{4,3,2,1,0:T(8,128)(2,1)}), bf16[32,1,2,128,128]{4,3,2,1,0:T(8,128)(2,1)S(1)}, u32[]{:S(2)}, u32[]{:S(2)}) async-start(bf16[32,1,2,128,128]{4,3,2,1,0:T(8,128)(2,1)} %copy-done.1), calls=%async_computation.2 | async-start | bytes 4194304 | tf_op jit(solution)/shard_map/all_to_all | solution.py:405

commit v8 on v6

--- a/solution.py
+++ b/solution.py
@@ -14,7 +14,7 @@
 HISTORY = TAPS - 1
 FRAME_BLOCK = 16
 ROWS = 16
-VMEM_LIMIT = 40 * 1024 * 1024
+VMEM_LIMIT = 56 * 1024 * 1024
 VISIBILITY_LIMIT = 40 * 1024 * 1024
 
 
@@ -58,8 +58,8 @@
 
 def build_direct(channel, devices, chan_local):
     matrix = build_dft([channel], devices, chan_local, FFT)
-    high, low = split_high_low(np.concatenate([matrix * taps[None, :] for taps in build_taps()]))
-    return np.concatenate([high, low], axis=0)
+    parts = [part for taps in build_taps() for part in split_high_low(matrix * taps[None, :])]
+    return np.ascontiguousarray(np.concatenate(parts, axis=0).T)
 
 
 def history_specs(history, inputs_here, first_block):
@@ -80,38 +80,24 @@
 
     def multiply(frames):
         samples = jnp.concatenate([source[:, at : at + FFT] for source, at in frames], axis=0)
-        result = lax.dot_general(
-            transform[...],
-            samples.astype(jnp.float32).astype(jnp.bfloat16),
-            (((1,), (1,)), ((), ())),
-            preferred_element_type=jnp.float32,
-        )
-        return [result[:, k * inputs_here : (k + 1) * inputs_here] for k in range(len(frames))]
-
-    def keep(place, product):
-        for part in range(2):
-            start = part * TAPS * rows
-            kept = slice(part * newest * rows, (part + 1) * newest * rows)
-            products[place, kept, :] = product[start : start + newest * rows]
+        samples = samples.astype(jnp.float32).astype(jnp.bfloat16)
+        result = jnp.dot(samples, transform[...], preferred_element_type=jnp.float32)
+        return [result[k * inputs_here : (k + 1) * inputs_here] for k in range(len(frames))]
 
     @pl.when(pl.program_id(0) == 0)
     def _():
         for k, source in enumerate(history):
-            keep(k, multiply([(source, 0)])[0])
+            products[k] = multiply([(source, 0)])[0][:, : 2 * newest * rows]
 
     for first in range(0, FRAME_BLOCK, batch):
         frames = range(first, first + batch)
         for frame, product in zip(frames, multiply([(voltages, frame * FFT) for frame in frames])):
-            keep(HISTORY + frame, product)
-            total = None
-            for part in (1, 0):
-                start = (part * TAPS + newest) * rows
-                term = product[start : start + rows]
-                total = term if total is None else total + term
-                for offset in range(newest):
-                    start = (part * newest + offset) * rows
-                    total = total + products[frame + offset, start : start + rows, :]
-            turned[pl.ds(frame, rows, stride=FRAME_BLOCK), :] = total
+            products[HISTORY + frame] = product[:, : 2 * newest * rows]
+            total = product[:, 2 * newest * rows :]
+            for offset in range(newest):
+                total = total + products[frame + offset, :, 2 * offset * rows : 2 * (offset + 1) * rows]
+            total = total.T
+            turned[pl.ds(frame, rows, stride=FRAME_BLOCK), :] = total[:rows] + total[rows:]
     for frame in range(HISTORY):
         products[frame] = products[FRAME_BLOCK + frame]
     output[...] = turned[...].reshape(output.shape).astype(jnp.bfloat16)
@@ -141,12 +127,12 @@
             jax.ShapeDtypeStruct((inputs_here, HISTORY * FFT), jnp.bfloat16),
         ],
         scratch_shapes=[
-            pltpu.VMEM((HISTORY + FRAME_BLOCK, transform.shape[0] // TAPS * (TAPS - 1), inputs_here), jnp.float32),
+            pltpu.VMEM((HISTORY + FRAME_BLOCK, inputs_here, transform.shape[1] // TAPS * (TAPS - 1)), jnp.float32),
             pltpu.VMEM((devices * 2 * FRAME_BLOCK, inputs_here), jnp.float32),
         ],
         compiler_params=pltpu.CompilerParams(vmem_limit_bytes=VMEM_LIMIT),
         cost_estimate=pl.CostEstimate(
-            flops=2 * frames * inputs_here * FFT * transform.shape[0],
+            flops=2 * frames * inputs_here * FFT * transform.shape[1],
             bytes_accessed=frames * inputs_here * (4 * FFT + 4 * devices),
             transcendentals=0,
         ),

time: 419 us -> 418 us (level)
  waiting for transfers between devices: 251 us -> 259 us
  local copies, waits for them, and re-layouts: 12.1 us -> 4.62 us
    all_to_all x4, waiting for transfers between devices: 251 us -> 259 us  [exchange(): lax.all_to_all(array, ('chan', 'blk'), split_axis=0, concat_axis=0, tiled...]
    unnamed x26 -> x10, local copies, waits for them, and re-layouts: 12.1 us -> 4.62 us
  transfers between devices with their start and end apart: 5 -> 5, of which waited for: 4 -> 4; matrix products, arithmetic and copies ran while one was open for 0% -> 0% of each run, Pallas kernels for 28% -> 27%
where the time goes in v8:
time: 418 us; the launch traced here: 417 us
  waiting for transfers between devices  259 us (62%)
  Pallas kernels  132 us (32%)
  starting transfers between devices  20.2 us (5%)
  local copies, waits for them, and re-layouts  4.62 us (1%)
    all_to_all x4, waiting for transfers between devices, exchange(): lax.all_to_all(array, ('chan', 'blk'), split_axis=0, concat_axis=0, tiled...  259 us
    pallas_call x2, Pallas kernels, spectra(): pl.pallas_call(functools.partial(spectra_kernel, groups, folds, places, l...  56.2 us
    pallas_call x4, Pallas kernels, visibilities(): pl.pallas_call(functools.partial(visibility_kernel, piece_units, len(carr...  50.8 us
    pallas_call x2, Pallas kernels, direct_spectra(): pl.pallas_call(functools.partial(direct_kernel, len(history)), grid=(fram...  25.3 us
    all_to_all x4, starting transfers between devices, exchange(): lax.all_to_all(array, ('chan', 'blk'), split_axis=0, concat_axis=0, tiled...  18.1 us
  transfers between devices with their start and end apart: 5, of which 4 were waited for; matrix products, arithmetic and copies ran while one was open for 0% of the time, Pallas kernels for 27%

profile of v8, /device:TPU:0, one launch (start us, length us, event | category | flops | bytes accessed | tf_op | source)
XLA Modules:
  0.0 417.3 jit_solution(2902880769484346282)
XLA Ops:
  0.6 12.7 %direct_spectra.2 = (bf16[32,1,2,80,128]{4,3,2,1,0:T(8,128)(2,1)}, bf16[128,1536]{1,0:T(8,128)(2,1)}) custom-call(s32[128,65536]{1,0:T(8,128)} %voltages.7, s32[128,65536]{1,0:T(8,128)} %voltages.7, s32[128,65536]{1,0:T(8,128)} %voltages.7, s32[128,65536]{1,0:T(8,128)} %voltages.7, bf16[512,512]{1,0:T(8,128)(2,1)} %constant.12.clone.refs_3_), custom_call_target="tpu_custom_call" | custom-call | flops 5368709120 | bytes 22282240 | tf_op jit(solution)/shard_map/direct_spectra/pallas_call | solution.py:115
  13.3 7.3 %all-to-all-start.1 = ((bf16[32,1,2,80,128]{4,3,2,1,0:T(8,128)(2,1)}), bf16[32,1,2,80,128]{4,3,2,1,0:T(8,128)(2,1)S(1)}, u32[]{:S(2)}, u32[]{:S(2)}) async-start(bf16[32,1,2,80,128]{4,3,2,1,0:T(8,128)(2,1)} %get-tuple-element.16), calls=%async_computation.1 | async-start | bytes 2621440 | tf_op jit(solution)/shard_map/all_to_all | solution.py:370
  20.6 2.2 collective-permute-start
  22.8 12.7 %direct_spectra.3 = (bf16[32,11,2,16,128]{4,3,2,1,0:T(8,128)(2,1)}, bf16[128,1536]{1,0:T(8,128)(2,1)}) custom-call(s32[128,65536]{1,0:T(8,128)} %voltages.7, s32[128,65536]{1,0:T(8,128)} %voltages.7, s32[128,65536]{1,0:T(8,128)} %voltages.7, s32[128,65536]{1,0:T(8,128)} %voltages.7, bf16[512,512]{1,0:T(8,128)(2,1)} %constant.13.clone.refs_3_), custom_call_target="tpu_custom_call" | custom-call | flops 5368709120 | bytes 22282240 | tf_op jit(solution)/shard_map/direct_spectra/pallas_call | solution.py:115
  35.4 0.0 collective-permute-done.refs_0_
  35.5 0.0 copy-start.4
  35.5 0.7 copy-done.4
  36.2 12.3 %spectra.2 = bf16[32,11,2,16,128]{4,3,2,1,0:T(8,128)(2,1)} custom-call(s32[128,65536]{1,0:T(8,128)} %voltages.7, bf16[128,1536]{1,0:T(8,128)(2,1)} %copy-done.4, f32[4,512]{1,0:T(4,128)} %constant.15.clone.refs_1_, bf16[128,768]{1,0:T(8,128)(2,1)} %constant.14.clone.refs_2_, ...), custom_call_target="tpu_custom_call", output_to_operand_aliasing={{}: (4, {})} | custom-call | flops 1207959552 | bytes 14155776 | tf_op jit(solution)/shard_map/spectra/pallas_call | solution.py:232
  48.5 4.2 %all-to-all-done.1 = bf16[32,1,2,80,128]{4,3,2,1,0:T(8,128)(2,1)S(1)} async-done(((bf16[32,1,2,80,128]{4,3,2,1,0:T(8,128)(2,1)}), bf16[32,1,2,80,128]{4,3,2,1,0:T(8,128)(2,1)S(1)}, u32[]{:S(2)}, u32[]{:S(2)}) %all-to-all-start.1) | async-done | bytes 1310752 | tf_op jit(solution)/shard_map/all_to_all | solution.py:370
  52.7 0.0 copy-start.2
  52.7 1.1 copy-done.2
  53.8 3.6 all-to-all-start
  57.4 43.9 %spectra.3 = (bf16[32,5,2,128,128]{4,3,2,1,0:T(8,128)(2,1)}, bf16[32,1,2,128,128]{4,3,2,1,0:T(8,128)(2,1)}) custom-call(s32[128,65536]{1,0:T(8,128)} %voltages.7, bf16[128,1536]{1,0:T(8,128)(2,1)} %copy-done.4, f32[4,512]{1,0:T(4,128)} %constant.15.clone.refs_1_, bf16[128,768]{1,0:T(8,128)(2,1)} %constant.16.clone.refs_2_, ...), custom_call_target="tpu_custom_call" | custom-call | flops 9663676416 | bytes 46137344 | tf_op jit(solution)/shard_map/spectra/pallas_call | solution.py:232
  101.3 21.9 %all-to-all-done = bf16[32,11,2,16,128]{4,3,2,1,0:T(8,128)(2,1)S(1)} async-done(((bf16[32,11,2,16,128]{4,3,2,1,0:T(8,128)(2,1)}), bf16[32,11,2,16,128]{4,3,2,1,0:T(8,128)(2,1)S(1)}, u32[]{:S(2)}, u32[]{:S(2)}) %all-to-all-start) | async-done | bytes 2883616 | tf_op jit(solution)/shard_map/all_to_all | solution.py:370
  123.2 4.2 %all-to-all-start.3 = ((bf16[32,5,2,128,128]{4,3,2,1,0:T(8,128)(2,1)}), bf16[32,5,2,128,128]{4,3,2,1,0:T(8,128)(2,1)}, u32[]{:S(2)}, u32[]{:S(2)}) async-start(bf16[32,5,2,128,128]{4,3,2,1,0:T(8,128)(2,1)} %get-tuple-element.21), calls=%async_computation.3 | async-start | bytes 20971520 | tf_op jit(solution)/shard_map/all_to_all | solution.py:370
  127.4 0.0 copy-start
  127.5 0.0 copy-start.3
  127.5 1.5 copy-done.3
  128.9 5.8 %visibilities.4 = (f32[8,1024,1024]{2,1,0:T(8,128)}, f32[8,1024,1024]{2,1,0:T(8,128)}) custom-call(bf16[8,4,1,2,80,128]{5,4,3,2,1,0:T(8,128)(2,1)S(1)} %bitcast.7, bf16[8,4,11,2,16,128]{5,4,3,2,1,0:T(8,128)(2,1)S(1)} %bitcast.4), custom_call_target="tpu_custom_call" | custom-call | flops 4294967296 | bytes 10485760 | tf_op jit(solution)/shard_map/visibilities/pallas_call | solution.py:334
  134.7 0.0 copy-done
  134.7 5.8 %visibilities.5 = (f32[8,1024,1024]{2,1,0:T(8,128)}, f32[8,1024,1024]{2,1,0:T(8,128)}, bf16[32,1,2,128,128]{4,3,2,1,0:T(8,128)(2,1)S(1)}) custom-call(bf16[8,4,11,2,16,128]{5,4,3,2,1,0:T(8,128)(2,1)S(1)} %bitcast.5, f32[8,1024,1024]{2,1,0:T(8,128)} %get-tuple-element.17.refs_1_, ...), custom_call_target="tpu_custom_call", output_to_operand_aliasing={{0}: (1, {}), {1}: (2, {}), {2}: (3, {})} | custom-call | flops 4294967296 | bytes 10485760 | tf_op jit(solution)/shard_map/visibilities/pallas_call | solution.py:334
  140.4 0.0 copy-start.1
  140.4 1.4 copy-done.1
  141.8 217.8 %all-to-all-done.3 = bf16[32,5,2,128,128]{4,3,2,1,0:T(8,128)(2,1)} async-done(((bf16[32,5,2,128,128]{4,3,2,1,0:T(8,128)(2,1)}), bf16[32,5,2,128,128]{4,3,2,1,0:T(8,128)(2,1)}, u32[]{:S(2)}, u32[]{:S(2)}) %all-to-all-start.3) | async-done | bytes 10485792 | tf_op jit(solution)/shard_map/all_to_all | solution.py:370
  359.6 2.9 all-to-all-start.2
  362.6 33.5 %visibilities.6 = (f32[8,1024,1024]{2,1,0:T(8,128)}, f32[8,1024,1024]{2,1,0:T(8,128)}) custom-call(bf16[8,4,5,2,128,128]{5,4,3,2,1,0:T(8,128)(2,1)} %bitcast.3.refs_0_, f32[8,1024,1024]{2,1,0:T(8,128)} %get-tuple-element.22.refs_1_, f32[8,1024,1024]{2,1,0:T(8,128)} %get-tuple-element.23.refs_2_), custom_call_target="tpu_custom_call", output_to_operand_aliasing={{0}: (1, {}), {1}: (2, {})} | custom-call | flops 21474836480 | bytes 52428800 | tf_op jit(solution)/shard_map/visibilities/pallas_call | solution.py:334
  396.1 15.4 %all-to-all-done.2 = bf16[32,1,2,128,128]{4,3,2,1,0:T(8,128)(2,1)S(1)} async-done(((bf16[32,1,2,128,128]{4,3,2,1,0:T(8,128)(2,1)}), bf16[32,1,2,128,128]{4,3,2,1,0:T(8,128)(2,1)S(1)}, u32[]{:S(2)}, u32[]{:S(2)}) %all-to-all-start.2) | async-done | bytes 2097184 | tf_op jit(solution)/shard_map/all_to_all | solution.py:370
  411.5 5.8 %visibilities.7 = (f32[8,1024,1024]{2,1,0:T(8,128)}, f32[8,1024,1024]{2,1,0:T(8,128)}) custom-call(bf16[8,4,1,2,128,128]{5,4,3,2,1,0:T(8,128)(2,1)S(1)} %bitcast.6, f32[8,1024,1024]{2,1,0:T(8,128)} %get-tuple-element.24.refs_1_, f32[8,1024,1024]{2,1,0:T(8,128)} %get-tuple-element.25.refs_2_), custom_call_target="tpu_custom_call", output_to_operand_aliasing={{0}: (1, {}), {1}: (2, {})} | custom-call | flops 4294967296 | bytes 10485760 | tf_op jit(solution)/shard_map/visibilities/pallas_call | solution.py:334
Async XLA Ops:
  13.3 39.4 %all-to-all-start.1 = ((bf16[32,1,2,80,128]{4,3,2,1,0:T(8,128)(2,1)}), bf16[32,1,2,80,128]{4,3,2,1,0:T(8,128)(2,1)S(1)}, u32[]{:S(2)}, u32[]{:S(2)}) async-start(bf16[32,1,2,80,128]{4,3,2,1,0:T(8,128)(2,1)} %get-tuple-element.16), calls=%async_computation.1 | async-start | bytes 2621440 | tf_op jit(solution)/shard_map/all_to_all | solution.py:370
  20.6 14.8 %collective-permute-start = (bf16[128,1536]{1,0:T(8,128)(2,1)}, bf16[128,1536]{1,0:T(8,128)(2,1)S(1)}, u32[]{:S(2)}, u32[]{:S(2)}) collective-permute-start(bf16[128,1536]{1,0:T(8,128)(2,1)} %get-tuple-element.14), channel_id=1, source_target_pairs={{0,1},{1,2},{2,3},{4,5},{5,6},{6,7},{8,9},{9,10},{10,11},{12,13},{... | collective-permute-start | bytes 1179656 | tf_op jit(solution)/shard_map/ppermute | solution.py:24
  35.5 0.8 copy-start.4
  52.7 1.1 copy-start.2
  53.8 69.4 %all-to-all-start = ((bf16[32,11,2,16,128]{4,3,2,1,0:T(8,128)(2,1)}), bf16[32,11,2,16,128]{4,3,2,1,0:T(8,128)(2,1)S(1)}, u32[]{:S(2)}, u32[]{:S(2)}) async-start(bf16[32,11,2,16,128]{4,3,2,1,0:T(8,128)(2,1)} %spectra.2), calls=%async_computation | async-start | bytes 5767168 | tf_op jit(solution)/shard_map/all_to_all | solution.py:370
  123.2 236.4 %all-to-all-start.3 = ((bf16[32,5,2,128,128]{4,3,2,1,0:T(8,128)(2,1)}), bf16[32,5,2,128,128]{4,3,2,1,0:T(8,128)(2,1)}, u32[]{:S(2)}, u32[]{:S(2)}) async-start(bf16[32,5,2,128,128]{4,3,2,1,0:T(8,128)(2,1)} %get-tuple-element.21), calls=%async_computation.3 | async-start | bytes 20971520 | tf_op jit(solution)/shard_map/all_to_all | solution.py:370
  127.4 7.2 %copy-start = (bf16[32,1,2,128,128]{4,3,2,1,0:T(8,128)(2,1)S(1)}, bf16[32,1,2,128,128]{4,3,2,1,0:T(8,128)(2,1)}, u32[]{:S(2)}) copy-start(bf16[32,1,2,128,128]{4,3,2,1,0:T(8,128)(2,1)} %get-tuple-element.19.refs_3_) | copy-start | bytes 6291460
  127.5 1.5 copy-start.3
  140.4 1.4 copy-start.1
  359.6 51.9 %all-to-all-start.2 = ((bf16[32,1,2,128,128]{4,3,2,1,0:T(8,128)(2,1)}), bf16[32,1,2,128,128]{4,3,2,1,0:T(8,128)(2,1)S(1)}, u32[]{:S(2)}, u32[]{:S(2)}) async-start(bf16[32,1,2,128,128]{4,3,2,1,0:T(8,128)(2,1)} %copy-done.1), calls=%async_computation.2 | async-start | bytes 4194304 | tf_op jit(solution)/shard_map/all_to_all | solution.py:370

commit v9 on v8

--- a/solution.py
+++ b/solution.py
@@ -14,7 +14,8 @@
 HISTORY = TAPS - 1
 FRAME_BLOCK = 16
 ROWS = 16
-VMEM_LIMIT = 56 * 1024 * 1024
+DIRECT_LIMIT = 56 * 1024 * 1024
+VMEM_LIMIT = 40 * 1024 * 1024
 VISIBILITY_LIMIT = 40 * 1024 * 1024
 
 
@@ -130,7 +131,7 @@
             pltpu.VMEM((HISTORY + FRAME_BLOCK, inputs_here, transform.shape[1] // TAPS * (TAPS - 1)), jnp.float32),
             pltpu.VMEM((devices * 2 * FRAME_BLOCK, inputs_here), jnp.float32),
         ],
-        compiler_params=pltpu.CompilerParams(vmem_limit_bytes=VMEM_LIMIT),
+        compiler_params=pltpu.CompilerParams(vmem_limit_bytes=DIRECT_LIMIT),
         cost_estimate=pl.CostEstimate(
             flops=2 * frames * inputs_here * FFT * transform.shape[1],
             bytes_accessed=frames * inputs_here * (4 * FFT + 4 * devices),

time: 418 us -> 419 us (level)
  waiting for transfers between devices: 259 us -> 251 us
  local copies, waits for them, and re-layouts: 4.62 us -> 11.1 us
    all_to_all x4, waiting for transfers between devices: 259 us -> 250 us  [exchange(): lax.all_to_all(array, ('chan', 'blk'), split_axis=0, concat_axis=0, tiled...]
    unnamed x10 -> x20, local copies, waits for them, and re-layouts: 4.62 us -> 11.1 us
  transfers between devices with their start and end apart: 5 -> 5, of which waited for: 4 -> 4; matrix products, arithmetic and copies ran while one was open for 0% -> 0% of each run, Pallas kernels for 27% -> 28%
where the time goes in v9:
time: 419 us; the launch traced here: 418 us
  waiting for transfers between devices  251 us (60%)
  Pallas kernels  134 us (32%)
  starting transfers between devices  22 us (5%)
  local copies, waits for them, and re-layouts  11.1 us (3%)
    all_to_all x4, waiting for transfers between devices, exchange(): lax.all_to_all(array, ('chan', 'blk'), split_axis=0, concat_axis=0, tiled...  250 us
    pallas_call x2, Pallas kernels, spectra(): pl.pallas_call(functools.partial(spectra_kernel, groups, folds, places, l...  56 us
    pallas_call x4, Pallas kernels, visibilities(): pl.pallas_call(functools.partial(visibility_kernel, piece_units, len(carr...  52.3 us
    pallas_call x2, Pallas kernels, direct_spectra(): pl.pallas_call(functools.partial(direct_kernel, len(history)), grid=(fram...  25.3 us
    all_to_all x4, starting transfers between devices, exchange(): lax.all_to_all(array, ('chan', 'blk'), split_axis=0, concat_axis=0, tiled...  19.8 us
    unnamed x20, local copies, waits for them, and re-layouts  11.1 us
  transfers between devices with their start and end apart: 5, of which 4 were waited for; matrix products, arithmetic and copies ran while one was open for 0% of the time, Pallas kernels for 28%

profile of v9, /device:TPU:0, one launch (start us, length us, event | category | flops | bytes accessed | tf_op | source)
XLA Modules:
  0.0 417.9 jit_solution(9920960551344255808)
XLA Ops:
  0.6 12.7 %direct_spectra.2 = (bf16[32,1,2,80,128]{4,3,2,1,0:T(8,128)(2,1)}, bf16[128,1536]{1,0:T(8,128)(2,1)}) custom-call(s32[128,65536]{1,0:T(8,128)} %voltages.7, s32[128,65536]{1,0:T(8,128)} %voltages.7, s32[128,65536]{1,0:T(8,128)} %voltages.7, s32[128,65536]{1,0:T(8,128)} %voltages.7, bf16[512,512]{1,0:T(8,128)(2,1)} %constant.12.clone.refs_3_), custom_call_target="tpu_custom_call" | custom-call | flops 5368709120 | bytes 22282240 | tf_op jit(solution)/shard_map/direct_spectra/pallas_call | solution.py:116
  13.3 7.4 %all-to-all-start.1 = ((bf16[32,1,2,80,128]{4,3,2,1,0:T(8,128)(2,1)}), bf16[32,1,2,80,128]{4,3,2,1,0:T(8,128)(2,1)}, u32[]{:S(2)}, u32[]{:S(2)}) async-start(bf16[32,1,2,80,128]{4,3,2,1,0:T(8,128)(2,1)} %get-tuple-element.16), calls=%async_computation.1 | async-start | bytes 2621440 | tf_op jit(solution)/shard_map/all_to_all | solution.py:371
  20.7 0.0 copy-start.6
  20.7 0.0 copy-start.7
  20.7 2.2 collective-permute-start
  23.0 12.7 %direct_spectra.3 = (bf16[32,11,2,16,128]{4,3,2,1,0:T(8,128)(2,1)}, bf16[128,1536]{1,0:T(8,128)(2,1)}) custom-call(s32[128,65536]{1,0:T(8,128)} %voltages.7, s32[128,65536]{1,0:T(8,128)} %voltages.7, s32[128,65536]{1,0:T(8,128)} %voltages.7, s32[128,65536]{1,0:T(8,128)} %voltages.7, bf16[512,512]{1,0:T(8,128)(2,1)} %constant.13.clone.refs_3_), custom_call_target="tpu_custom_call" | custom-call | flops 5368709120 | bytes 22282240 | tf_op jit(solution)/shard_map/direct_spectra/pallas_call | solution.py:116
  35.7 0.0 collective-permute-done.refs_0_
  35.7 0.0 copy-done.6
  35.7 0.0 copy-done.7
  35.7 0.0 copy-start
  35.7 1.8 copy-done
  37.5 0.0 copy-start.9
  37.5 11.7 %spectra.2 = bf16[32,11,2,16,128]{4,3,2,1,0:T(8,128)(2,1)S(1)} custom-call(s32[128,65536]{1,0:T(8,128)} %voltages.7, bf16[128,1536]{1,0:T(8,128)(2,1)S(1)} %collective-permute-done.refs_0_, f32[4,512]{1,0:T(4,128)S(1)} %copy-done.7, bf16[128,768]{1,0:T(8,128)(2,1)S(1)} %copy-done.6, ...), custom_call_target="tpu_custom_call", output_to_operand_aliasing={{}: (4, {})} | custom-call | flops 1207959552 | bytes 14155776 | tf_op jit(solution)/shard_map/spectra/pallas_call | solution.py:233
  49.2 0.0 copy-start.1
  49.2 1.6 copy-done.1
  50.8 2.0 all-to-all-done.1
  52.8 5.2 %all-to-all-start = ((bf16[32,11,2,16,128]{4,3,2,1,0:T(8,128)(2,1)}), bf16[32,11,2,16,128]{4,3,2,1,0:T(8,128)(2,1)S(1)}, u32[]{:S(2)}, u32[]{:S(2)}) async-start(bf16[32,11,2,16,128]{4,3,2,1,0:T(8,128)(2,1)} %copy-done.1), calls=%async_computation | async-start | bytes 5767168 | tf_op jit(solution)/shard_map/all_to_all | solution.py:371
  58.1 0.0 copy-done.9
  58.1 0.0 copy-start.8
  58.1 1.0 copy-done.8
  59.1 44.2 %spectra.3 = (bf16[32,5,2,128,128]{4,3,2,1,0:T(8,128)(2,1)S(1)}, bf16[32,1,2,128,128]{4,3,2,1,0:T(8,128)(2,1)S(1)}) custom-call(s32[128,65536]{1,0:T(8,128)} %voltages.7, bf16[128,1536]{1,0:T(8,128)(2,1)S(1)} %collective-permute-done.refs_0_, f32[4,512]{1,0:T(4,128)S(1)} %copy-done.7, bf16[128,768]{1,0:T(8,128)(2,1)S(1)} %copy-done.9, ...), custom_call_target="tpu_custom_call" | custom-call | flops 9663676416 | bytes 46137344 | tf_op jit(solution)/shard_map/spectra/pallas_call | solution.py:233
  103.3 0.0 copy-start.2
  103.3 4.0 copy-done.2
  107.3 0.0 copy-start.3
  107.3 1.3 copy-done.3
  108.7 15.2 %all-to-all-done = bf16[32,11,2,16,128]{4,3,2,1,0:T(8,128)(2,1)S(1)} async-done(((bf16[32,11,2,16,128]{4,3,2,1,0:T(8,128)(2,1)}), bf16[32,11,2,16,128]{4,3,2,1,0:T(8,128)(2,1)S(1)}, u32[]{:S(2)}, u32[]{:S(2)}) %all-to-all-start) | async-done | bytes 2883616 | tf_op jit(solution)/shard_map/all_to_all | solution.py:371
  123.9 4.2 %all-to-all-start.3 = ((bf16[32,5,2,128,128]{4,3,2,1,0:T(8,128)(2,1)}), bf16[32,5,2,128,128]{4,3,2,1,0:T(8,128)(2,1)}, u32[]{:S(2)}, u32[]{:S(2)}) async-start(bf16[32,5,2,128,128]{4,3,2,1,0:T(8,128)(2,1)} %copy-done.2), calls=%async_computation.3 | async-start | bytes 20971520 | tf_op jit(solution)/shard_map/all_to_all | solution.py:371
  128.1 0.0 copy-start.4
  128.1 7.2 %visibilities.4 = (f32[8,1024,1024]{2,1,0:T(8,128)}, f32[8,1024,1024]{2,1,0:T(8,128)}) custom-call(bf16[8,4,1,2,80,128]{5,4,3,2,1,0:T(8,128)(2,1)} %bitcast.1.refs_0_, bf16[8,4,11,2,16,128]{5,4,3,2,1,0:T(8,128)(2,1)S(1)} %bitcast.4), custom_call_target="tpu_custom_call" | custom-call | flops 4294967296 | bytes 10485760 | tf_op jit(solution)/shard_map/visibilities/pallas_call | solution.py:335
  135.4 0.0 copy-done.4
  135.4 5.8 %visibilities.5 = (f32[8,1024,1024]{2,1,0:T(8,128)}, f32[8,1024,1024]{2,1,0:T(8,128)}, bf16[32,1,2,128,128]{4,3,2,1,0:T(8,128)(2,1)S(1)}) custom-call(bf16[8,4,11,2,16,128]{5,4,3,2,1,0:T(8,128)(2,1)S(1)} %bitcast.5, f32[8,1024,1024]{2,1,0:T(8,128)} %get-tuple-element.17.refs_1_, ...), custom_call_target="tpu_custom_call", output_to_operand_aliasing={{0}: (1, {}), {1}: (2, {}), {2}: (3, {})} | custom-call | flops 4294967296 | bytes 10485760 | tf_op jit(solution)/shard_map/visibilities/pallas_call | solution.py:335
  141.1 0.0 copy-start.5
  141.1 1.3 copy-done.5
  142.5 217.8 %all-to-all-done.3 = bf16[32,5,2,128,128]{4,3,2,1,0:T(8,128)(2,1)} async-done(((bf16[32,5,2,128,128]{4,3,2,1,0:T(8,128)(2,1)}), bf16[32,5,2,128,128]{4,3,2,1,0:T(8,128)(2,1)}, u32[]{:S(2)}, u32[]{:S(2)}) %all-to-all-start.3) | async-done | bytes 10485792 | tf_op jit(solution)/shard_map/all_to_all | solution.py:371
  360.3 2.9 all-to-all-start.2
  363.3 33.5 %visibilities.6 = (f32[8,1024,1024]{2,1,0:T(8,128)}, f32[8,1024,1024]{2,1,0:T(8,128)}) custom-call(bf16[8,4,5,2,128,128]{5,4,3,2,1,0:T(8,128)(2,1)} %bitcast.3.refs_0_, f32[8,1024,1024]{2,1,0:T(8,128)} %get-tuple-element.22.refs_1_, f32[8,1024,1024]{2,1,0:T(8,128)} %get-tuple-element.23.refs_2_), custom_call_target="tpu_custom_call", output_to_operand_aliasing={{0}: (1, {}), {1}: (2, {})} | custom-call | flops 21474836480 | bytes 52428800 | tf_op jit(solution)/shard_map/visibilities/pallas_call | solution.py:335
  396.8 15.4 %all-to-all-done.2 = bf16[32,1,2,128,128]{4,3,2,1,0:T(8,128)(2,1)S(1)} async-done(((bf16[32,1,2,128,128]{4,3,2,1,0:T(8,128)(2,1)}), bf16[32,1,2,128,128]{4,3,2,1,0:T(8,128)(2,1)S(1)}, u32[]{:S(2)}, u32[]{:S(2)}) %all-to-all-start.2) | async-done | bytes 2097184 | tf_op jit(solution)/shard_map/all_to_all | solution.py:371
  412.2 5.8 %visibilities.7 = (f32[8,1024,1024]{2,1,0:T(8,128)}, f32[8,1024,1024]{2,1,0:T(8,128)}) custom-call(bf16[8,4,1,2,128,128]{5,4,3,2,1,0:T(8,128)(2,1)S(1)} %bitcast.6, f32[8,1024,1024]{2,1,0:T(8,128)} %get-tuple-element.24.refs_1_, f32[8,1024,1024]{2,1,0:T(8,128)} %get-tuple-element.25.refs_2_), custom_call_target="tpu_custom_call", output_to_operand_aliasing={{0}: (1, {}), {1}: (2, {})} | custom-call | flops 4294967296 | bytes 10485760 | tf_op jit(solution)/shard_map/visibilities/pallas_call | solution.py:335
Async XLA Ops:
  13.3 39.5 %all-to-all-start.1 = ((bf16[32,1,2,80,128]{4,3,2,1,0:T(8,128)(2,1)}), bf16[32,1,2,80,128]{4,3,2,1,0:T(8,128)(2,1)}, u32[]{:S(2)}, u32[]{:S(2)}) async-start(bf16[32,1,2,80,128]{4,3,2,1,0:T(8,128)(2,1)} %get-tuple-element.16), calls=%async_computation.1 | async-start | bytes 2621440 | tf_op jit(solution)/shard_map/all_to_all | solution.py:371
  20.7 14.9 %copy-start.6 = (bf16[128,768]{1,0:T(8,128)(2,1)S(1)}, bf16[128,768]{1,0:T(8,128)(2,1)}, u32[]{:S(2)}) copy-start(bf16[128,768]{1,0:T(8,128)(2,1)} %constant.14.clone.refs_2_) | copy-start | bytes 589828
  20.7 14.9 %copy-start.7 = (f32[4,512]{1,0:T(4,128)S(1)}, f32[4,512]{1,0:T(4,128)}, u32[]{:S(2)}) copy-start(f32[4,512]{1,0:T(4,128)} %constant.15.clone.refs_1_) | copy-start | bytes 24580
  20.7 14.9 %collective-permute-start = (bf16[128,1536]{1,0:T(8,128)(2,1)}, bf16[128,1536]{1,0:T(8,128)(2,1)S(1)}, u32[]{:S(2)}, u32[]{:S(2)}) collective-permute-start(bf16[128,1536]{1,0:T(8,128)(2,1)} %get-tuple-element.14), channel_id=1, source_target_pairs={{0,1},{1,2},{2,3},{4,5},{5,6},{6,7},{8,9},{9,10},{10,11},{12,13},{... | collective-permute-start | bytes 1179656 | tf_op jit(solution)/shard_map/ppermute | solution.py:25
  35.7 1.8 copy-start
  37.5 20.6 %copy-start.9 = (bf16[128,768]{1,0:T(8,128)(2,1)S(1)}, bf16[128,768]{1,0:T(8,128)(2,1)}, u32[]{:S(2)}) copy-start(bf16[128,768]{1,0:T(8,128)(2,1)} %constant.16.clone.refs_2_) | copy-start | bytes 589828
  49.2 1.6 copy-start.1
  52.8 71.0 %all-to-all-start = ((bf16[32,11,2,16,128]{4,3,2,1,0:T(8,128)(2,1)}), bf16[32,11,2,16,128]{4,3,2,1,0:T(8,128)(2,1)S(1)}, u32[]{:S(2)}, u32[]{:S(2)}) async-start(bf16[32,11,2,16,128]{4,3,2,1,0:T(8,128)(2,1)} %copy-done.1), calls=%async_computation | async-start | bytes 5767168 | tf_op jit(solution)/shard_map/all_to_all | solution.py:371
  58.1 1.0 copy-start.8
  103.3 4.0 copy-start.2
  107.3 1.3 copy-start.3
  123.9 236.4 %all-to-all-start.3 = ((bf16[32,5,2,128,128]{4,3,2,1,0:T(8,128)(2,1)}), bf16[32,5,2,128,128]{4,3,2,1,0:T(8,128)(2,1)}, u32[]{:S(2)}, u32[]{:S(2)}) async-start(bf16[32,5,2,128,128]{4,3,2,1,0:T(8,128)(2,1)} %copy-done.2), calls=%async_computation.3 | async-start | bytes 20971520 | tf_op jit(solution)/shard_map/all_to_all | solution.py:371
  128.1 7.3 %copy-start.4 = (bf16[32,1,2,128,128]{4,3,2,1,0:T(8,128)(2,1)S(1)}, bf16[32,1,2,128,128]{4,3,2,1,0:T(8,128)(2,1)}, u32[]{:S(2)}) copy-start(bf16[32,1,2,128,128]{4,3,2,1,0:T(8,128)(2,1)} %copy-done.3) | copy-start | bytes 6291460
  141.1 1.3 copy-start.5
  360.3 51.9 %all-to-all-start.2 = ((bf16[32,1,2,128,128]{4,3,2,1,0:T(8,128)(2,1)}), bf16[32,1,2,128,128]{4,3,2,1,0:T(8,128)(2,1)S(1)}, u32[]{:S(2)}, u32[]{:S(2)}) async-start(bf16[32,1,2,128,128]{4,3,2,1,0:T(8,128)(2,1)} %copy-done.5), calls=%async_computation.2 | async-start | bytes 4194304 | tf_op jit(solution)/shard_map/all_to_all | solution.py:371
